TPU v7x, 128 devices: a whole 4x4x4 slice. The times are simulated.
128 devices in a mesh: inner: 8 (over x_lo, y), outer: 16 (over x_hi, z, core).
Axes of the slice: x: 4 (x_hi: 2, x_lo: 2; x = x_hi * 2 + x_lo), y: 4, z: 4, core: 2. Of those that a mesh axis runs over, the one named last changes fastest.
Arguments:
- points: bfloat16 [16, 32768, 512], P('outer', 'inner'), may hold values from -6 to 6
- bases: bfloat16 [7, 16, 32768, 128], P(None, 'outer', 'inner'), may hold values from -0.09375 to 0.09375
- near_tiles: bfloat16 [16, 6144, 4096], P('outer', 'inner'), may hold values from -0.21875 to 0.21875
- tile_rows: int32 [16, 6144], P('outer', 'inner'), may hold values from 0 to 63, as said below
- tile_cols: int32 [16, 6144], P('outer', 'inner'), may hold values from 0 to 63, as said below
Outputs:
- applied: bfloat16 [16, 32768, 512], P('outer', 'inner')
Inputs may be any that keep to these rules, and one draw needn't show every extreme that they name: Each leaf's 768 entries of tile_rows and tile_cols, read together, are distinct pairs (row tile, column tile) of that leaf, sorted by row tile and then column tile; every diagonal pair (a, a) is present, so every row tile has at least one tile. `tile_cols`: read together with tile_rows.
All inputs are finite; a program needn't handle non-finite values.
Results may differ from a plain program's by a relative error of at most 0.0046.
Values sent between devices are 32-bit elements; how exact they have to be, the bound alone decides.
No kernel may reach another device: no remote copies, remote signals or barrier semaphores. Data moves between devices by JAX's collectives and lax.ppermute only.
A program may use at most 192 MiB of HBM per device.

v0:
```python
import jax
import jax.numpy as jnp
from jax import lax
from jax.sharding import PartitionSpec as P

LEAF = 4096
TILE = 64


def from_partner(block, axis, bit):
    count = lax.axis_size(axis)
    route = []
    for low in range(count):
        high = low | 1 << bit
        if high != low and high < count:
            route += [(low, high), (high, low)]
    return lax.ppermute(block, axis, route)


def local(points, bases, near_tiles, tile_rows, tile_cols):
    local_points = points[0]
    rhs_count = local_points.shape[1]
    stacked = bases[:, 0]
    inner_levels = lax.axis_size("inner").bit_length() - 1
    outer_levels = lax.axis_size("outer").bit_length() - 1
    partial_value = jnp.einsum(
        "hpr,pb->hrb", stacked, local_points, preferred_element_type=jnp.float32
    )
    carried = partial_value
    siblings = []
    for bit_index in range(inner_levels):
        received = from_partner(carried, "inner", bit_index)
        parent_sum = carried + received
        siblings.append(parent_sum[0] - carried[0])
        carried = parent_sum[1:]
    sib_inner = jnp.stack(siblings)
    remaining = carried
    carried = remaining
    siblings = []
    for bit_index in range(outer_levels):
        received = from_partner(carried, "outer", bit_index)
        parent_sum = carried + received
        siblings.append(parent_sum[0] - carried[0])
        carried = parent_sum[1:]
    sib_outer = jnp.stack(siblings)
    row_tiles = LEAF // TILE
    tile_count = tile_rows.shape[1]
    block_width = 128
    block_count = rhs_count // block_width
    tile_blocks = near_tiles[0].reshape(tile_count, TILE, TILE)
    tile_ids = jnp.arange(row_tiles, dtype=jnp.int32)
    col_select = (tile_cols[0][:, None] == tile_ids[None, :]).astype(jnp.bfloat16)
    row_select = (tile_ids[:, None] == tile_rows[0][None, :]).astype(jnp.float32)
    by_block = local_points.reshape(row_tiles, TILE, block_count, block_width).transpose(2, 0, 1, 3)

    def near_block(block_points):
        flat_block = block_points.reshape(row_tiles, TILE * block_width)
        picked = jnp.dot(col_select, flat_block, preferred_element_type=jnp.float32).astype(
            jnp.bfloat16
        )
        picked = picked.reshape(tile_count, TILE, block_width)
        products = jnp.einsum(
            "nij,njb->nib", tile_blocks, picked, preferred_element_type=jnp.float32
        )
        products = products.reshape(tile_count, TILE * block_width)
        summed = jnp.dot(
            row_select,
            products,
            precision=lax.Precision.HIGHEST,
            preferred_element_type=jnp.float32,
        )
        return summed.reshape(row_tiles, TILE, block_width)

    block_sums = lax.map(near_block, by_block)
    near_field = block_sums.transpose(1, 2, 0, 3).reshape(LEAF, rhs_count)
    coefficients = jnp.concatenate([sib_inner, sib_outer], axis=0).astype(jnp.bfloat16)
    far_field = jnp.einsum("hpr,hrb->pb", stacked, coefficients, preferred_element_type=jnp.float32)
    return (near_field + far_field).astype(jnp.bfloat16)[None]


def solution(mesh):
    placed = (
        P("outer", "inner", None),
        P(None, "outer", "inner", None),
        P("outer", "inner", None),
        P("outer", "inner"),
        P("outer", "inner"),
    )
    return jax.shard_map(
        local, mesh=mesh, in_specs=placed, out_specs=P("outer", "inner", None), check_vma=False
    )
```

profile of v0, /device:TPU:1, one launch (start us, length us, event | category | flops | bytes accessed | tf_op | source)
XLA Modules:
  0.0 525.6 jit_solution(12421036408603557826)
XLA Ops:
  0.0 8.1 %fusion.20 = f32[7,128,512]{2,1,0:T(8,128)S(1)} fusion(bf16[7,1,4096,128]{3,2,1,0:T(8,128)(2,1)} %param.8, bf16[1,4096,512]{2,1,0:T(8,128)(2,1)} %param.7), kind=kOutput, calls=%fused_computation.21 | convolution fusion | flops 3758096384 | bytes 13369344 | tf_op jit(solution)/shard_map/hpr,pb->hrb/dot_general | solution.py:26
  10.3 39.3 %collective-permute-done = f32[7,128,512]{2,1,0:T(8,128)S(1)} collective-permute-done((f32[7,128,512]{2,1,0:T(8,128)S(1)}, f32[7,128,512]{2,1,0:T(8,128)S(1)}, u32[]{:S(2)}, u32[]{:S(2)}) %collective-permute-start) | collective-permute-done | bytes 1835040 | tf_op jit(solution)/shard_map/ppermute | solution.py:17
  53.5 33.0 %collective-permute-done.1 = f32[6,128,512]{2,1,0:T(8,128)S(1)} collective-permute-done((f32[6,128,512]{2,1,0:T(8,128)S(1)}, f32[6,128,512]{2,1,0:T(8,128)S(1)}, u32[]{:S(2)}, u32[]{:S(2)}) %collective-permute-start.1) | collective-permute-done | bytes 1572896 | tf_op jit(solution)/shard_map/ppermute | solution.py:17
  88.3 26.8 %collective-permute-done.2 = f32[5,128,512]{2,1,0:T(8,128)S(1)} collective-permute-done((f32[5,128,512]{2,1,0:T(8,128)S(1)}, f32[5,128,512]{2,1,0:T(8,128)S(1)}, u32[]{:S(2)}, u32[]{:S(2)}) %collective-permute-start.2) | collective-permute-done | bytes 1310752 | tf_op jit(solution)/shard_map/ppermute | solution.py:17
  118.8 6.9 %reshape_squeeze.6 = bf16[64,64,4,128]{3,2,1,0:T(4,128)(2,1)} reshape(bf16[1,4096,512]{2,1,0:T(8,128)(2,1)} %param.7) | data formatting | bytes 8388608 | tf_op jit(solution)/shard_map/reshape;squeeze | solution.py:54
  125.7 5.3 %copy.13 = bf16[4,64,64,128]{3,2,1,0:T(8,128)(2,1)} copy(bf16[4,64,64,128]{3,0,2,1:T(4,128)(2,1)} %bitcast.78) | data formatting | bytes 8388608
  130.9 8.7 %copy.12 = bf16[1,768,4096]{1,2,0:T(8,128)(2,1)} copy(bf16[1,768,4096]{2,1,0:T(8,128)(2,1)} %param.9) | data formatting | bytes 12582912 | tf_op args[2]
  139.6 18.6 %copy.14 = bf16[768,64,64]{2,1,0:T(8,128)(2,1)} copy(bf16[768,64,64]{0,2,1:T(8,128)(2,1)} %bitcast.77) | data formatting | bytes 12582912
  161.9 290.7 %while.11 = (s32[]{:T(128)}, f32[4,64,64,128]{3,2,1,0:T(8,128)}, bf16[4,64,64,128]{3,2,1,0:T(8,128)(2,1)}, bf16[768,64,64]{2,1,0:T(8,128)(2,1)}, s32[768]{0:T(1024)S(1)}, /*index=5*/s32[768]{0:T(1024)S(1)}, s32[]{:T(128)}) while((s32[]{:T(128)}, f32[4,64,64,128]{3,2,1,0:T(8,128)}, bf16[4,64,64,128]{3,2,1,0:T(8,128)(2,1)}, ...), condition=%wide.region_1.2_spmd.clone, body=%wide.region_0.1_spmd.clone.sunk | while | flops 6448939008 | bytes 120592480 | solution.py:74
  163.2 7.8 %convolution_convert_fusion.2 = bf16[8192,768]{1,0:T(8,128)(2,1)} fusion(bf16[8,8,64,128]{3,2,1,0:T(8,128)(2,1)S(1)} %bitcast.76, s32[768]{0:T(1024)S(1)} %get-tuple-element.128), kind=kOutput, calls=%fused_computation.5.clone.1 | convolution fusion | flops 811696128 | bytes 13634560 | tf_op jit(solution)/shard_map/while/body/eval_jaxpr/dot_general | solution.py:58
  171.0 16.8 %copy.43 = bf16[768,64,128]{2,1,0:T(8,128)(2,1)} copy(bf16[768,64,128]{0,2,1:T(8,128)(2,1)} %bitcast.74) | data formatting | bytes 25165824 | tf_op jit(solution)/shard_map/while/body/eval_jaxpr/reshape | solution.py:61
  187.7 16.4 %fusion.60 = f32[768,128,64]{1,2,0:T(8,128)} fusion(bf16[768,64,64]{2,1,0:T(8,128)(2,1)} %get-tuple-element.127, bf16[768,64,128]{2,1,0:T(8,128)(2,1)} %copy.43), kind=kOutput, calls=%fused_computation.51.clone.1 | convolution fusion | flops 805306368 | bytes 44040192 | tf_op jit(solution)/shard_map/while/body/eval_jaxpr/nij,njb->nib/dot_general | solution.py:62
  204.1 28.6 %fusion.61 = f32[8,8,64,128]{3,1,2,0:T(8,128)S(1)} fusion(f32[96,8,64,128]{3,2,1,0:T(8,128)} %bitcast.73, s32[768]{0:T(1024)S(1)} %get-tuple-element.129), kind=kOutput, calls=%fused_computation.7.clone.1 | convolution fusion | flops 4831936512 | bytes 27266048 | tf_op jit(solution)/shard_map/while/body/eval_jaxpr/dot_general | solution.py:66
  235.9 7.8 %convolution_convert_fusion.2 = bf16[8192,768]{1,0:T(8,128)(2,1)} fusion(bf16[8,8,64,128]{3,2,1,0:T(8,128)(2,1)S(1)} %bitcast.76, s32[768]{0:T(1024)S(1)} %get-tuple-element.128), kind=kOutput, calls=%fused_computation.5.clone.1 | convolution fusion | flops 811696128 | bytes 13634560 | tf_op jit(solution)/shard_map/while/body/eval_jaxpr/dot_general | solution.py:58
  243.6 16.8 %copy.43 = bf16[768,64,128]{2,1,0:T(8,128)(2,1)} copy(bf16[768,64,128]{0,2,1:T(8,128)(2,1)} %bitcast.74) | data formatting | bytes 25165824 | tf_op jit(solution)/shard_map/while/body/eval_jaxpr/reshape | solution.py:61
  260.4 16.4 %fusion.60 = f32[768,128,64]{1,2,0:T(8,128)} fusion(bf16[768,64,64]{2,1,0:T(8,128)(2,1)} %get-tuple-element.127, bf16[768,64,128]{2,1,0:T(8,128)(2,1)} %copy.43), kind=kOutput, calls=%fused_computation.51.clone.1 | convolution fusion | flops 805306368 | bytes 44040192 | tf_op jit(solution)/shard_map/while/body/eval_jaxpr/nij,njb->nib/dot_general | solution.py:62
  276.8 28.6 %fusion.61 = f32[8,8,64,128]{3,1,2,0:T(8,128)S(1)} fusion(f32[96,8,64,128]{3,2,1,0:T(8,128)} %bitcast.73, s32[768]{0:T(1024)S(1)} %get-tuple-element.129), kind=kOutput, calls=%fused_computation.7.clone.1 | convolution fusion | flops 4831936512 | bytes 27266048 | tf_op jit(solution)/shard_map/while/body/eval_jaxpr/dot_general | solution.py:66
  308.6 7.8 %convolution_convert_fusion.2 = bf16[8192,768]{1,0:T(8,128)(2,1)} fusion(bf16[8,8,64,128]{3,2,1,0:T(8,128)(2,1)S(1)} %bitcast.76, s32[768]{0:T(1024)S(1)} %get-tuple-element.128), kind=kOutput, calls=%fused_computation.5.clone.1 | convolution fusion | flops 811696128 | bytes 13634560 | tf_op jit(solution)/shard_map/while/body/eval_jaxpr/dot_general | solution.py:58
  316.4 16.8 %copy.43 = bf16[768,64,128]{2,1,0:T(8,128)(2,1)} copy(bf16[768,64,128]{0,2,1:T(8,128)(2,1)} %bitcast.74) | data formatting | bytes 25165824 | tf_op jit(solution)/shard_map/while/body/eval_jaxpr/reshape | solution.py:61
  333.1 16.4 %fusion.60 = f32[768,128,64]{1,2,0:T(8,128)} fusion(bf16[768,64,64]{2,1,0:T(8,128)(2,1)} %get-tuple-element.127, bf16[768,64,128]{2,1,0:T(8,128)(2,1)} %copy.43), kind=kOutput, calls=%fused_computation.51.clone.1 | convolution fusion | flops 805306368 | bytes 44040192 | tf_op jit(solution)/shard_map/while/body/eval_jaxpr/nij,njb->nib/dot_general | solution.py:62
  349.5 28.6 %fusion.61 = f32[8,8,64,128]{3,1,2,0:T(8,128)S(1)} fusion(f32[96,8,64,128]{3,2,1,0:T(8,128)} %bitcast.73, s32[768]{0:T(1024)S(1)} %get-tuple-element.129), kind=kOutput, calls=%fused_computation.7.clone.1 | convolution fusion | flops 4831936512 | bytes 27266048 | tf_op jit(solution)/shard_map/while/body/eval_jaxpr/dot_general | solution.py:66
  381.3 7.8 %convolution_convert_fusion.2 = bf16[8192,768]{1,0:T(8,128)(2,1)} fusion(bf16[8,8,64,128]{3,2,1,0:T(8,128)(2,1)S(1)} %bitcast.76, s32[768]{0:T(1024)S(1)} %get-tuple-element.128), kind=kOutput, calls=%fused_computation.5.clone.1 | convolution fusion | flops 811696128 | bytes 13634560 | tf_op jit(solution)/shard_map/while/body/eval_jaxpr/dot_general | solution.py:58
  389.0 16.8 %copy.43 = bf16[768,64,128]{2,1,0:T(8,128)(2,1)} copy(bf16[768,64,128]{0,2,1:T(8,128)(2,1)} %bitcast.74) | data formatting | bytes 25165824 | tf_op jit(solution)/shard_map/while/body/eval_jaxpr/reshape | solution.py:61
  405.8 16.4 %fusion.60 = f32[768,128,64]{1,2,0:T(8,128)} fusion(bf16[768,64,64]{2,1,0:T(8,128)(2,1)} %get-tuple-element.127, bf16[768,64,128]{2,1,0:T(8,128)(2,1)} %copy.43), kind=kOutput, calls=%fused_computation.51.clone.1 | convolution fusion | flops 805306368 | bytes 44040192 | tf_op jit(solution)/shard_map/while/body/eval_jaxpr/nij,njb->nib/dot_general | solution.py:62
  422.2 28.6 %fusion.61 = f32[8,8,64,128]{3,1,2,0:T(8,128)S(1)} fusion(f32[96,8,64,128]{3,2,1,0:T(8,128)} %bitcast.73, s32[768]{0:T(1024)S(1)} %get-tuple-element.129), kind=kOutput, calls=%fused_computation.7.clone.1 | convolution fusion | flops 4831936512 | bytes 27266048 | tf_op jit(solution)/shard_map/while/body/eval_jaxpr/dot_general | solution.py:66
  452.6 16.2 %copy.22 = f32[64,64,4,128]{1,0,3,2:T(8,128)} copy(f32[64,64,4,128]{3,1,0,2:T(8,128)} %bitcast.79) | data formatting | bytes 16777216 | tf_op jit(solution)/shard_map/reshape | solution.py:75
  468.9 14.9 %reshape.22 = f32[4096,512]{0,1:T(8,128)} reshape(f32[64,64,4,128]{1,0,3,2:T(8,128)} %copy.22) | data formatting | bytes 16777216 | tf_op jit(solution)/shard_map/reshape | solution.py:75
  486.3 3.4 collective-permute-start.5
  492.8 8.6 %collective-permute-done.5 = f32[2,128,512]{2,1,0:T(8,128)S(1)} collective-permute-done((f32[2,128,512]{2,1,0:T(8,128)S(1)}, f32[2,128,512]{2,1,0:T(8,128)S(1)}, u32[]{:S(2)}, u32[]{:S(2)}) %collective-permute-start.5) | collective-permute-done | bytes 524320 | tf_op jit(solution)/shard_map/ppermute | solution.py:17
  504.5 5.3 %collective-permute-done.6 = f32[1,128,512]{2,1,0:T(8,128)S(1)} collective-permute-done((f32[1,128,512]{2,1,0:T(8,128)S(1)}, f32[1,128,512]{2,1,0:T(8,128)S(1)}, u32[]{:S(2)}, u32[]{:S(2)}) %collective-permute-start.6) | collective-permute-done | bytes 262176 | tf_op jit(solution)/shard_map/ppermute | solution.py:17
  509.9 9.3 %fusion.24 = bf16[1,4096,512]{1,2,0:T(8,128)(2,1)} fusion(f32[4096,512]{0,1:T(8,128)S(1)} %copy-done.5, bf16[7,128,512]{2,1,0:T(8,128)(2,1)S(1)} %fusion.41, bf16[7,1,4096,128]{3,2,1,0:T(8,128)(2,1)} %param.8), kind=kOutput, calls=%fused_computation.23 | convolution fusion | flops 3762290688 | bytes 20840448 | tf_op jit(solution)/shard_map/hpr,hrb->pb/dot_general | solution.py:77
  519.2 6.4 %copy.19 = bf16[1,4096,512]{2,1,0:T(8,128)(2,1)} copy(bf16[1,4096,512]{1,2,0:T(8,128)(2,1)} %fusion.24) | data formatting | bytes 8388608 | tf_op jit(solution)/shard_map/broadcast_in_dim | solution.py:78
  (60 shorter events, 36.5 us)
Async XLA Ops:
  8.1 42.2 %copy-start.6 = (f32[7,128,512]{2,1,0:T(8,128)}, f32[7,128,512]{2,1,0:T(8,128)S(1)}, u32[]{:S(2)}) copy-start(f32[7,128,512]{2,1,0:T(8,128)S(1)} %fusion.20) | copy-start | bytes 5505028
  8.1 41.5 %collective-permute-start = (f32[7,128,512]{2,1,0:T(8,128)S(1)}, f32[7,128,512]{2,1,0:T(8,128)S(1)}, u32[]{:S(2)}, u32[]{:S(2)}) collective-permute-start(f32[7,128,512]{2,1,0:T(8,128)S(1)} %fusion.20), channel_id=1, source_target_pairs={{0,16},{16,0},{32,48},{48,32},{64,80},{80,64},{96,112},{112,96},{1... | collective-permute-start | bytes 5505032 | tf_op jit(solution)/shard_map/ppermute | solution.py:17
  50.1 37.0 %copy-start = (f32[7,128,512]{2,1,0:T(8,128)}, f32[7,128,512]{2,1,0:T(8,128)S(1)}, u32[]{:S(2)}) copy-start(f32[7,128,512]{2,1,0:T(8,128)S(1)} %add.27) | copy-start | bytes 5505028
  50.3 36.2 %collective-permute-start.1 = (f32[6,128,512]{2,1,0:T(8,128)S(1)}, f32[6,128,512]{2,1,0:T(8,128)S(1)}, u32[]{:S(2)}, u32[]{:S(2)}) collective-permute-start(f32[6,128,512]{2,1,0:T(8,128)S(1)} %slice.79), channel_id=1, source_target_pairs={{0,32},{32,0},{16,48},{48,16},{64,96},{96,64},{80,112},{112,80},{1... | collective-permute-start | bytes 4718600 | tf_op jit(solution)/shard_map/ppermute | solution.py:17
  86.9 28.5 %copy-start.1 = (f32[6,128,512]{2,1,0:T(8,128)}, f32[6,128,512]{2,1,0:T(8,128)S(1)}, u32[]{:S(2)}) copy-start(f32[6,128,512]{2,1,0:T(8,128)S(1)} %slice_add_fusion.4) | copy-start | bytes 4718596
  87.0 28.0 %collective-permute-start.2 = (f32[5,128,512]{2,1,0:T(8,128)S(1)}, f32[5,128,512]{2,1,0:T(8,128)S(1)}, u32[]{:S(2)}, u32[]{:S(2)}) collective-permute-start(f32[5,128,512]{2,1,0:T(8,128)S(1)} %slice.82), channel_id=1, source_target_pairs={{0,64},{64,0},{16,80},{80,16},{32,96},{96,32},{48,112},{112,48},{1... | collective-permute-start | bytes 3932168 | tf_op jit(solution)/shard_map/ppermute | solution.py:17
  115.3 42.9 %copy-start.2 = (f32[5,128,512]{2,1,0:T(8,128)}, f32[5,128,512]{2,1,0:T(8,128)S(1)}, u32[]{:S(2)}) copy-start(f32[5,128,512]{2,1,0:T(8,128)S(1)} %slice_add_fusion.3) | copy-start | bytes 3932164
  115.4 42.8 %collective-permute-start.3 = (f32[4,128,512]{2,1,0:T(8,128)S(1)}, f32[4,128,512]{2,1,0:T(8,128)S(1)}, u32[]{:S(2)}, u32[]{:S(2)}) collective-permute-start(f32[4,128,512]{2,1,0:T(8,128)S(1)} %slice.85), channel_id=1, source_target_pairs={{0,1},{1,0},{2,3},{3,2},{4,5},{5,4},{6,7},{7,6},{8,9},{9,8},{10,11... | collective-permute-start | bytes 3145736 | tf_op jit(solution)/shard_map/ppermute | solution.py:17
  139.6 18.6 %copy-start.7 = (s32[1,768]{1,0:T(1,128)S(1)}, s32[1,768]{1,0:T(1,128)}, u32[]{:S(2)}) copy-start(s32[1,768]{1,0:T(1,128)} %param.11) | copy-start | bytes 9220
  139.6 18.6 %copy-start.8 = (s32[1,768]{1,0:T(1,128)S(1)}, s32[1,768]{1,0:T(1,128)}, u32[]{:S(2)}) copy-start(s32[1,768]{1,0:T(1,128)} %param.10) | copy-start | bytes 9220
  158.4 1.0 copy-start.3
  160.3 324.5 %collective-permute-start.4 = (f32[3,128,512]{2,1,0:T(8,128)}, f32[3,128,512]{2,1,0:T(8,128)}, u32[]{:S(2)}, u32[]{:S(2)}) collective-permute-start(f32[3,128,512]{2,1,0:T(8,128)} %slice.88), channel_id=1, source_target_pairs={{0,2},{2,0},{1,3},{3,1},{4,6},{6,4},{5,7},{7,5},{8,10},{10,8},{9,1... | collective-permute-start | bytes 2359304 | tf_op jit(solution)/shard_map/ppermute | solution.py:17
  468.9 16.0 %copy-start.4 = (f32[4,128,512]{2,1,0:T(8,128)S(1)}, f32[4,128,512]{2,1,0:T(8,128)}, u32[]{:S(2)}) copy-start(f32[4,128,512]{2,1,0:T(8,128)} %copy-done.3) | copy-start | bytes 3145732
  484.8 25.1 %copy-start.5 = (f32[4096,512]{0,1:T(8,128)S(1)}, f32[4096,512]{0,1:T(8,128)}, u32[]{:S(2)}) copy-start(f32[4096,512]{0,1:T(8,128)} %reshape.22) | copy-start | bytes 25165828
  486.3 15.1 %collective-permute-start.5 = (f32[2,128,512]{2,1,0:T(8,128)S(1)}, f32[2,128,512]{2,1,0:T(8,128)S(1)}, u32[]{:S(2)}, u32[]{:S(2)}) collective-permute-start(f32[2,128,512]{2,1,0:T(8,128)S(1)} %slice.91), channel_id=1, source_target_pairs={{0,4},{4,0},{1,5},{5,1},{2,6},{6,2},{3,7},{7,3},{8,12},{12,8},{9,1... | collective-permute-start | bytes 1572872 | tf_op jit(solution)/shard_map/ppermute | solution.py:17
  501.6 8.3 %collective-permute-start.6 = (f32[1,128,512]{2,1,0:T(8,128)S(1)}, f32[1,128,512]{2,1,0:T(8,128)S(1)}, u32[]{:S(2)}, u32[]{:S(2)}) collective-permute-start(f32[1,128,512]{2,1,0:T(8,128)S(1)} %slice.94), channel_id=1, source_target_pairs={{0,8},{8,0},{1,9},{9,1},{2,10},{10,2},{3,11},{11,3},{4,12},{12,4},... | collective-permute-start | bytes 786440 | tf_op jit(solution)/shard_map/ppermute | solution.py:17
where the time goes:
time: 530 us; the launch traced here: 526 us
  matrix products  228 us (43%)
  local copies, waits for them, and re-layouts  159 us (30%)
  waiting for transfers between devices  113 us (21%)
  starting transfers between devices  17.8 us (3%)
  other arithmetic  7.11 us (1%)
    dot_general x4, matrix products, near_block(): jnp.dot(row_select, products, precision=lax.Precision.HIGHEST, preferred_...  114 us
    ppermute x7, waiting for transfers between devices, from_partner(): return lax.ppermute(block, axis, route)  113 us
    reshape x4, local copies, waits for them, and re-layouts, near_block(): picked = picked.reshape(tile_count, TILE, block_width)  67.1 us
    dot_general x4, matrix products, near_block(): jnp.einsum('nij,njb->nib', tile_blocks, picked, preferred_element_type=jn...  65.5 us
    unnamed x21, local copies, waits for them, and re-layouts  33.5 us
    reshape x2, local copies, waits for them, and re-layouts, local(): near_field = block_sums.transpose(1, 2, 0, 3).reshape(LEAF, rhs_count)  31.1 us
    dot_general x4, matrix products, near_block(): jnp.dot(col_select, flat_block, preferred_element_type=jnp.float32)  31 us
    ppermute x7, starting transfers between devices, from_partner(): return lax.ppermute(block, axis, route)  17.8 us
  transfers between devices with their start and end apart: 7, of which 5 were waited for; matrix products, arithmetic and copies ran while one was open for 70% of the time, Pallas kernels for 0%

commit v1 on v0

v1 whole, which is shorter than its diff:
```python
import jax
import jax.numpy as jnp
from jax import lax
from jax.experimental import pallas as pl
from jax.experimental.pallas import tpu as pltpu
from jax.sharding import PartitionSpec as P

LEAF = 4096
TILE = 64
ROW_TILES = 64
TILES = 768
GROUP = 16
RANK = 128
LEVELS = 7
PAIR = TILE // 2
LANES = 128
PEERS = 8
CHUNK_TILES = 16
MM_ROWS = 512

BF16 = jnp.bfloat16
F32 = jnp.float32


def flip(block, mask):
    def place(leaf):
        return (leaf % PEERS) * 16 + leaf // PEERS

    route = [(place(leaf), place(leaf ^ mask)) for leaf in range(128)]
    return lax.ppermute(block, ("inner", "outer"), route)


def near_kernel(first, count, rows_s, cols_s, starts_s, tiles_h, points, out, dense, raw, pairs, sem):
    low, high = starts_s[first], starts_s[first + count]
    group_low, group_high = low // GROUP, (high + GROUP - 1) // GROUP

    def fetch(group):
        rows = pl.ds(pl.multiple_of(group * GROUP, GROUP), GROUP)
        return pltpu.make_async_copy(tiles_h.at[rows, :], raw.at[group], sem.at[group])

    def start(group, carry):
        fetch(group).start()
        return carry

    lax.fori_loop(group_low, group_high, start, 0)

    def clear(step, carry):
        dense[pl.ds(pl.multiple_of(step * 64, 64), 64), :] = jnp.zeros((64, LEAF), BF16)
        return carry

    lax.fori_loop(0, count, clear, 0)
    half = lax.broadcasted_iota(jnp.int32, (TILE, LANES), 1) // TILE

    def place(group, carry):
        fetch(group).wait()
        chunks = [raw[group, :, LANES * k : LANES * k + LANES] for k in range(PAIR)]
        by_tile = jnp.swapaxes(jnp.stack(chunks, axis=0), 0, 1)
        pairs[0] = by_tile
        pairs[1] = jnp.concatenate([by_tile[:, :, TILE:], by_tile[:, :, :TILE]], axis=2)
        for i in range(GROUP):
            n = group * GROUP + i
            inside = (n >= low) & (n < high)
            row = jnp.where(inside, rows_s[n] - first, count)
            col = cols_s[n]
            odd = lax.rem(col, 2)
            at_rows = pl.ds(pl.multiple_of(row * TILE, TILE), TILE)
            at_lanes = pl.ds(pl.multiple_of((col // 2) * LANES, LANES), LANES)
            value = jnp.concatenate([pairs[odd, i], pairs[1 - odd, i]], axis=0)
            dense[at_rows, at_lanes] = jnp.where(half == odd, value, dense[at_rows, at_lanes])
        return carry

    lax.fori_loop(group_low, group_high, place, 0)

    def multiply(step, carry):
        base = pl.multiple_of(step * MM_ROWS, MM_ROWS)
        total = jnp.dot(dense[pl.ds(base, MM_ROWS), :], points[...], preferred_element_type=F32)
        for t in range(MM_ROWS // TILE):
            for p in range(2):
                top = TILE * t + PAIR * p
                for q in range(4):
                    out[q, pl.ds(base + TILE * t + p, PAIR, stride=2), :] = total[
                        top : top + PAIR, LANES * q : LANES * q + LANES
                    ]
        return carry

    lax.fori_loop(0, count * TILE // MM_ROWS, multiply, 0)


def near_rows(first, count, rows, cols, starts, tiles, points):
    size = count * TILE
    width = points.shape[1]

    def body(*refs):
        near_kernel(first, count, *refs)

    return pl.pallas_call(
        body,
        grid_spec=pltpu.PrefetchScalarGridSpec(
            num_scalar_prefetch=3,
            grid=(1,),
            in_specs=[
                pl.BlockSpec(memory_space=pl.ANY),
                pl.BlockSpec((LEAF, width), lambda i, *_: (0, 0)),
            ],
            out_specs=pl.BlockSpec((4, size, LANES), lambda i, *_: (0, 0, 0)),
            scratch_shapes=[
                pltpu.VMEM((size + TILE, LEAF), BF16),
                pltpu.VMEM((TILES // GROUP, GROUP, TILE * TILE), BF16),
                pltpu.VMEM((2, GROUP, PAIR, LANES), BF16),
                pltpu.SemaphoreType.DMA((TILES // GROUP,)),
            ],
        ),
        out_shape=jax.ShapeDtypeStruct((4, size, LANES), F32),
        compiler_params=pltpu.CompilerParams(vmem_limit_bytes=40 << 20),
        cost_estimate=pl.CostEstimate(
            flops=2 * size * LEAF * width, bytes_accessed=8 << 20, transcendentals=0
        ),
        name="near_rows",
    )(rows, cols, starts, tiles, points)


FAR_ROWS = 512


def far_kernel(bases, coefficients, near, out, rounded):
    @pl.when(pl.program_id(0) == 0)
    def _():
        rounded[...] = coefficients[...].astype(BF16)

    wide = jnp.concatenate([bases[h, 0] for h in range(LEVELS)], axis=1)
    total = jnp.dot(wide, rounded[...], preferred_element_type=F32)
    base = jnp.concatenate([near[q] for q in range(4)], axis=1)
    out[...] = (total + base).astype(BF16)


def far_rows(bases, coefficients, near, first, count):
    width = coefficients.shape[1]
    return pl.pallas_call(
        far_kernel,
        grid=(count,),
        in_specs=[
            pl.BlockSpec((LEVELS, 1, FAR_ROWS, RANK), lambda i: (0, 0, first + i, 0)),
            pl.BlockSpec((LEVELS * RANK, width), lambda i: (0, 0)),
            pl.BlockSpec((4, FAR_ROWS, LANES), lambda i: (0, i, 0)),
        ],
        out_specs=pl.BlockSpec((FAR_ROWS, width), lambda i: (i, 0)),
        scratch_shapes=[pltpu.VMEM((LEVELS * RANK, width), BF16)],
        out_shape=jax.ShapeDtypeStruct((count * FAR_ROWS, width), BF16),
        compiler_params=pltpu.CompilerParams(vmem_limit_bytes=32 << 20),
        name="far_rows",
    )(bases, coefficients, near)


def siblings(partial):
    width = partial.shape[2]
    me = lax.axis_index("inner")
    core = lax.rem(lax.axis_index("outer"), 2)
    halves = partial[4:].reshape(3, 2, RANK // 2, width)
    upper = lax.dynamic_index_in_dim(halves, core, 1, keepdims=False) + flip(
        lax.dynamic_index_in_dim(halves, 1 - core, 1, keepdims=False), 8
    )
    low_part = partial[1:4].reshape(3, PEERS, 16, width).transpose(1, 0, 2, 3).reshape(PEERS, 48, width)
    up_part = upper.reshape(3, PEERS, 8, width).transpose(1, 0, 2, 3).reshape(PEERS, 24, width)
    owned = jnp.concatenate([low_part, up_part], axis=1)
    got = [lax.dynamic_index_in_dim(owned, me, 0, keepdims=False)]
    for mask in range(1, PEERS):
        got.append(flip(lax.dynamic_index_in_dim(owned, me ^ mask, 0, keepdims=False), mask))
    first = flip(partial[0], 1)
    level1 = [got[2 * i][:16] + got[2 * i + 1][:16] for i in range(4)]
    level2 = [sum(got[4 * i + j][16:32] for j in range(4)) for i in range(2)]
    rest = sum(got[i][32:] for i in range(PEERS))
    level3 = flip(rest[:16], 8)
    up = rest[16:]
    moved = flip(up, 16)
    level4 = moved[:8]
    up = up[8:] + moved[8:]
    moved = flip(up, 48)
    level5 = moved[:8]
    up = up[8:] + moved[8:]
    level6 = flip(up, 64)
    shared = jnp.concatenate([level3, level4, level5, level6], axis=0)
    back = []
    for mask in range(PEERS):
        block = jnp.concatenate([level1[(mask >> 1) ^ 1], level2[(mask >> 2) ^ 1], shared], axis=0)
        back.append(flip(block, mask) if mask else block)
    back = jnp.stack(back)
    ordered = jnp.stack([lax.dynamic_index_in_dim(back, me ^ j, 0, keepdims=False) for j in range(PEERS)])
    lower = ordered[:, :48].reshape(PEERS, 3, 16, width).transpose(1, 0, 2, 3).reshape(3, RANK, width)
    mine = ordered[:, 48:].reshape(PEERS, 3, 8, width).transpose(1, 0, 2, 3).reshape(3, RANK // 2, width)
    other = flip(mine, 8)
    swapped = core == 1
    upper = jnp.concatenate([jnp.where(swapped, other, mine), jnp.where(swapped, mine, other)], axis=1)
    return jnp.concatenate([first[None], lower, upper], axis=0)


def local(points, bases, near_tiles, tile_rows, tile_cols):
    local_points = points[0]
    width = local_points.shape[1]
    rows, cols = tile_rows[0], tile_cols[0]
    starts = jnp.sum(
        (rows[None, :] < jnp.arange(ROW_TILES + 1, dtype=jnp.int32)[:, None]).astype(jnp.int32), axis=1
    )
    partial = jnp.einsum("hpr,pb->hrb", bases[:, 0], local_points, preferred_element_type=F32)
    coefficients = siblings(partial).reshape(LEVELS * RANK, width)
    near = [
        near_rows(first, CHUNK_TILES, rows, cols, starts, near_tiles[0], local_points)
        for first in range(0, ROW_TILES, CHUNK_TILES)
    ]
    near = jnp.concatenate(near, axis=1)
    return far_rows(bases, coefficients, near, 0, LEAF // FAR_ROWS)[None]


def solution(mesh):
    placed = (
        P("outer", "inner", None),
        P(None, "outer", "inner", None),
        P("outer", "inner", None),
        P("outer", "inner"),
        P("outer", "inner"),
    )
    return jax.shard_map(
        local, mesh=mesh, in_specs=placed, out_specs=P("outer", "inner", None), check_vma=False
    )
```

time: 530 us -> 144 us (0.27)
  matrix products: 228 us -> 8.11 us
  local copies, waits for them, and re-layouts: 159 us -> 13.5 us
  waiting for transfers between devices: 113 us -> 23.2 us
  Pallas kernels: 0 us -> 54.9 us
  starting transfers between devices: 17.8 us -> 34.9 us
    dot_general x14 -> x1, matrix products: 228 us -> 8.11 us  [local(): jnp.einsum('hpr,pb->hrb', bases[:, 0], local_points, preferred_element_ty...]
    reshape x6 -> x2, local copies, waits for them, and re-layouts: 98.2 us -> 0.09 us  [the longest x1 0.07 us: siblings(): partial[1:4].reshape(3, PEERS, 16, width).transpose(1, 0, 2, 3)]
    ppermute x7 -> x21, waiting for transfers between devices: 113 us -> 23.2 us  [flip(): return lax.ppermute(block, ('inner', 'outer'), route)]
    pallas_call x0 -> x5, Pallas kernels: none -> 54.9 us  [the longest x4 47.1 us: near_rows(): pl.pallas_call(body, grid_spec=pltpu.PrefetchScalarGridSpec(num_scalar_pr...]
    unnamed x21 -> x51, local copies, waits for them, and re-layouts: 33.5 us -> 11.9 us
    ppermute x7 -> x21, starting transfers between devices: 17.8 us -> 34.9 us  [flip(): return lax.ppermute(block, ('inner', 'outer'), route)]
    another operation x1 -> x2, local copies, waits for them, and re-layouts: 6.88 us -> 0.03 us  [the longest x1 0.02 us: siblings(): jnp.stack([lax.dynamic_index_in_dim(back, me ^ j, 0, keepdims=False) for...]
    broadcast_in_dim x1 -> x0, local copies, waits for them, and re-layouts: 6.4 us -> none  [local(): return (near_field + far_field).astype(jnp.bfloat16)[None]]
  transfers between devices with their start and end apart: 7 -> 21, of which waited for: 5 -> 7; matrix products, arithmetic and copies ran while one was open for 70% -> 5% of each run, Pallas kernels for 0% -> 33%
where the time goes in v1:
time: 144 us; the launch traced here: 143 us
  Pallas kernels  54.9 us (38%)
  starting transfers between devices  34.9 us (24%)
  waiting for transfers between devices  23.2 us (16%)
  local copies, waits for them, and re-layouts  13.5 us (9%)
  matrix products  8.11 us (6%)
  other arithmetic  7.84 us (5%)
    pallas_call x4, Pallas kernels, near_rows(): pl.pallas_call(body, grid_spec=pltpu.PrefetchScalarGridSpec(num_scalar_pr...  47.1 us
    ppermute x21, starting transfers between devices, flip(): return lax.ppermute(block, ('inner', 'outer'), route)  34.9 us
    ppermute x21, waiting for transfers between devices, flip(): return lax.ppermute(block, ('inner', 'outer'), route)  23.2 us
    unnamed x51, local copies, waits for them, and re-layouts  11.9 us
    dot_general x1, matrix products, local(): jnp.einsum('hpr,pb->hrb', bases[:, 0], local_points, preferred_element_ty...  8.11 us
    pallas_call x1, Pallas kernels, far_rows(): pl.pallas_call(far_kernel, grid=(count,), in_specs=[pl.BlockSpec((LEVELS,...  7.79 us
  transfers between devices with their start and end apart: 21, of which 7 were waited for; matrix products, arithmetic and copies ran while one was open for 5% of the time, Pallas kernels for 33%

profile of v1, /device:TPU:1, one launch (start us, length us, event | category | flops | bytes accessed | tf_op | source)
XLA Modules:
  0.0 143.0 jit_solution(14669244559997696475)
XLA Ops:
  0.0 8.1 %fusion = f32[7,128,512]{2,1,0:T(8,128)S(1)} fusion(bf16[7,1,4096,128]{3,2,1,0:T(8,128)(2,1)} %bases.1, bf16[1,4096,512]{2,1,0:T(8,128)(2,1)} %param.5), kind=kOutput, calls=%fused_computation.1 | convolution fusion | flops 3758096384 | bytes 13369344 | tf_op jit(solution)/shard_map/hpr,pb->hrb/dot_general | solution.py:203
  9.5 1.5 %collective-permute-start.1 = (f32[3,64,512]{2,1,0:T(8,128)S(1)}, f32[3,64,512]{2,1,0:T(8,128)}, u32[]{:S(2)}, u32[]{:S(2)}) collective-permute-start(f32[3,64,512]{2,1,0:T(8,128)S(1)} %dynamic-slice_bitcast_fusion), channel_id=1, source_target_pairs={{0,1},{16,17},{32,33},{48,49},{64,65},{80,81},{96,97},{112,113},{1... | collective-permute-start | bytes 1179656 | tf_op jit(solution)/shard_map/ppermute | solution.py:30
  11.3 2.8 %copy-done.5 = bf16[1,768,4096]{2,1,0:T(8,128)(2,1)S(1)} copy-done((bf16[1,768,4096]{2,1,0:T(8,128)(2,1)S(1)}, bf16[1,768,4096]{2,1,0:T(8,128)(2,1)}, u32[]{:S(2)}) %copy-start.5) | copy-done | bytes 6291480
  14.1 2.2 %copy-done.7 = bf16[1,4096,512]{2,1,0:T(8,128)(2,1)S(1)} copy-done((bf16[1,4096,512]{2,1,0:T(8,128)(2,1)S(1)}, bf16[1,4096,512]{2,1,0:T(8,128)(2,1)}, u32[]{:S(2)}) %copy-start.7) | copy-done | bytes 4194328
  16.3 11.4 %near_rows.7 = f32[4,1024,128]{2,1,0:T(8,128)S(1)} custom-call(s32[768]{0:T(1024)S(1)} %reduce.refs_0_, s32[768]{0:T(1024)S(1)} %reduce.1.refs_1_, s32[65]{0:T(128)S(1)} %convert_reduce_fusion.refs_2_, bf16[768,4096]{1,0:T(8,128)(2,1)S(1)} %bitcast.94, bf16[4096,512]{1,0:T(8,128)(2,1)S(1)} %bitcast.98), custom_call_target="tpu_custom_call" | custom-call | flops 4294967296 | bytes 8388608 | tf_op jit(solution)/shard_map/near_rows/pallas_call | solution.py:96
  27.7 11.4 %near_rows.6 = f32[4,1024,128]{2,1,0:T(8,128)S(1)} custom-call(s32[768]{0:T(1024)S(1)} %reduce.refs_0_, s32[768]{0:T(1024)S(1)} %reduce.1.refs_1_, s32[65]{0:T(128)S(1)} %convert_reduce_fusion.refs_2_, bf16[768,4096]{1,0:T(8,128)(2,1)S(1)} %bitcast.95, bf16[4096,512]{1,0:T(8,128)(2,1)S(1)} %bitcast.99), custom_call_target="tpu_custom_call" | custom-call | flops 4294967296 | bytes 8388608 | tf_op jit(solution)/shard_map/near_rows/pallas_call | solution.py:96
  39.2 1.3 copy_bitcast_fusion.1
  41.5 1.3 collective-permute-start.4
  42.8 3.3 %collective-permute-start.2 = (f32[72,512]{1,0:T(8,128)}, f32[72,512]{1,0:T(8,128)}, u32[]{:S(2)}, u32[]{:S(2)}) collective-permute-start(f32[72,512]{1,0:T(8,128)} %get-tuple-element.12), channel_id=1, source_target_pairs={{0,32},{16,48},{32,0},{48,16},{64,96},{80,112},{96,64},{112,80},{1... | collective-permute-start | bytes 442376 | tf_op jit(solution)/shard_map/ppermute | solution.py:30
  46.1 12.3 %near_rows.5 = f32[4,1024,128]{2,1,0:T(8,128)S(1)} custom-call(s32[768]{0:T(1024)S(1)} %reduce.refs_0_, s32[768]{0:T(1024)S(1)} %reduce.1.refs_1_, s32[65]{0:T(128)S(1)} %convert_reduce_fusion.refs_2_, bf16[768,4096]{1,0:T(8,128)(2,1)S(1)} %bitcast.96, bf16[4096,512]{1,0:T(8,128)(2,1)S(1)} %bitcast.100), custom_call_target="tpu_custom_call" | custom-call | flops 4294967296 | bytes 8388608 | tf_op jit(solution)/shard_map/near_rows/pallas_call | solution.py:96
  58.4 1.4 copy-done.2
  59.9 4.6 %collective-permute-start.6 = (f32[72,512]{1,0:T(8,128)}, f32[72,512]{1,0:T(8,128)S(1)}, u32[]{:S(2)}, u32[]{:S(2)}) collective-permute-start(f32[72,512]{1,0:T(8,128)} %get-tuple-element.15), channel_id=1, source_target_pairs={{0,96},{16,112},{32,64},{48,80},{64,32},{80,48},{96,0},{112,16},{1... | collective-permute-start | bytes 442376 | tf_op jit(solution)/shard_map/ppermute | solution.py:30
  66.2 1.3 collective-permute-start
  67.5 2.8 %collective-permute-done.6 = f32[72,512]{1,0:T(8,128)S(1)} collective-permute-done((f32[72,512]{1,0:T(8,128)}, f32[72,512]{1,0:T(8,128)S(1)}, u32[]{:S(2)}, u32[]{:S(2)}) %collective-permute-start.6) | collective-permute-done | bytes 147488 | tf_op jit(solution)/shard_map/ppermute | solution.py:30
  70.2 3.3 %collective-permute-done.7 = f32[72,512]{1,0:T(8,128)S(1)} collective-permute-done((f32[72,512]{1,0:T(8,128)S(1)}, f32[72,512]{1,0:T(8,128)S(1)}, u32[]{:S(2)}, u32[]{:S(2)}) %collective-permute-start.7) | collective-permute-done | bytes 147488 | tf_op jit(solution)/shard_map/ppermute | solution.py:30
  77.9 3.0 %collective-permute-start.9 = (f32[16,512]{1,0:T(8,128)S(1)}, f32[16,512]{1,0:T(8,128)S(1)}, u32[]{:S(2)}, u32[]{:S(2)}) collective-permute-start(f32[16,512]{1,0:T(8,128)S(1)} %get-tuple-element.25), channel_id=1, source_target_pairs={{0,1},{16,17},{32,33},{48,49},{64,65},{80,81},{96,97},{112,113},{1... | collective-permute-start | bytes 98312 | tf_op jit(solution)/shard_map/ppermute | solution.py:30
  80.9 3.4 %collective-permute-start.11 = (f32[16,512]{1,0:T(8,128)S(1)}, f32[16,512]{1,0:T(8,128)S(1)}, u32[]{:S(2)}, u32[]{:S(2)}) collective-permute-start(f32[16,512]{1,0:T(8,128)S(1)} %get-tuple-element.24), channel_id=1, source_target_pairs={{0,6},{16,22},{32,38},{48,54},{64,70},{80,86},{96,102},{112,118},{... | collective-permute-start | bytes 98312 | tf_op jit(solution)/shard_map/ppermute | solution.py:30
  84.3 1.6 %collective-permute-done.11 = f32[16,512]{1,0:T(8,128)S(1)} collective-permute-done((f32[16,512]{1,0:T(8,128)S(1)}, f32[16,512]{1,0:T(8,128)S(1)}, u32[]{:S(2)}, u32[]{:S(2)}) %collective-permute-start.11) | collective-permute-done | bytes 32800 | tf_op jit(solution)/shard_map/ppermute | solution.py:30
  85.9 2.5 %collective-permute-start.12 = (f32[8,512]{1,0:T(8,128)S(1)}, f32[8,512]{1,0:T(8,128)S(1)}, u32[]{:S(2)}, u32[]{:S(2)}) collective-permute-start(f32[8,512]{1,0:T(8,128)S(1)} %get-tuple-element.33), channel_id=1, source_target_pairs={{0,8},{16,24},{32,40},{48,56},{64,72},{80,88},{96,104},{112,120},{... | collective-permute-start | bytes 49160 | tf_op jit(solution)/shard_map/ppermute | solution.py:30
  88.4 2.8 %copy-done.6 = bf16[1,768,4096]{2,1,0:T(8,128)(2,1)S(1)} copy-done((bf16[1,768,4096]{2,1,0:T(8,128)(2,1)S(1)}, bf16[1,768,4096]{2,1,0:T(8,128)(2,1)}, u32[]{:S(2)}) %copy-start.6) | copy-done | bytes 6291480
  91.2 12.0 %near_rows.4 = f32[4,1024,128]{2,1,0:T(8,128)S(1)} custom-call(s32[768]{0:T(1024)S(1)} %reduce.refs_0_, s32[768]{0:T(1024)S(1)} %reduce.1.refs_1_, s32[65]{0:T(128)S(1)} %convert_reduce_fusion.refs_2_, bf16[768,4096]{1,0:T(8,128)(2,1)S(1)} %bitcast.97, bf16[4096,512]{1,0:T(8,128)(2,1)S(1)} %bitcast.101), custom_call_target="tpu_custom_call" | custom-call | flops 4294967296 | bytes 8388608 | tf_op jit(solution)/shard_map/near_rows/pallas_call | solution.py:96
  103.2 1.3 copy-done.4
  104.5 1.7 %collective-permute-start.19 = (f32[72,512]{1,0:T(8,128)S(1)}, f32[72,512]{1,0:T(8,128)S(1)}, u32[]{:S(2)}, u32[]{:S(2)}) collective-permute-start(f32[72,512]{1,0:T(8,128)S(1)} %get-tuple-element.39), channel_id=1, source_target_pairs={{0,112},{16,96},{32,80},{48,64},{64,48},{80,32},{96,16},{112,0},{1... | collective-permute-start | bytes 442376 | tf_op jit(solution)/shard_map/ppermute | solution.py:30
  106.3 1.3 collective-permute-start.18
  107.5 1.8 %collective-permute-start.15 = (f32[72,512]{1,0:T(8,128)S(1)}, f32[72,512]{1,0:T(8,128)S(1)}, u32[]{:S(2)}, u32[]{:S(2)}) collective-permute-start(f32[72,512]{1,0:T(8,128)S(1)} %get-tuple-element.41), channel_id=1, source_target_pairs={{0,48},{16,32},{32,16},{48,0},{64,112},{80,96},{96,80},{112,64},{1... | collective-permute-start | bytes 442376 | tf_op jit(solution)/shard_map/ppermute | solution.py:30
  110.0 6.4 %collective-permute-done.13 = f32[72,512]{1,0:T(8,128)S(1)} collective-permute-done((f32[72,512]{1,0:T(8,128)S(1)}, f32[72,512]{1,0:T(8,128)S(1)}, u32[]{:S(2)}, u32[]{:S(2)}) %collective-permute-start.13) | collective-permute-done | bytes 147488 | tf_op jit(solution)/shard_map/ppermute | solution.py:30
  117.4 4.5 %collective-permute-done.14 = f32[72,512]{1,0:T(8,128)S(1)} collective-permute-done((f32[72,512]{1,0:T(8,128)S(1)}, f32[72,512]{1,0:T(8,128)S(1)}, u32[]{:S(2)}, u32[]{:S(2)}) %collective-permute-start.14) | collective-permute-done | bytes 147488 | tf_op jit(solution)/shard_map/ppermute | solution.py:30
  122.7 1.9 %collective-permute-start.16 = (f32[72,512]{1,0:T(8,128)S(1)}, f32[72,512]{1,0:T(8,128)S(1)}, u32[]{:S(2)}, u32[]{:S(2)}) collective-permute-start(f32[72,512]{1,0:T(8,128)S(1)} %get-tuple-element.40), channel_id=1, source_target_pairs={{0,64},{16,80},{32,96},{48,112},{64,0},{80,16},{96,32},{112,48},{1... | collective-permute-start | bytes 442376 | tf_op jit(solution)/shard_map/ppermute | solution.py:30
  124.6 4.5 %collective-permute-done.16 = f32[72,512]{1,0:T(8,128)S(1)} collective-permute-done((f32[72,512]{1,0:T(8,128)S(1)}, f32[72,512]{1,0:T(8,128)S(1)}, u32[]{:S(2)}, u32[]{:S(2)}) %collective-permute-start.16) | collective-permute-done | bytes 147488 | tf_op jit(solution)/shard_map/ppermute | solution.py:30
  129.5 3.5 %collective-permute-start.20 = (f32[3,64,512]{2,1,0:T(8,128)S(1)}, f32[3,64,512]{2,1,0:T(8,128)S(1)}, u32[]{:S(2)}, u32[]{:S(2)}) collective-permute-start(f32[3,64,512]{2,1,0:T(8,128)S(1)} %copy_bitcast_fusion), channel_id=1, source_target_pairs={{0,1},{16,17},{32,33},{48,49},{64,65},{80,81},{96,97},{112,113},{1... | collective-permute-start | bytes 1179656 | tf_op jit(solution)/shard_map/ppermute | solution.py:30
  133.0 1.8 %pad_maximum_fusion.near = f32[4,4096,128]{2,1,0:T(8,128)S(1)} fusion(f32[4,1024,128]{2,1,0:T(8,128)S(1)} %near_rows.7, f32[4,1024,128]{2,1,0:T(8,128)S(1)} %copy-done.1, f32[4,1024,128]{2,1,0:T(8,128)S(1)} %copy-done.3, f32[4,1024,128]{2,1,0:T(8,128)} %copy-done.4), kind=kLoop, calls=%fused_computation | loop fusion | flops 6291456 | bytes 16777216 | tf_op jit(solution)/shard_map/concatenate | solution.py:209
  135.3 7.8 %far_rows.1 = bf16[4096,512]{1,0:T(8,128)(2,1)} custom-call(bf16[7,1,4096,128]{3,2,1,0:T(8,128)(2,1)S(1)} %bitcast.93, f32[896,512]{1,0:T(8,128)S(1)} %bitcast.91, f32[4,4096,128]{2,1,0:T(8,128)S(1)} %pad_maximum_fusion.near), custom_call_target="tpu_custom_call" | custom-call | tf_op jit(solution)/shard_map/far_rows/pallas_call | solution.py:138
  (94 shorter events, 11.8 us)
Async XLA Ops:
  9.5 29.7 %collective-permute-start.1 = (f32[3,64,512]{2,1,0:T(8,128)S(1)}, f32[3,64,512]{2,1,0:T(8,128)}, u32[]{:S(2)}, u32[]{:S(2)}) collective-permute-start(f32[3,64,512]{2,1,0:T(8,128)S(1)} %dynamic-slice_bitcast_fusion), channel_id=1, source_target_pairs={{0,1},{16,17},{32,33},{48,49},{64,65},{80,81},{96,97},{112,113},{1... | collective-permute-start | bytes 1179656 | tf_op jit(solution)/shard_map/ppermute | solution.py:30
  11.3 2.8 %copy-start.5 = (bf16[1,768,4096]{2,1,0:T(8,128)(2,1)S(1)}, bf16[1,768,4096]{2,1,0:T(8,128)(2,1)}, u32[]{:S(2)}) copy-start(bf16[1,768,4096]{2,1,0:T(8,128)(2,1)} %param.7) | copy-start | bytes 18874372
  14.1 2.2 %copy-start.7 = (bf16[1,4096,512]{2,1,0:T(8,128)(2,1)S(1)}, bf16[1,4096,512]{2,1,0:T(8,128)(2,1)}, u32[]{:S(2)}) copy-start(bf16[1,4096,512]{2,1,0:T(8,128)(2,1)} %param.5) | copy-start | bytes 12582916
  16.3 11.4 %copy-start.8 = (bf16[1,4096,512]{2,1,0:T(8,128)(2,1)S(1)}, bf16[1,4096,512]{2,1,0:T(8,128)(2,1)}, u32[]{:S(2)}) copy-start(bf16[1,4096,512]{2,1,0:T(8,128)(2,1)} %param.5) | copy-start | bytes 12582916
  27.7 11.5 %copy-start.11 = (f32[3,128,512]{2,1,0:T(8,128)S(1)}, f32[3,128,512]{2,1,0:T(8,128)}, u32[]{:S(2)}) copy-start(f32[3,128,512]{2,1,0:T(8,128)} %copy-done.10) | copy-start | bytes 2359300
  39.2 2.3 %copy-start = (f32[4,1024,128]{2,1,0:T(8,128)}, f32[4,1024,128]{2,1,0:T(8,128)S(1)}, u32[]{:S(2)}) copy-start(f32[4,1024,128]{2,1,0:T(8,128)S(1)} %near_rows.6) | copy-start | bytes 6291460
  41.5 23.1 %collective-permute-start.4 = (f32[72,512]{1,0:T(8,128)}, f32[72,512]{1,0:T(8,128)}, u32[]{:S(2)}, u32[]{:S(2)}) collective-permute-start(f32[72,512]{1,0:T(8,128)} %get-tuple-element.11), channel_id=1, source_target_pairs={{0,64},{16,80},{32,96},{48,112},{64,0},{80,16},{96,32},{112,48},{1... | collective-permute-start | bytes 442376 | tf_op jit(solution)/shard_map/ppermute | solution.py:30
  42.8 22.2 %collective-permute-start.2 = (f32[72,512]{1,0:T(8,128)}, f32[72,512]{1,0:T(8,128)}, u32[]{:S(2)}, u32[]{:S(2)}) collective-permute-start(f32[72,512]{1,0:T(8,128)} %get-tuple-element.12), channel_id=1, source_target_pairs={{0,32},{16,48},{32,0},{48,16},{64,96},{80,112},{96,64},{112,80},{1... | collective-permute-start | bytes 442376 | tf_op jit(solution)/shard_map/ppermute | solution.py:30
  59.8 6.4 %collective-permute-start.3 = (f32[72,512]{1,0:T(8,128)}, f32[72,512]{1,0:T(8,128)S(1)}, u32[]{:S(2)}, u32[]{:S(2)}) collective-permute-start(f32[72,512]{1,0:T(8,128)} %get-tuple-element.13), channel_id=1, source_target_pairs={{0,48},{16,32},{32,16},{48,0},{64,112},{80,96},{96,80},{112,64},{1... | collective-permute-start | bytes 442376 | tf_op jit(solution)/shard_map/ppermute | solution.py:30
  59.8 7.7 %collective-permute-start.5 = (f32[72,512]{1,0:T(8,128)}, f32[72,512]{1,0:T(8,128)S(1)}, u32[]{:S(2)}, u32[]{:S(2)}) collective-permute-start(f32[72,512]{1,0:T(8,128)} %get-tuple-element.14), channel_id=1, source_target_pairs={{0,80},{16,64},{32,112},{48,96},{64,16},{80,0},{96,48},{112,32},{1... | collective-permute-start | bytes 442376 | tf_op jit(solution)/shard_map/ppermute | solution.py:30
  59.9 10.3 %collective-permute-start.6 = (f32[72,512]{1,0:T(8,128)}, f32[72,512]{1,0:T(8,128)S(1)}, u32[]{:S(2)}, u32[]{:S(2)}) collective-permute-start(f32[72,512]{1,0:T(8,128)} %get-tuple-element.15), channel_id=1, source_target_pairs={{0,96},{16,112},{32,64},{48,80},{64,32},{80,48},{96,0},{112,16},{1... | collective-permute-start | bytes 442376 | tf_op jit(solution)/shard_map/ppermute | solution.py:30
  64.5 23.9 %copy-start.9 = (bf16[1,4096,512]{2,1,0:T(8,128)(2,1)S(1)}, bf16[1,4096,512]{2,1,0:T(8,128)(2,1)}, u32[]{:S(2)}) copy-start(bf16[1,4096,512]{2,1,0:T(8,128)(2,1)} %param.5) | copy-start | bytes 12582916
  64.6 9.0 %collective-permute-start.7 = (f32[72,512]{1,0:T(8,128)S(1)}, f32[72,512]{1,0:T(8,128)S(1)}, u32[]{:S(2)}, u32[]{:S(2)}) collective-permute-start(f32[72,512]{1,0:T(8,128)S(1)} %get-tuple-element.16), channel_id=1, source_target_pairs={{0,112},{16,96},{32,80},{48,64},{64,48},{80,32},{96,16},{112,0},{1... | collective-permute-start | bytes 442376 | tf_op jit(solution)/shard_map/ppermute | solution.py:30
  65.0 8.6 %collective-permute-start.8 = (f32[72,512]{1,0:T(8,128)S(1)}, f32[72,512]{1,0:T(8,128)S(1)}, u32[]{:S(2)}, u32[]{:S(2)}) collective-permute-start(f32[72,512]{1,0:T(8,128)S(1)} %get-tuple-element.18), channel_id=1, source_target_pairs={{0,16},{16,0},{32,48},{48,32},{64,80},{80,64},{96,112},{112,96},{1... | collective-permute-start | bytes 442376 | tf_op jit(solution)/shard_map/ppermute | solution.py:30
  66.2 68.9 %collective-permute-start = (f32[128,512]{1,0:T(8,128)S(1)}, f32[128,512]{1,0:T(8,128)S(1)}, u32[]{:S(2)}, u32[]{:S(2)}) collective-permute-start(f32[128,512]{1,0:T(8,128)S(1)} %slice_bitcast_fusion.1), channel_id=1, source_target_pairs={{0,16},{16,0},{32,48},{48,32},{64,80},{80,64},{96,112},{112,96},{1... | collective-permute-start | bytes 786440 | tf_op jit(solution)/shard_map/ppermute | solution.py:30
  74.6 3.3 %collective-permute-start.10 = (f32[24,512]{1,0:T(8,128)S(1)}, f32[24,512]{1,0:T(8,128)S(1)}, u32[]{:S(2)}, u32[]{:S(2)}) collective-permute-start(f32[24,512]{1,0:T(8,128)S(1)} %slice.179), channel_id=1, source_target_pairs={{0,2},{16,18},{32,34},{48,50},{64,66},{80,82},{96,98},{112,114},{1... | collective-permute-start | bytes 147464 | tf_op jit(solution)/shard_map/ppermute | solution.py:30
  77.9 6.4 %collective-permute-start.9 = (f32[16,512]{1,0:T(8,128)S(1)}, f32[16,512]{1,0:T(8,128)S(1)}, u32[]{:S(2)}, u32[]{:S(2)}) collective-permute-start(f32[16,512]{1,0:T(8,128)S(1)} %get-tuple-element.25), channel_id=1, source_target_pairs={{0,1},{16,17},{32,33},{48,49},{64,65},{80,81},{96,97},{112,113},{1... | collective-permute-start | bytes 98312 | tf_op jit(solution)/shard_map/ppermute | solution.py:30
  80.9 5.0 %collective-permute-start.11 = (f32[16,512]{1,0:T(8,128)S(1)}, f32[16,512]{1,0:T(8,128)S(1)}, u32[]{:S(2)}, u32[]{:S(2)}) collective-permute-start(f32[16,512]{1,0:T(8,128)S(1)} %get-tuple-element.24), channel_id=1, source_target_pairs={{0,6},{16,22},{32,38},{48,54},{64,70},{80,86},{96,102},{112,118},{... | collective-permute-start | bytes 98312 | tf_op jit(solution)/shard_map/ppermute | solution.py:30
  85.9 18.6 %collective-permute-start.12 = (f32[8,512]{1,0:T(8,128)S(1)}, f32[8,512]{1,0:T(8,128)S(1)}, u32[]{:S(2)}, u32[]{:S(2)}) collective-permute-start(f32[8,512]{1,0:T(8,128)S(1)} %get-tuple-element.33), channel_id=1, source_target_pairs={{0,8},{16,24},{32,40},{48,56},{64,72},{80,88},{96,104},{112,120},{... | collective-permute-start | bytes 49160 | tf_op jit(solution)/shard_map/ppermute | solution.py:30
  88.4 2.8 %copy-start.6 = (bf16[1,768,4096]{2,1,0:T(8,128)(2,1)S(1)}, bf16[1,768,4096]{2,1,0:T(8,128)(2,1)}, u32[]{:S(2)}) copy-start(bf16[1,768,4096]{2,1,0:T(8,128)(2,1)} %param.7) | copy-start | bytes 18874372
  104.5 24.6 %collective-permute-start.19 = (f32[72,512]{1,0:T(8,128)S(1)}, f32[72,512]{1,0:T(8,128)S(1)}, u32[]{:S(2)}, u32[]{:S(2)}) collective-permute-start(f32[72,512]{1,0:T(8,128)S(1)} %get-tuple-element.39), channel_id=1, source_target_pairs={{0,112},{16,96},{32,80},{48,64},{64,48},{80,32},{96,16},{112,0},{1... | collective-permute-start | bytes 442376 | tf_op jit(solution)/shard_map/ppermute | solution.py:30
  106.3 22.9 %collective-permute-start.18 = (f32[72,512]{1,0:T(8,128)S(1)}, f32[72,512]{1,0:T(8,128)S(1)}, u32[]{:S(2)}, u32[]{:S(2)}) collective-permute-start(f32[72,512]{1,0:T(8,128)S(1)} %get-tuple-element.39), channel_id=1, source_target_pairs={{0,96},{16,112},{32,64},{48,80},{64,32},{80,48},{96,0},{112,16},{1... | collective-permute-start | bytes 442376 | tf_op jit(solution)/shard_map/ppermute | solution.py:30
  107.5 15.2 %collective-permute-start.15 = (f32[72,512]{1,0:T(8,128)S(1)}, f32[72,512]{1,0:T(8,128)S(1)}, u32[]{:S(2)}, u32[]{:S(2)}) collective-permute-start(f32[72,512]{1,0:T(8,128)S(1)} %get-tuple-element.41), channel_id=1, source_target_pairs={{0,48},{16,32},{32,16},{48,0},{64,112},{80,96},{96,80},{112,64},{1... | collective-permute-start | bytes 442376 | tf_op jit(solution)/shard_map/ppermute | solution.py:30
  109.3 7.1 %collective-permute-start.13 = (f32[72,512]{1,0:T(8,128)S(1)}, f32[72,512]{1,0:T(8,128)S(1)}, u32[]{:S(2)}, u32[]{:S(2)}) collective-permute-start(f32[72,512]{1,0:T(8,128)S(1)} %get-tuple-element.42), channel_id=1, source_target_pairs={{0,16},{16,0},{32,48},{48,32},{64,80},{80,64},{96,112},{112,96},{1... | collective-permute-start | bytes 442376 | tf_op jit(solution)/shard_map/ppermute | solution.py:30
  116.4 5.5 %collective-permute-start.14 = (f32[72,512]{1,0:T(8,128)S(1)}, f32[72,512]{1,0:T(8,128)S(1)}, u32[]{:S(2)}, u32[]{:S(2)}) collective-permute-start(f32[72,512]{1,0:T(8,128)S(1)} %get-tuple-element.41), channel_id=1, source_target_pairs={{0,32},{16,48},{32,0},{48,16},{64,96},{80,112},{96,64},{112,80},{1... | collective-permute-start | bytes 442376 | tf_op jit(solution)/shard_map/ppermute | solution.py:30
  121.9 7.2 %collective-permute-start.17 = (f32[72,512]{1,0:T(8,128)S(1)}, f32[72,512]{1,0:T(8,128)S(1)}, u32[]{:S(2)}, u32[]{:S(2)}) collective-permute-start(f32[72,512]{1,0:T(8,128)S(1)} %get-tuple-element.40), channel_id=1, source_target_pairs={{0,80},{16,64},{32,112},{48,96},{64,16},{80,0},{96,48},{112,32},{1... | collective-permute-start | bytes 442376 | tf_op jit(solution)/shard_map/ppermute | solution.py:30
  122.7 6.4 %collective-permute-start.16 = (f32[72,512]{1,0:T(8,128)S(1)}, f32[72,512]{1,0:T(8,128)S(1)}, u32[]{:S(2)}, u32[]{:S(2)}) collective-permute-start(f32[72,512]{1,0:T(8,128)S(1)} %get-tuple-element.40), channel_id=1, source_target_pairs={{0,64},{16,80},{32,96},{48,112},{64,0},{80,16},{96,32},{112,48},{1... | collective-permute-start | bytes 442376 | tf_op jit(solution)/shard_map/ppermute | solution.py:30
  129.1 3.9 %copy-start.3 = (f32[4,1024,128]{2,1,0:T(8,128)S(1)}, f32[4,1024,128]{2,1,0:T(8,128)}, u32[]{:S(2)}) copy-start(f32[4,1024,128]{2,1,0:T(8,128)} %copy-done.2) | copy-start | bytes 6291460
  129.3 3.7 %copy-start.1 = (f32[4,1024,128]{2,1,0:T(8,128)S(1)}, f32[4,1024,128]{2,1,0:T(8,128)}, u32[]{:S(2)}) copy-start(f32[4,1024,128]{2,1,0:T(8,128)} %copy-done) | copy-start | bytes 6291460
  129.4 5.8 %slice-start = ((s8[7340032]{0:T(1024)(128)(4,1)}), s8[4194304]{0:T(1024)(128)(4,1)S(1)}, s32[]{:S(2)}) async-start(s8[7340032]{0:T(1024)(128)(4,1)} %bitcast.92), calls=%async_computation | async-start | bytes 8388608
  129.5 5.8 %slice-start.1 = ((s8[7340032]{0:T(1024)(128)(4,1)}), s8[3145728]{0:T(1024)(128)(4,1)S(1)}, s32[]{:S(2)}) async-start(s8[7340032]{0:T(1024)(128)(4,1)} %bitcast.92), calls=%async_computation.1 | async-start | bytes 6291456
  129.5 5.5 %collective-permute-start.20 = (f32[3,64,512]{2,1,0:T(8,128)S(1)}, f32[3,64,512]{2,1,0:T(8,128)S(1)}, u32[]{:S(2)}, u32[]{:S(2)}) collective-permute-start(f32[3,64,512]{2,1,0:T(8,128)S(1)} %copy_bitcast_fusion), channel_id=1, source_target_pairs={{0,1},{16,17},{32,33},{48,49},{64,65},{80,81},{96,97},{112,113},{1... | collective-permute-start | bytes 1179656 | tf_op jit(solution)/shard_map/ppermute | solution.py:30
  (6 other events, 9.2 us)

commit v2 on v1

v2 whole, which is shorter than its diff:
```python
import jax
import jax.numpy as jnp
from jax import lax
from jax.experimental import pallas as pl
from jax.experimental.pallas import tpu as pltpu
from jax.sharding import PartitionSpec as P

LEAF = 4096
TILE = 64
ROW_TILES = 64
TILES = 768
GROUP = 16
RANK = 128
LEVELS = 7
PAIR = TILE // 2
LANES = 128
PEERS = 8
CHUNKS = ((0, 16), (16, 16), (32, 16), (48, 8), (56, 8))
MM_ROWS = 512

BF16 = jnp.bfloat16
F32 = jnp.float32


def flip(block, mask):
    def place(leaf):
        return (leaf % PEERS) * 16 + leaf // PEERS

    route = [(place(leaf), place(leaf ^ mask)) for leaf in range(128)]
    return lax.ppermute(block, ("inner", "outer"), route)


def near_kernel(first, count, rows_s, cols_s, tiles, points_h, out_h, dense, raw, pairs, points, out, tile_sem, sem):
    def tiles_before(row):
        def halve(step, span):
            below, size = span
            middle = below + size // 2
            smaller = (size > 0) & (rows_s[0, jnp.minimum(middle, TILES - 1)] < row)
            return jnp.where(smaller, middle + 1, below), jnp.where(smaller, size - size // 2 - 1, size // 2)

        return lax.fori_loop(0, TILES.bit_length(), halve, (jnp.int32(0), jnp.int32(TILES)))[0]

    low, high = tiles_before(first), tiles_before(first + count)
    group_low, group_high = low // GROUP, (high + GROUP - 1) // GROUP

    def fetch(group):
        part = pl.ds(pl.multiple_of(group * GROUP, GROUP), GROUP)
        return pltpu.make_async_copy(tiles.at[part, :], raw.at[group], tile_sem.at[group])

    def start(group, carry):
        fetch(group).start()
        return carry

    lax.fori_loop(group_low, group_high, start, 0)
    whole = pltpu.make_async_copy(points_h, points, sem.at[0])
    whole.start()

    def clear(step, carry):
        dense[pl.ds(pl.multiple_of(step * 64, 64), 64), :] = jnp.zeros((64, LEAF), BF16)
        return carry

    lax.fori_loop(0, count, clear, 0)
    half = lax.broadcasted_iota(jnp.int32, (TILE, LANES), 1) // TILE

    def place(group, carry):
        fetch(group).wait()
        chunks = [raw[group, :, LANES * k : LANES * k + LANES] for k in range(PAIR)]
        by_tile = jnp.swapaxes(jnp.stack(chunks, axis=0), 0, 1)
        pairs[0] = by_tile
        pairs[1] = jnp.concatenate([by_tile[:, :, TILE:], by_tile[:, :, :TILE]], axis=2)
        for i in range(GROUP):
            n = group * GROUP + i
            inside = (n >= low) & (n < high)
            row = jnp.where(inside, rows_s[0, n] - first, count)
            col = cols_s[0, n]
            odd = lax.rem(col, 2)
            at_rows = pl.ds(pl.multiple_of(row * TILE, TILE), TILE)
            at_lanes = pl.ds(pl.multiple_of((col // 2) * LANES, LANES), LANES)
            value = jnp.concatenate([pairs[odd, i], pairs[1 - odd, i]], axis=0)
            dense[at_rows, at_lanes] = jnp.where(half == odd, value, dense[at_rows, at_lanes])
        return carry

    lax.fori_loop(group_low, group_high, place, 0)
    whole.wait()

    def store(step):
        part = pl.ds(pl.multiple_of(step * MM_ROWS, MM_ROWS), MM_ROWS)
        target = pl.ds(pl.multiple_of(first * TILE + step * MM_ROWS, MM_ROWS), MM_ROWS)
        return pltpu.make_async_copy(out.at[:, part, :], out_h.at[:, target, :], sem.at[1 + step])

    def multiply(step, carry):
        base = pl.multiple_of(step * MM_ROWS, MM_ROWS)
        total = jnp.dot(dense[pl.ds(base, MM_ROWS), :], points[...], preferred_element_type=F32)
        for t in range(MM_ROWS // TILE):
            for p in range(2):
                top = TILE * t + PAIR * p
                for q in range(4):
                    out[q, pl.ds(base + TILE * t + p, PAIR, stride=2), :] = total[
                        top : top + PAIR, LANES * q : LANES * q + LANES
                    ]
        store(step).start()
        return carry

    steps = count * TILE // MM_ROWS
    lax.fori_loop(0, steps, multiply, 0)
    for step in range(steps):
        store(step).wait()


def near_rows(first, count, rows, cols, tiles, points, earlier):
    size = count * TILE
    width = points.shape[1]

    given = [] if earlier is None else [earlier]

    def body(rows_s, cols_s, tiles_h, points_h, *refs):
        near_kernel(first, count, rows_s, cols_s, tiles_h, points_h, *refs[len(given) :])

    return pl.pallas_call(
        body,
        in_specs=[pl.BlockSpec(memory_space=pltpu.SMEM)] * 2 + [pl.BlockSpec(memory_space=pl.ANY)] * (2 + len(given)),
        out_specs=pl.BlockSpec(memory_space=pl.ANY),
        scratch_shapes=[
            pltpu.VMEM((size + TILE, LEAF), BF16),
            pltpu.VMEM((TILES // GROUP, GROUP, TILE * TILE), BF16),
            pltpu.VMEM((2, GROUP, PAIR, LANES), BF16),
            pltpu.VMEM((LEAF, width), BF16),
            pltpu.VMEM((4, size, LANES), F32),
            pltpu.SemaphoreType.DMA((TILES // GROUP,)),
            pltpu.SemaphoreType.DMA((1 + size // MM_ROWS,)),
        ],
        out_shape=jax.ShapeDtypeStruct((4, LEAF, LANES), F32),
        input_output_aliases={4: 0} if given else {},
        compiler_params=pltpu.CompilerParams(vmem_limit_bytes=56 << 20),
        cost_estimate=pl.CostEstimate(
            flops=2 * size * LEAF * width, bytes_accessed=8 << 20, transcendentals=0
        ),
        name="near_rows",
    )(rows, cols, tiles, points, *given)


FAR_ROWS = 512


def far_rows(bases, place, pieces, near):
    width = pieces[0].shape[1]
    steps = LEAF // FAR_ROWS

    def body(place_s, bases_h, near_h, first, *refs):
        *back, side_other, core_own, core_other, out_h, bases_v, near_v, out, ordered, rounded, sem = refs

        def rows_of(step):
            return pl.ds(pl.multiple_of(step * FAR_ROWS, FAR_ROWS), FAR_ROWS)

        def fetch_bases(step):
            return pltpu.make_async_copy(
                bases_h.at[:, 0, rows_of(step), :], bases_v.at[:, rows_of(step), :], sem.at[0, step]
            )

        def fetch_near(step):
            return pltpu.make_async_copy(near_h.at[:, rows_of(step), :], near_v.at[:, rows_of(step), :], sem.at[1, step])

        def store(step):
            return pltpu.make_async_copy(out.at[rows_of(step), :], out_h.at[rows_of(step), :], sem.at[2, step])

        for step in range(steps):
            fetch_bases(step).start()
            fetch_near(step).start()
        ring, side, core = place_s[0], place_s[1], place_s[2]

        def put(row, value):
            ordered[pl.ds(pl.multiple_of(row, 8), value.shape[0]), :] = value

        def put_upper(source, offset, mask, its_core, its_side):
            for level in range(3):
                row = 512 + RANK * level + 64 * its_core + 32 * its_side + 8 * (ring ^ mask)
                put(row, source[offset + 8 * level : offset + 8 * level + 8, :])

        put(0, first[...])
        for mask in range(4):
            slot = ring ^ mask
            put(128 + 32 * slot, back[mask][0:32, :])
            put(256 + 32 * slot, back[mask][32:64, :])
            put(384 + 64 * side + 16 * slot, back[mask][64:80, :])
            put(384 + 64 * (1 - side) + 16 * slot, side_other[mask, 0:16, :])
            put_upper(back[mask], 80, mask, core, side)
            put_upper(side_other.at[mask], 16, mask, core, 1 - side)
            put_upper(core_own.at[mask], 0, mask, 1 - core, side)
            put_upper(core_other.at[mask], 0, mask, 1 - core, 1 - side)
        rounded[...] = ordered[...].astype(BF16)

        def compute(step, carry):
            rows = rows_of(step)
            fetch_bases(step).wait()
            fetch_near(step).wait()
            wide = jnp.concatenate([bases_v[h, rows, :] for h in range(LEVELS)], axis=1)
            total = jnp.dot(wide, rounded[...], preferred_element_type=F32)
            base = jnp.concatenate([near_v[q, rows, :] for q in range(4)], axis=1)
            out[rows, :] = (total + base).astype(BF16)
            store(step).start()
            return carry

        lax.fori_loop(0, steps, compute, 0)
        for step in range(steps):
            store(step).wait()

    return pl.pallas_call(
        body,
        in_specs=[pl.BlockSpec(memory_space=pltpu.SMEM)]
        + [pl.BlockSpec(memory_space=pl.ANY)] * 2
        + [pl.BlockSpec(memory_space=pltpu.VMEM)] * len(pieces),
        out_specs=pl.BlockSpec(memory_space=pl.ANY),
        scratch_shapes=[
            pltpu.VMEM((LEVELS, LEAF, RANK), BF16),
            pltpu.VMEM((4, LEAF, LANES), F32),
            pltpu.VMEM((LEAF, width), BF16),
            pltpu.VMEM((LEVELS * RANK, width), F32),
            pltpu.VMEM((LEVELS * RANK, width), BF16),
            pltpu.SemaphoreType.DMA((3, steps)),
        ],
        out_shape=jax.ShapeDtypeStruct((LEAF, width), BF16),
        compiler_params=pltpu.CompilerParams(vmem_limit_bytes=56 << 20),
        name="far_rows",
    )(place, bases, near, *pieces)


def after(value, *others):
    return lax.optimization_barrier((value, *others))[0]


def spread(block, parts, size):
    levels, _, width = block.shape
    return block.reshape(levels, parts, size, width).transpose(1, 0, 2, 3).reshape(parts, levels * size, width)


def halves_of(block, bit):
    levels, rows, width = block.shape
    cut = block.reshape(levels, 2, rows // 2, width)
    return (
        lax.dynamic_index_in_dim(cut, bit, 1, keepdims=False),
        lax.dynamic_index_in_dim(cut, 1 - bit, 1, keepdims=False),
    )


def siblings(partial, near_part, own_rows):
    width = partial.shape[2]
    me = lax.axis_index("inner")
    ring, side = lax.rem(me, 4), me // 4
    core = lax.rem(lax.axis_index("outer"), 2)
    mine, other = halves_of(partial[4:], core)
    upper = mine + flip(other, 8)
    mine3, other3 = halves_of(partial[3:4], side)
    mine, other = halves_of(upper, side)
    sent = jnp.concatenate([other3.reshape(64, width), other.reshape(96, width)], axis=0)
    near = near_part(0, after(own_rows, sent), None)
    received = flip(sent, 4)
    first = flip(after(partial[0], sent), 1)
    received, first, near = lax.optimization_barrier((received, first, near))
    level3 = mine3 + received[None, :64]
    upper = mine + received[64:].reshape(3, 32, width)
    owned = jnp.concatenate([spread(partial[1:3], 4, 32), spread(level3, 4, 16), spread(upper, 4, 8)], axis=1)
    got = [lax.dynamic_index_in_dim(owned, ring, 0, keepdims=False)]
    near = near_part(1, after(own_rows, owned), near)
    for mask in range(1, 4):
        got.append(flip(lax.dynamic_index_in_dim(owned, ring ^ mask, 0, keepdims=False), mask))
    *got, near = lax.optimization_barrier((*got, near))
    level1 = [got[2][:32] + got[3][:32], got[0][:32] + got[1][:32]]
    total = got[0][32:] + got[1][32:] + got[2][32:] + got[3][32:]
    near = near_part(2, after(own_rows, total), near)
    level2 = flip(total[:32], 4)
    level3 = flip(total[32:48], 8)
    up4, up5, up6 = total[48:56], total[56:64], total[64:72]
    moved1 = flip(jnp.concatenate([up4, up6]), 16)
    pair = jnp.concatenate([up5, up6])
    moved2, moved3 = flip(pair, 32), flip(pair, 48)
    level4 = moved1[:8]
    level5 = moved2[:8] + moved3[:8]
    up6, near = lax.optimization_barrier((up6 + moved1[8:] + moved2[8:] + moved3[8:], near))
    level6 = flip(up6, 64)
    shared = jnp.concatenate([level2, level3, level4, level5, level6], axis=0)
    near = near_part(3, after(own_rows, shared), near)
    back = []
    for mask in range(4):
        block = jnp.concatenate([level1[mask >> 1], shared], axis=0)
        back.append(flip(block, mask) if mask else block)
    *back, near = lax.optimization_barrier((*back, near))
    both = jnp.stack([block[64:] for block in back])
    near = near_part(4, after(own_rows, both), near)
    core_own = flip(both[:, 16:], 8)
    side_other = flip(both, 4)
    side_other, core_own, near = lax.optimization_barrier((side_other, core_own, near))
    core_other = flip(side_other[:, 16:], 8)
    return (first, *back, side_other, core_own, core_other), near


def local(points, bases, near_tiles, tile_rows, tile_cols):
    local_points = points[0]
    width = local_points.shape[1]
    partial = jnp.einsum("hpr,pb->hrb", bases[:, 0], local_points, preferred_element_type=F32)

    def near_part(part, own_rows, earlier):
        return near_rows(*CHUNKS[part], own_rows, tile_cols, near_tiles[0], local_points, earlier)

    pieces, near = siblings(partial, near_part, tile_rows)
    inner, outer = lax.axis_index("inner"), lax.axis_index("outer")
    place = jnp.stack([lax.rem(inner, 4), inner // 4, lax.rem(outer, 2)]).astype(jnp.int32)
    return far_rows(bases, place, pieces, near)[None]


def solution(mesh):
    placed = (
        P("outer", "inner", None),
        P(None, "outer", "inner", None),
        P("outer", "inner", None),
        P("outer", "inner"),
        P("outer", "inner"),
    )
    return jax.shard_map(
        local, mesh=mesh, in_specs=placed, out_specs=P("outer", "inner", None), check_vma=False
    )
```

time: 144 us -> 101 us (0.70)
  waiting for transfers between devices: 23.2 us -> 3.01 us
  starting transfers between devices: 34.9 us -> 24.4 us
  local copies, waits for them, and re-layouts: 13.5 us -> 4.43 us
  other arithmetic: 7.84 us -> 0.92 us
  Pallas kernels: 54.9 us -> 58.8 us
    ppermute x21 -> x18, waiting for transfers between devices: 23.2 us -> 3.01 us  [flip(): return lax.ppermute(block, ('inner', 'outer'), route)]
    ppermute x21 -> x18, starting transfers between devices: 34.9 us -> 24.4 us  [flip(): return lax.ppermute(block, ('inner', 'outer'), route)]
    unnamed x51 -> x21, local copies, waits for them, and re-layouts: 11.9 us -> 1.95 us
    pallas_call x5 -> x6, Pallas kernels: 54.9 us -> 58.8 us  [the longest x5 49.1 us: near_rows(): pl.pallas_call(body, in_specs=[pl.BlockSpec(memory_space=pltpu.SMEM)] * 2...]
    unnamed x7 -> x2, other arithmetic: 2.37 us -> 0.03 us
    concatenate x3, other arithmetic: 2 us -> 0.1 us  [the longest x1 0.07 us: siblings(): jnp.concatenate([spread(partial[1:3], 4, 32), spread(level3, 4, 16), spre...]
  transfers between devices with their start and end apart: 21 -> 18, of which waited for: 7 -> 3; matrix products, arithmetic and copies ran while one was open for 5% -> 3% of each run, Pallas kernels for 33% -> 49%
where the time goes in v2:
time: 101 us; the launch traced here: 100 us
  Pallas kernels  58.8 us (58%)
  starting transfers between devices  24.4 us (24%)
  matrix products  8.11 us (8%)
  local copies, waits for them, and re-layouts  4.43 us (4%)
  waiting for transfers between devices  3.01 us (3%)
    pallas_call x5, Pallas kernels, near_rows(): pl.pallas_call(body, in_specs=[pl.BlockSpec(memory_space=pltpu.SMEM)] * 2...  49.1 us
    ppermute x18, starting transfers between devices, flip(): return lax.ppermute(block, ('inner', 'outer'), route)  24.4 us
    pallas_call x1, Pallas kernels, far_rows(): pl.pallas_call(body, in_specs=[pl.BlockSpec(memory_space=pltpu.SMEM)] + [...  9.72 us
    dot_general x1, matrix products, local(): jnp.einsum('hpr,pb->hrb', bases[:, 0], local_points, preferred_element_ty...  8.11 us
    ppermute x18, waiting for transfers between devices, flip(): return lax.ppermute(block, ('inner', 'outer'), route)  3.01 us
  transfers between devices with their start and end apart: 18, of which 3 were waited for; matrix products, arithmetic and copies ran while one was open for 3% of the time, Pallas kernels for 49%

profile of v2, /device:TPU:1, one launch (start us, length us, event | category | flops | bytes accessed | tf_op | source)
XLA Modules:
  0.0 100.3 jit_solution(13209863146449763162)
XLA Ops:
  0.0 8.1 %fusion = f32[7,128,512]{2,1,0:T(8,128)S(1)} fusion(bf16[7,1,4096,128]{3,2,1,0:T(8,128)(2,1)} %bases_h.1, bf16[1,4096,512]{2,1,0:T(8,128)(2,1)} %param.5), kind=kOutput, calls=%fused_computation | convolution fusion | flops 3758096384 | bytes 13369344 | tf_op jit(solution)/shard_map/hpr,pb->hrb/dot_general | solution.py:299
  8.1 1.2 %copy-done = f32[7,128,512]{2,1,0:T(8,128)} copy-done((f32[7,128,512]{2,1,0:T(8,128)}, f32[7,128,512]{2,1,0:T(8,128)S(1)}, u32[]{:S(2)}) %copy-start) | copy-done | bytes 1835032
  9.4 1.5 %collective-permute-start = (f32[3,64,512]{2,1,0:T(8,128)S(1)}, f32[3,64,512]{2,1,0:T(8,128)S(1)}, u32[]{:S(2)}, u32[]{:S(2)}) collective-permute-start(f32[3,64,512]{2,1,0:T(8,128)S(1)} %dynamic-slice_bitcast_fusion), channel_id=1, source_target_pairs={{0,1},{16,17},{32,33},{48,49},{64,65},{80,81},{96,97},{112,113},{1... | collective-permute-start | bytes 1179656 | tf_op jit(solution)/shard_map/ppermute | solution.py:30
  10.9 1.1 %slice.122 = f32[2,128,512]{2,1,0:T(8,128)S(1)} slice(f32[7,128,512]{2,1,0:T(8,128)} %copy-done), slice={[1:3], [0:128], [0:512]} | slice | bytes 1048576 | tf_op jit(solution)/shard_map/slice | solution.py:261
  12.1 1.1 %slice_bitcast_fusion = (f32[128,512]{1,0:T(8,128)S(1)}, f32[1,128,512]{2,1,0:T(8,128)S(1)}) fusion(f32[7,128,512]{2,1,0:T(8,128)} %copy-done), kind=kLoop, calls=%fused_computation.8 | loop fusion | bytes 1048576 | tf_op jit(solution)/shard_map/squeeze | solution.py:257
  13.4 1.4 %collective-permute-start.1 = (f32[160,512]{1,0:T(8,128)S(1)}, f32[160,512]{1,0:T(8,128)S(1)}, u32[]{:S(2)}, u32[]{:S(2)}) collective-permute-start(f32[160,512]{1,0:T(8,128)S(1)} %pad_maximum_fusion.1), channel_id=1, source_target_pairs={{0,64},{16,80},{32,96},{48,112},{64,0},{80,16},{96,32},{112,48},{1... | collective-permute-start | bytes 983048 | tf_op jit(solution)/shard_map/ppermute | solution.py:30
  14.7 1.3 %collective-permute-start.2 = (f32[128,512]{1,0:T(8,128)S(1)}, f32[128,512]{1,0:T(8,128)S(1)}, u32[]{:S(2)}, u32[]{:S(2)}) collective-permute-start(f32[128,512]{1,0:T(8,128)S(1)} %get-tuple-element.28), channel_id=1, source_target_pairs={{0,16},{16,0},{32,48},{48,32},{64,80},{80,64},{96,112},{112,96},{1... | collective-permute-start | bytes 786440 | tf_op jit(solution)/shard_map/ppermute | solution.py:30
  16.0 11.1 %near_rows.5.refs_0_ = f32[4,4096,128]{2,1,0:T(8,128)} custom-call(s32[1,768]{1,0:T(1,128)} %rows_s.4, s32[1,768]{1,0:T(1,128)} %cols_s.9, bf16[768,4096]{1,0:T(8,128)(2,1)} %bitcast.58, bf16[4096,512]{1,0:T(8,128)(2,1)} %bitcast.63), custom_call_target="tpu_custom_call" | custom-call | flops 4294967296 | bytes 8388608 | tf_op jit(solution)/shard_map/near_rows/pallas_call | solution.py:119
  27.3 0.1 dynamic-slice_bitcast_fusion.1
  27.4 2.2 %collective-permute-start.5 = (f32[104,512]{1,0:T(8,128)S(1)}, f32[104,512]{1,0:T(8,128)S(1)}, u32[]{:S(2)}, u32[]{:S(2)}) collective-permute-start(f32[104,512]{1,0:T(8,128)S(1)} %get-tuple-element.53), channel_id=1, source_target_pairs={{0,48},{16,32},{32,16},{48,0},{64,112},{80,96},{96,80},{112,64},{1... | collective-permute-start | bytes 638984 | tf_op jit(solution)/shard_map/ppermute | solution.py:30
  29.6 1.1 %collective-permute-start.4 = (f32[104,512]{1,0:T(8,128)S(1)}, f32[104,512]{1,0:T(8,128)S(1)}, u32[]{:S(2)}, u32[]{:S(2)}) collective-permute-start(f32[104,512]{1,0:T(8,128)S(1)} %get-tuple-element.54), channel_id=1, source_target_pairs={{0,32},{16,48},{32,0},{48,16},{64,96},{80,112},{96,64},{112,80},{1... | collective-permute-start | bytes 638984 | tf_op jit(solution)/shard_map/ppermute | solution.py:30
  30.7 11.5 %near_rows.6.refs_0_ = f32[4,4096,128]{2,1,0:T(8,128)} custom-call(s32[1,768]{1,0:T(1,128)} %rows_s.4, s32[1,768]{1,0:T(1,128)} %cols_s.9, bf16[768,4096]{1,0:T(8,128)(2,1)} %bitcast.59, bf16[4096,512]{1,0:T(8,128)(2,1)} %bitcast.64, f32[4,4096,128]{2,1,0:T(8,128)} %near_rows.5.refs_0_), custom_call_target="tpu_custom_call", output_to_operand_aliasing={{}: (4, {})} | custom-call | flops 4294967296 | bytes 8388608 | tf_op jit(solution)/shard_map/near_rows/pallas_call | solution.py:119
  42.4 3.4 %collective-permute-start.10 = (f32[16,512]{1,0:T(8,128)S(1)}, f32[16,512]{1,0:T(8,128)S(1)}, u32[]{:S(2)}, u32[]{:S(2)}) collective-permute-start(f32[16,512]{1,0:T(8,128)S(1)} %get-tuple-element.57), channel_id=1, source_target_pairs={{0,6},{16,22},{32,38},{48,54},{64,70},{80,86},{96,102},{112,118},{... | collective-permute-start | bytes 98312 | tf_op jit(solution)/shard_map/ppermute | solution.py:30
  45.8 0.4 collective-permute-start.9
  46.2 0.2 collective-permute-start.8
  46.4 2.5 %collective-permute-start.7 = (f32[16,512]{1,0:T(8,128)S(1)}, f32[16,512]{1,0:T(8,128)S(1)}, u32[]{:S(2)}, u32[]{:S(2)}) collective-permute-start(f32[16,512]{1,0:T(8,128)S(1)} %get-tuple-element.58), channel_id=1, source_target_pairs={{0,1},{16,17},{32,33},{48,49},{64,65},{80,81},{96,97},{112,113},{1... | collective-permute-start | bytes 98312 | tf_op jit(solution)/shard_map/ppermute | solution.py:30
  49.0 11.6 %near_rows.7.refs_0_ = f32[4,4096,128]{2,1,0:T(8,128)} custom-call(s32[1,768]{1,0:T(1,128)} %rows_s.4, s32[1,768]{1,0:T(1,128)} %cols_s.9, bf16[768,4096]{1,0:T(8,128)(2,1)} %bitcast.60, bf16[4096,512]{1,0:T(8,128)(2,1)} %bitcast.65, f32[4,4096,128]{2,1,0:T(8,128)} %near_rows.6.refs_0_), custom_call_target="tpu_custom_call", output_to_operand_aliasing={{}: (4, {})} | custom-call | flops 4294967296 | bytes 8388608 | tf_op jit(solution)/shard_map/near_rows/pallas_call | solution.py:119
  60.8 3.1 %collective-permute-start.11 = (f32[8,512]{1,0:T(8,128)S(1)}, f32[8,512]{1,0:T(8,128)S(1)}, u32[]{:S(2)}, u32[]{:S(2)}) collective-permute-start(f32[8,512]{1,0:T(8,128)S(1)} %get-tuple-element.39), channel_id=1, source_target_pairs={{0,8},{16,24},{32,40},{48,56},{64,72},{80,88},{96,104},{112,120},{... | collective-permute-start | bytes 49160 | tf_op jit(solution)/shard_map/ppermute | solution.py:30
  63.8 1.1 %collective-permute-done.11 = f32[8,512]{1,0:T(8,128)S(1)} collective-permute-done((f32[8,512]{1,0:T(8,128)S(1)}, f32[8,512]{1,0:T(8,128)S(1)}, u32[]{:S(2)}, u32[]{:S(2)}) %collective-permute-start.11) | collective-permute-done | bytes 16416 | tf_op jit(solution)/shard_map/ppermute | solution.py:30
  65.0 1.9 %collective-permute-start.14 = (f32[104,512]{1,0:T(8,128)S(1)}, f32[104,512]{1,0:T(8,128)S(1)}, u32[]{:S(2)}, u32[]{:S(2)}) collective-permute-start(f32[104,512]{1,0:T(8,128)S(1)} %get-tuple-element.70), channel_id=1, source_target_pairs={{0,48},{16,32},{32,16},{48,0},{64,112},{80,96},{96,80},{112,64},{1... | collective-permute-start | bytes 638984 | tf_op jit(solution)/shard_map/ppermute | solution.py:30
  66.9 0.5 collective-permute-start.13
  67.4 0.8 collective-permute-start.12
  68.2 7.4 %near_rows.8.refs_0_ = f32[4,4096,128]{2,1,0:T(8,128)} custom-call(s32[1,768]{1,0:T(1,128)} %rows_s.4, s32[1,768]{1,0:T(1,128)} %cols_s.9, bf16[768,4096]{1,0:T(8,128)(2,1)} %bitcast.61, bf16[4096,512]{1,0:T(8,128)(2,1)} %bitcast.66, f32[4,4096,128]{2,1,0:T(8,128)} %near_rows.7.refs_0_), custom_call_target="tpu_custom_call", output_to_operand_aliasing={{}: (4, {})} | custom-call | flops 2147483648 | bytes 8388608 | tf_op jit(solution)/shard_map/near_rows/pallas_call | solution.py:119
  75.7 1.0 %collective-permute-done.12.refs_1_ = f32[104,512]{1,0:T(8,128)S(1)} collective-permute-done((f32[104,512]{1,0:T(8,128)S(1)}, f32[104,512]{1,0:T(8,128)S(1)}, u32[]{:S(2)}, u32[]{:S(2)}) %collective-permute-start.12) | collective-permute-done | bytes 213024 | tf_op jit(solution)/shard_map/ppermute | solution.py:30
  76.8 1.0 collective-permute-start.15
  77.8 2.9 %collective-permute-start.16 = (f32[4,24,512]{2,1,0:T(8,128)S(1)}, f32[4,24,512]{2,1,0:T(8,128)S(1)}, u32[]{:S(2)}, u32[]{:S(2)}) collective-permute-start(f32[4,24,512]{2,1,0:T(8,128)S(1)} %slice.136), channel_id=1, source_target_pairs={{0,1},{16,17},{32,33},{48,49},{64,65},{80,81},{96,97},{112,113},{1... | collective-permute-start | bytes 589832 | tf_op jit(solution)/shard_map/ppermute | solution.py:30
  80.8 7.4 %near_rows.9.near_h = f32[4,4096,128]{2,1,0:T(8,128)} custom-call(s32[1,768]{1,0:T(1,128)} %rows_s.4, s32[1,768]{1,0:T(1,128)} %cols_s.9, bf16[768,4096]{1,0:T(8,128)(2,1)} %bitcast.62, bf16[4096,512]{1,0:T(8,128)(2,1)} %bitcast.67, f32[4,4096,128]{2,1,0:T(8,128)} %near_rows.8.refs_0_), custom_call_target="tpu_custom_call", output_to_operand_aliasing={{}: (4, {})} | custom-call | flops 2147483648 | bytes 8388608 | tf_op jit(solution)/shard_map/near_rows/pallas_call | solution.py:119
  88.3 0.1 collective-permute-start.17
  88.4 0.6 pad_add_fusion.place_s
  89.0 0.8 collective-permute-done.17.refs_6_
  89.8 0.7 copy-done.8
  90.5 9.7 %far_rows.1 = bf16[4096,512]{1,0:T(8,128)(2,1)} custom-call(s32[3]{0:T(128)} %pad_add_fusion.place_s, bf16[7,1,4096,128]{3,2,1,0:T(8,128)(2,1)} %bases_h.1, f32[4,4096,128]{2,1,0:T(8,128)} %near_rows.9.near_h, f32[128,512]{1,0:T(8,128)} %copy-done.6, f32[104,512]{1,0:T(8,128)} %copy-done.2, f32[104,512]{1,0:T(8,128)} %copy-done.5, f32[104,512]{1,0:T(8,128)} %copy-done.4, ...), custom_call_target="tpu_custom_call" | custom-call | tf_op jit(solution)/shard_map/far_rows/pallas_call | solution.py:207
  (62 shorter events, 0.7 us)
Async XLA Ops:
  8.1 1.2 %copy-start = (f32[7,128,512]{2,1,0:T(8,128)}, f32[7,128,512]{2,1,0:T(8,128)S(1)}, u32[]{:S(2)}) copy-start(f32[7,128,512]{2,1,0:T(8,128)S(1)} %fusion) | copy-start | bytes 5505028
  9.4 3.8 %collective-permute-start = (f32[3,64,512]{2,1,0:T(8,128)S(1)}, f32[3,64,512]{2,1,0:T(8,128)S(1)}, u32[]{:S(2)}, u32[]{:S(2)}) collective-permute-start(f32[3,64,512]{2,1,0:T(8,128)S(1)} %dynamic-slice_bitcast_fusion), channel_id=1, source_target_pairs={{0,1},{16,17},{32,33},{48,49},{64,65},{80,81},{96,97},{112,113},{1... | collective-permute-start | bytes 1179656 | tf_op jit(solution)/shard_map/ppermute | solution.py:30
  13.4 13.8 %collective-permute-start.1 = (f32[160,512]{1,0:T(8,128)S(1)}, f32[160,512]{1,0:T(8,128)S(1)}, u32[]{:S(2)}, u32[]{:S(2)}) collective-permute-start(f32[160,512]{1,0:T(8,128)S(1)} %pad_maximum_fusion.1), channel_id=1, source_target_pairs={{0,64},{16,80},{32,96},{48,112},{64,0},{80,16},{96,32},{112,48},{1... | collective-permute-start | bytes 983048 | tf_op jit(solution)/shard_map/ppermute | solution.py:30
  14.7 12.4 %collective-permute-start.2 = (f32[128,512]{1,0:T(8,128)S(1)}, f32[128,512]{1,0:T(8,128)S(1)}, u32[]{:S(2)}, u32[]{:S(2)}) collective-permute-start(f32[128,512]{1,0:T(8,128)S(1)} %get-tuple-element.28), channel_id=1, source_target_pairs={{0,16},{16,0},{32,48},{48,32},{64,80},{80,64},{96,112},{112,96},{1... | collective-permute-start | bytes 786440 | tf_op jit(solution)/shard_map/ppermute | solution.py:30
  27.1 15.2 %copy-start.6 = (f32[128,512]{1,0:T(8,128)}, f32[128,512]{1,0:T(8,128)S(1)}, u32[]{:S(2)}) copy-start(f32[128,512]{1,0:T(8,128)S(1)} %collective-permute-done.2.first) | copy-start | bytes 786436
  27.4 14.9 %collective-permute-start.5 = (f32[104,512]{1,0:T(8,128)S(1)}, f32[104,512]{1,0:T(8,128)S(1)}, u32[]{:S(2)}, u32[]{:S(2)}) collective-permute-start(f32[104,512]{1,0:T(8,128)S(1)} %get-tuple-element.53), channel_id=1, source_target_pairs={{0,48},{16,32},{32,16},{48,0},{64,112},{80,96},{96,80},{112,64},{1... | collective-permute-start | bytes 638984 | tf_op jit(solution)/shard_map/ppermute | solution.py:30
  29.6 12.7 %collective-permute-start.4 = (f32[104,512]{1,0:T(8,128)S(1)}, f32[104,512]{1,0:T(8,128)S(1)}, u32[]{:S(2)}, u32[]{:S(2)}) collective-permute-start(f32[104,512]{1,0:T(8,128)S(1)} %get-tuple-element.54), channel_id=1, source_target_pairs={{0,32},{16,48},{32,0},{48,16},{64,96},{80,112},{96,64},{112,80},{1... | collective-permute-start | bytes 638984 | tf_op jit(solution)/shard_map/ppermute | solution.py:30
  30.7 11.6 %collective-permute-start.3 = (f32[104,512]{1,0:T(8,128)S(1)}, f32[104,512]{1,0:T(8,128)S(1)}, u32[]{:S(2)}, u32[]{:S(2)}) collective-permute-start(f32[104,512]{1,0:T(8,128)S(1)} %get-tuple-element.55), channel_id=1, source_target_pairs={{0,16},{16,0},{32,48},{48,32},{64,80},{80,64},{96,112},{112,96},{1... | collective-permute-start | bytes 638984 | tf_op jit(solution)/shard_map/ppermute | solution.py:30
  42.4 18.3 %collective-permute-start.10 = (f32[16,512]{1,0:T(8,128)S(1)}, f32[16,512]{1,0:T(8,128)S(1)}, u32[]{:S(2)}, u32[]{:S(2)}) collective-permute-start(f32[16,512]{1,0:T(8,128)S(1)} %get-tuple-element.57), channel_id=1, source_target_pairs={{0,6},{16,22},{32,38},{48,54},{64,70},{80,86},{96,102},{112,118},{... | collective-permute-start | bytes 98312 | tf_op jit(solution)/shard_map/ppermute | solution.py:30
  45.8 15.0 %collective-permute-start.9 = (f32[16,512]{1,0:T(8,128)S(1)}, f32[16,512]{1,0:T(8,128)S(1)}, u32[]{:S(2)}, u32[]{:S(2)}) collective-permute-start(f32[16,512]{1,0:T(8,128)S(1)} %get-tuple-element.57), channel_id=1, source_target_pairs={{0,4},{16,20},{32,36},{48,52},{64,68},{80,84},{96,100},{112,116},{... | collective-permute-start | bytes 98312 | tf_op jit(solution)/shard_map/ppermute | solution.py:30
  46.2 14.5 %collective-permute-start.8 = (f32[16,512]{1,0:T(8,128)S(1)}, f32[16,512]{1,0:T(8,128)S(1)}, u32[]{:S(2)}, u32[]{:S(2)}) collective-permute-start(f32[16,512]{1,0:T(8,128)S(1)} %pad_maximum_fusion.3), channel_id=1, source_target_pairs={{0,2},{16,18},{32,34},{48,50},{64,66},{80,82},{96,98},{112,114},{1... | collective-permute-start | bytes 98312 | tf_op jit(solution)/shard_map/ppermute | solution.py:30
  46.4 14.2 %collective-permute-start.7 = (f32[16,512]{1,0:T(8,128)S(1)}, f32[16,512]{1,0:T(8,128)S(1)}, u32[]{:S(2)}, u32[]{:S(2)}) collective-permute-start(f32[16,512]{1,0:T(8,128)S(1)} %get-tuple-element.58), channel_id=1, source_target_pairs={{0,1},{16,17},{32,33},{48,49},{64,65},{80,81},{96,97},{112,113},{1... | collective-permute-start | bytes 98312 | tf_op jit(solution)/shard_map/ppermute | solution.py:30
  49.0 11.7 %collective-permute-start.6 = (f32[32,512]{1,0:T(8,128)S(1)}, f32[32,512]{1,0:T(8,128)S(1)}, u32[]{:S(2)}, u32[]{:S(2)}) collective-permute-start(f32[32,512]{1,0:T(8,128)S(1)} %slice.126), channel_id=1, source_target_pairs={{0,64},{16,80},{32,96},{48,112},{64,0},{80,16},{96,32},{112,48},{1... | collective-permute-start | bytes 196616 | tf_op jit(solution)/shard_map/ppermute | solution.py:30
  60.8 4.2 %collective-permute-start.11 = (f32[8,512]{1,0:T(8,128)S(1)}, f32[8,512]{1,0:T(8,128)S(1)}, u32[]{:S(2)}, u32[]{:S(2)}) collective-permute-start(f32[8,512]{1,0:T(8,128)S(1)} %get-tuple-element.39), channel_id=1, source_target_pairs={{0,8},{16,24},{32,40},{48,56},{64,72},{80,88},{96,104},{112,120},{... | collective-permute-start | bytes 49160 | tf_op jit(solution)/shard_map/ppermute | solution.py:30
  65.0 11.7 %copy-start.2 = (f32[104,512]{1,0:T(8,128)}, f32[104,512]{1,0:T(8,128)S(1)}, u32[]{:S(2)}) copy-start(f32[104,512]{1,0:T(8,128)S(1)} %get-tuple-element.41.refs_0_) | copy-start | bytes 638980
  65.0 10.7 %collective-permute-start.14 = (f32[104,512]{1,0:T(8,128)S(1)}, f32[104,512]{1,0:T(8,128)S(1)}, u32[]{:S(2)}, u32[]{:S(2)}) collective-permute-start(f32[104,512]{1,0:T(8,128)S(1)} %get-tuple-element.70), channel_id=1, source_target_pairs={{0,48},{16,32},{32,16},{48,0},{64,112},{80,96},{96,80},{112,64},{1... | collective-permute-start | bytes 638984 | tf_op jit(solution)/shard_map/ppermute | solution.py:30
  66.9 8.8 %collective-permute-start.13 = (f32[104,512]{1,0:T(8,128)S(1)}, f32[104,512]{1,0:T(8,128)S(1)}, u32[]{:S(2)}, u32[]{:S(2)}) collective-permute-start(f32[104,512]{1,0:T(8,128)S(1)} %get-tuple-element.70), channel_id=1, source_target_pairs={{0,32},{16,48},{32,0},{48,16},{64,96},{80,112},{96,64},{112,80},{1... | collective-permute-start | bytes 638984 | tf_op jit(solution)/shard_map/ppermute | solution.py:30
  67.4 9.3 %collective-permute-start.12 = (f32[104,512]{1,0:T(8,128)S(1)}, f32[104,512]{1,0:T(8,128)S(1)}, u32[]{:S(2)}, u32[]{:S(2)}) collective-permute-start(f32[104,512]{1,0:T(8,128)S(1)} %get-tuple-element.41.refs_0_), channel_id=1, source_target_pairs={{0,16},{16,0},{32,48},{48,32},{64,80},{80,64},{96,112},{112,96},{1... | collective-permute-start | bytes 638984 | tf_op jit(solution)/shard_map/ppermute | solution.py:30
  75.6 12.5 %copy-start.3 = (f32[104,512]{1,0:T(8,128)}, f32[104,512]{1,0:T(8,128)S(1)}, u32[]{:S(2)}) copy-start(f32[104,512]{1,0:T(8,128)S(1)} %collective-permute-done.14.refs_3_) | copy-start | bytes 638980
  75.7 12.5 %copy-start.4 = (f32[104,512]{1,0:T(8,128)}, f32[104,512]{1,0:T(8,128)S(1)}, u32[]{:S(2)}) copy-start(f32[104,512]{1,0:T(8,128)S(1)} %collective-permute-done.13.refs_2_) | copy-start | bytes 638980
  76.7 11.5 %copy-start.5 = (f32[104,512]{1,0:T(8,128)}, f32[104,512]{1,0:T(8,128)S(1)}, u32[]{:S(2)}) copy-start(f32[104,512]{1,0:T(8,128)S(1)} %collective-permute-done.12.refs_1_) | copy-start | bytes 638980
  76.8 11.4 %collective-permute-start.15 = (f32[4,40,512]{2,1,0:T(8,128)S(1)}, f32[4,40,512]{2,1,0:T(8,128)S(1)}, u32[]{:S(2)}, u32[]{:S(2)}) collective-permute-start(f32[4,40,512]{2,1,0:T(8,128)S(1)} %pad_maximum_fusion.2), channel_id=1, source_target_pairs={{0,64},{16,80},{32,96},{48,112},{64,0},{80,16},{96,32},{112,48},{1... | collective-permute-start | bytes 983048 | tf_op jit(solution)/shard_map/ppermute | solution.py:30
  77.8 10.4 %collective-permute-start.16 = (f32[4,24,512]{2,1,0:T(8,128)S(1)}, f32[4,24,512]{2,1,0:T(8,128)S(1)}, u32[]{:S(2)}, u32[]{:S(2)}) collective-permute-start(f32[4,24,512]{2,1,0:T(8,128)S(1)} %slice.136), channel_id=1, source_target_pairs={{0,1},{16,17},{32,33},{48,49},{64,65},{80,81},{96,97},{112,113},{1... | collective-permute-start | bytes 589832 | tf_op jit(solution)/shard_map/ppermute | solution.py:30
  88.2 1.6 %copy-start.7 = (f32[4,24,512]{2,1,0:T(8,128)}, f32[4,24,512]{2,1,0:T(8,128)S(1)}, u32[]{:S(2)}) copy-start(f32[4,24,512]{2,1,0:T(8,128)S(1)} %collective-permute-done.16.refs_5_) | copy-start | bytes 589828
  88.2 1.6 %copy-start.1 = (f32[4,40,512]{2,1,0:T(8,128)}, f32[4,40,512]{2,1,0:T(8,128)S(1)}, u32[]{:S(2)}) copy-start(f32[4,40,512]{2,1,0:T(8,128)S(1)} %collective-permute-done.15.refs_4_) | copy-start | bytes 983044
  88.3 1.5 %collective-permute-start.17 = (f32[4,24,512]{2,1,0:T(8,128)S(1)}, f32[4,24,512]{2,1,0:T(8,128)S(1)}, u32[]{:S(2)}, u32[]{:S(2)}) collective-permute-start(f32[4,24,512]{2,1,0:T(8,128)S(1)} %slice.121), channel_id=1, source_target_pairs={{0,1},{16,17},{32,33},{48,49},{64,65},{80,81},{96,97},{112,113},{1... | collective-permute-start | bytes 589832 | tf_op jit(solution)/shard_map/ppermute | solution.py:30
  89.8 0.7 copy-start.8

commit v3 on v2

--- a/solution.py
+++ b/solution.py
@@ -30,7 +30,7 @@
     return lax.ppermute(block, ("inner", "outer"), route)
 
 
-def near_kernel(first, count, rows_s, cols_s, tiles, points_h, out_h, dense, raw, pairs, points, out, tile_sem, sem):
+def near_kernel(first, count, rows_s, cols_s, tiles, points_h, out, dense, raw, pairs, points, tile_sem, sem):
     def tiles_before(row):
         def halve(step, span):
             below, size = span
@@ -52,7 +52,7 @@
         return carry
 
     lax.fori_loop(group_low, group_high, start, 0)
-    whole = pltpu.make_async_copy(points_h, points, sem.at[0])
+    whole = pltpu.make_async_copy(points_h, points, sem)
     whole.start()
 
     def clear(step, carry):
@@ -83,11 +83,6 @@
     lax.fori_loop(group_low, group_high, place, 0)
     whole.wait()
 
-    def store(step):
-        part = pl.ds(pl.multiple_of(step * MM_ROWS, MM_ROWS), MM_ROWS)
-        target = pl.ds(pl.multiple_of(first * TILE + step * MM_ROWS, MM_ROWS), MM_ROWS)
-        return pltpu.make_async_copy(out.at[:, part, :], out_h.at[:, target, :], sem.at[1 + step])
-
     def multiply(step, carry):
         base = pl.multiple_of(step * MM_ROWS, MM_ROWS)
         total = jnp.dot(dense[pl.ds(base, MM_ROWS), :], points[...], preferred_element_type=F32)
@@ -98,56 +93,50 @@
                     out[q, pl.ds(base + TILE * t + p, PAIR, stride=2), :] = total[
                         top : top + PAIR, LANES * q : LANES * q + LANES
                     ]
-        store(step).start()
         return carry
 
-    steps = count * TILE // MM_ROWS
-    lax.fori_loop(0, steps, multiply, 0)
-    for step in range(steps):
-        store(step).wait()
-
-
-def near_rows(first, count, rows, cols, tiles, points, earlier):
+    lax.fori_loop(0, count * TILE // MM_ROWS, multiply, 0)
+
+
+def near_rows(first, count, rows, cols, tiles, points):
     size = count * TILE
     width = points.shape[1]
 
-    given = [] if earlier is None else [earlier]
-
-    def body(rows_s, cols_s, tiles_h, points_h, *refs):
-        near_kernel(first, count, rows_s, cols_s, tiles_h, points_h, *refs[len(given) :])
+    def body(*refs):
+        near_kernel(first, count, *refs)
 
     return pl.pallas_call(
         body,
-        in_specs=[pl.BlockSpec(memory_space=pltpu.SMEM)] * 2 + [pl.BlockSpec(memory_space=pl.ANY)] * (2 + len(given)),
-        out_specs=pl.BlockSpec(memory_space=pl.ANY),
+        in_specs=[pl.BlockSpec(memory_space=pltpu.SMEM)] * 2 + [pl.BlockSpec(memory_space=pl.ANY)] * 2,
+        out_specs=pl.BlockSpec(memory_space=pltpu.VMEM),
         scratch_shapes=[
             pltpu.VMEM((size + TILE, LEAF), BF16),
             pltpu.VMEM((TILES // GROUP, GROUP, TILE * TILE), BF16),
             pltpu.VMEM((2, GROUP, PAIR, LANES), BF16),
             pltpu.VMEM((LEAF, width), BF16),
-            pltpu.VMEM((4, size, LANES), F32),
             pltpu.SemaphoreType.DMA((TILES // GROUP,)),
-            pltpu.SemaphoreType.DMA((1 + size // MM_ROWS,)),
+            pltpu.SemaphoreType.DMA,
         ],
-        out_shape=jax.ShapeDtypeStruct((4, LEAF, LANES), F32),
-        input_output_aliases={4: 0} if given else {},
-        compiler_params=pltpu.CompilerParams(vmem_limit_bytes=56 << 20),
+        out_shape=jax.ShapeDtypeStruct((4, size, LANES), F32),
+        compiler_params=pltpu.CompilerParams(vmem_limit_bytes=44 << 20),
         cost_estimate=pl.CostEstimate(
             flops=2 * size * LEAF * width, bytes_accessed=8 << 20, transcendentals=0
         ),
         name="near_rows",
-    )(rows, cols, tiles, points, *given)
+    )(rows, cols, tiles, points)
 
 
 FAR_ROWS = 512
 
 
-def far_rows(bases, place, pieces, near):
+def far_rows(bases, pieces, near):
     width = pieces[0].shape[1]
     steps = LEAF // FAR_ROWS
 
-    def body(place_s, bases_h, near_h, first, *refs):
-        *back, side_other, core_own, core_other, out_h, bases_v, near_v, out, ordered, rounded, sem = refs
+    def body(bases_h, first, *refs):
+        *back, side_other, core_own, core_other = refs[: len(pieces) - 1]
+        near_v = refs[len(pieces) - 1 : -6]
+        out_h, bases_v, out, ordered, rounded, sem = refs[-6:]
 
         def rows_of(step):
             return pl.ds(pl.multiple_of(step * FAR_ROWS, FAR_ROWS), FAR_ROWS)
@@ -157,16 +146,13 @@
                 bases_h.at[:, 0, rows_of(step), :], bases_v.at[:, rows_of(step), :], sem.at[0, step]
             )
 
-        def fetch_near(step):
-            return pltpu.make_async_copy(near_h.at[:, rows_of(step), :], near_v.at[:, rows_of(step), :], sem.at[1, step])
-
         def store(step):
-            return pltpu.make_async_copy(out.at[rows_of(step), :], out_h.at[rows_of(step), :], sem.at[2, step])
+            return pltpu.make_async_copy(out.at[rows_of(step), :], out_h.at[rows_of(step), :], sem.at[1, step])
 
         for step in range(steps):
             fetch_bases(step).start()
-            fetch_near(step).start()
-        ring, side, core = place_s[0], place_s[1], place_s[2]
+        inner = lax.axis_index("inner")
+        ring, side, core = lax.rem(inner, 4), inner // 4, lax.rem(lax.axis_index("outer"), 2)
 
         def put(row, value):
             ordered[pl.ds(pl.multiple_of(row, 8), value.shape[0]), :] = value
@@ -189,39 +175,36 @@
             put_upper(core_other.at[mask], 0, mask, 1 - core, 1 - side)
         rounded[...] = ordered[...].astype(BF16)
 
-        def compute(step, carry):
-            rows = rows_of(step)
-            fetch_bases(step).wait()
-            fetch_near(step).wait()
-            wide = jnp.concatenate([bases_v[h, rows, :] for h in range(LEVELS)], axis=1)
-            total = jnp.dot(wide, rounded[...], preferred_element_type=F32)
-            base = jnp.concatenate([near_v[q, rows, :] for q in range(4)], axis=1)
-            out[rows, :] = (total + base).astype(BF16)
-            store(step).start()
-            return carry
-
-        lax.fori_loop(0, steps, compute, 0)
+        step = 0
+        for part in near_v:
+            for top in range(0, part.shape[1], FAR_ROWS):
+                rows = rows_of(step)
+                fetch_bases(step).wait()
+                wide = jnp.concatenate([bases_v[h, rows, :] for h in range(LEVELS)], axis=1)
+                total = jnp.dot(wide, rounded[...], preferred_element_type=F32)
+                base = jnp.concatenate([part[q, top : top + FAR_ROWS, :] for q in range(4)], axis=1)
+                out[rows, :] = (total + base).astype(BF16)
+                store(step).start()
+                step += 1
         for step in range(steps):
             store(step).wait()
 
     return pl.pallas_call(
         body,
-        in_specs=[pl.BlockSpec(memory_space=pltpu.SMEM)]
-        + [pl.BlockSpec(memory_space=pl.ANY)] * 2
-        + [pl.BlockSpec(memory_space=pltpu.VMEM)] * len(pieces),
+        in_specs=[pl.BlockSpec(memory_space=pl.ANY)]
+        + [pl.BlockSpec(memory_space=pltpu.VMEM)] * (len(pieces) + len(near)),
         out_specs=pl.BlockSpec(memory_space=pl.ANY),
         scratch_shapes=[
             pltpu.VMEM((LEVELS, LEAF, RANK), BF16),
-            pltpu.VMEM((4, LEAF, LANES), F32),
             pltpu.VMEM((LEAF, width), BF16),
             pltpu.VMEM((LEVELS * RANK, width), F32),
             pltpu.VMEM((LEVELS * RANK, width), BF16),
-            pltpu.SemaphoreType.DMA((3, steps)),
+            pltpu.SemaphoreType.DMA((2, steps)),
         ],
         out_shape=jax.ShapeDtypeStruct((LEAF, width), BF16),
-        compiler_params=pltpu.CompilerParams(vmem_limit_bytes=56 << 20),
+        compiler_params=pltpu.CompilerParams(vmem_limit_bytes=44 << 20),
         name="far_rows",
-    )(place, bases, near, *pieces)
+    )(bases, *pieces, *near)
 
 
 def after(value, *others):
@@ -252,21 +235,21 @@
     mine3, other3 = halves_of(partial[3:4], side)
     mine, other = halves_of(upper, side)
     sent = jnp.concatenate([other3.reshape(64, width), other.reshape(96, width)], axis=0)
-    near = near_part(0, after(own_rows, sent), None)
+    near = [near_part(0, after(own_rows, sent))]
     received = flip(sent, 4)
     first = flip(after(partial[0], sent), 1)
-    received, first, near = lax.optimization_barrier((received, first, near))
+    received, first, near[0] = lax.optimization_barrier((received, first, near[0]))
     level3 = mine3 + received[None, :64]
     upper = mine + received[64:].reshape(3, 32, width)
     owned = jnp.concatenate([spread(partial[1:3], 4, 32), spread(level3, 4, 16), spread(upper, 4, 8)], axis=1)
     got = [lax.dynamic_index_in_dim(owned, ring, 0, keepdims=False)]
-    near = near_part(1, after(own_rows, owned), near)
+    near.append(near_part(1, after(own_rows, owned)))
     for mask in range(1, 4):
         got.append(flip(lax.dynamic_index_in_dim(owned, ring ^ mask, 0, keepdims=False), mask))
-    *got, near = lax.optimization_barrier((*got, near))
+    *got, near[1] = lax.optimization_barrier((*got, near[1]))
     level1 = [got[2][:32] + got[3][:32], got[0][:32] + got[1][:32]]
     total = got[0][32:] + got[1][32:] + got[2][32:] + got[3][32:]
-    near = near_part(2, after(own_rows, total), near)
+    near.append(near_part(2, after(own_rows, total)))
     level2 = flip(total[:32], 4)
     level3 = flip(total[32:48], 8)
     up4, up5, up6 = total[48:56], total[56:64], total[64:72]
@@ -275,20 +258,20 @@
     moved2, moved3 = flip(pair, 32), flip(pair, 48)
     level4 = moved1[:8]
     level5 = moved2[:8] + moved3[:8]
-    up6, near = lax.optimization_barrier((up6 + moved1[8:] + moved2[8:] + moved3[8:], near))
+    up6, near[2] = lax.optimization_barrier((up6 + moved1[8:] + moved2[8:] + moved3[8:], near[2]))
     level6 = flip(up6, 64)
     shared = jnp.concatenate([level2, level3, level4, level5, level6], axis=0)
-    near = near_part(3, after(own_rows, shared), near)
+    near.append(near_part(3, after(own_rows, shared)))
     back = []
     for mask in range(4):
         block = jnp.concatenate([level1[mask >> 1], shared], axis=0)
         back.append(flip(block, mask) if mask else block)
-    *back, near = lax.optimization_barrier((*back, near))
+    *back, near[3] = lax.optimization_barrier((*back, near[3]))
     both = jnp.stack([block[64:] for block in back])
-    near = near_part(4, after(own_rows, both), near)
+    near.append(near_part(4, after(own_rows, both)))
     core_own = flip(both[:, 16:], 8)
     side_other = flip(both, 4)
-    side_other, core_own, near = lax.optimization_barrier((side_other, core_own, near))
+    side_other, core_own, near[4] = lax.optimization_barrier((side_other, core_own, near[4]))
     core_other = flip(side_other[:, 16:], 8)
     return (first, *back, side_other, core_own, core_other), near
 
@@ -298,13 +281,11 @@
     width = local_points.shape[1]
     partial = jnp.einsum("hpr,pb->hrb", bases[:, 0], local_points, preferred_element_type=F32)
 
-    def near_part(part, own_rows, earlier):
-        return near_rows(*CHUNKS[part], own_rows, tile_cols, near_tiles[0], local_points, earlier)
+    def near_part(part, own_rows):
+        return near_rows(*CHUNKS[part], own_rows, tile_cols, near_tiles[0], local_points)
 
     pieces, near = siblings(partial, near_part, tile_rows)
-    inner, outer = lax.axis_index("inner"), lax.axis_index("outer")
-    place = jnp.stack([lax.rem(inner, 4), inner // 4, lax.rem(outer, 2)]).astype(jnp.int32)
-    return far_rows(bases, place, pieces, near)[None]
+    return far_rows(bases, pieces, near)[None]
 
 
 def solution(mesh):

time: 101 us -> 95.4 us (0.945)
  Pallas kernels: 58.8 us -> 51.3 us
  waiting for transfers between devices: 3.01 us -> 4.71 us
  local copies, waits for them, and re-layouts: 4.43 us -> 5.92 us
    pallas_call x5, Pallas kernels: 49.1 us -> 43.5 us  [near_rows(): pl.pallas_call(body, in_specs=[pl.BlockSpec(memory_space=pltpu.SMEM)] * 2...]
    pallas_call x1, Pallas kernels: 9.72 us -> 7.8 us  [far_rows(): pl.pallas_call(body, in_specs=[pl.BlockSpec(memory_space=pl.ANY)] + [pl.B...]
    ppermute x18, waiting for transfers between devices: 3.01 us -> 4.71 us  [flip(): return lax.ppermute(block, ('inner', 'outer'), route)]
    unnamed x21 -> x11, local copies, waits for them, and re-layouts: 1.95 us -> 3.44 us
  transfers between devices with their start and end apart: 18 -> 18, of which waited for: 3 -> 4; matrix products, arithmetic and copies ran while one was open for 3% -> 2% of each run, Pallas kernels for 49% -> 46%
where the time goes in v3:
time: 95.4 us; the launch traced here: 94.8 us
  Pallas kernels  51.3 us (54%)
  starting transfers between devices  23.9 us (25%)
  matrix products  8.11 us (9%)
  local copies, waits for them, and re-layouts  5.92 us (6%)
  waiting for transfers between devices  4.71 us (5%)
    pallas_call x5, Pallas kernels, near_rows(): pl.pallas_call(body, in_specs=[pl.BlockSpec(memory_space=pltpu.SMEM)] * 2...  43.5 us
    ppermute x18, starting transfers between devices, flip(): return lax.ppermute(block, ('inner', 'outer'), route)  23.9 us
    dot_general x1, matrix products, local(): jnp.einsum('hpr,pb->hrb', bases[:, 0], local_points, preferred_element_ty...  8.11 us
    pallas_call x1, Pallas kernels, far_rows(): pl.pallas_call(body, in_specs=[pl.BlockSpec(memory_space=pl.ANY)] + [pl.B...  7.8 us
    ppermute x18, waiting for transfers between devices, flip(): return lax.ppermute(block, ('inner', 'outer'), route)  4.71 us
    unnamed x11, local copies, waits for them, and re-layouts  3.44 us
  transfers between devices with their start and end apart: 18, of which 4 were waited for; matrix products, arithmetic and copies ran while one was open for 2% of the time, Pallas kernels for 46%

profile of v3, /device:TPU:1, one launch (start us, length us, event | category | flops | bytes accessed | tf_op | source)
XLA Modules:
  0.0 94.8 jit_solution(5559478924927991519)
XLA Ops:
  0.0 8.1 %fusion = f32[7,128,512]{2,1,0:T(8,128)S(1)} fusion(bf16[7,1,4096,128]{3,2,1,0:T(8,128)(2,1)} %bases_h.1, bf16[1,4096,512]{2,1,0:T(8,128)(2,1)} %param.5), kind=kOutput, calls=%fused_computation | convolution fusion | flops 3758096384 | bytes 13369344 | tf_op jit(solution)/shard_map/hpr,pb->hrb/dot_general | solution.py:282
  8.1 1.2 %copy-done.3 = f32[7,128,512]{2,1,0:T(8,128)} copy-done((f32[7,128,512]{2,1,0:T(8,128)}, f32[7,128,512]{2,1,0:T(8,128)S(1)}, u32[]{:S(2)}) %copy-start.3) | copy-done | bytes 1835032
  9.4 1.5 %collective-permute-start = (f32[3,64,512]{2,1,0:T(8,128)S(1)}, f32[3,64,512]{2,1,0:T(8,128)S(1)}, u32[]{:S(2)}, u32[]{:S(2)}) collective-permute-start(f32[3,64,512]{2,1,0:T(8,128)S(1)} %dynamic-slice_bitcast_fusion), channel_id=1, source_target_pairs={{0,1},{16,17},{32,33},{48,49},{64,65},{80,81},{96,97},{112,113},{1... | collective-permute-start | bytes 1179656 | tf_op jit(solution)/shard_map/ppermute | solution.py:30
  10.9 1.1 %slice.125 = f32[2,128,512]{2,1,0:T(8,128)S(1)} slice(f32[7,128,512]{2,1,0:T(8,128)} %copy-done.3), slice={[1:3], [0:128], [0:512]} | slice | bytes 1048576 | tf_op jit(solution)/shard_map/slice | solution.py:244
  12.1 1.1 %slice_bitcast_fusion = (f32[128,512]{1,0:T(8,128)S(1)}, f32[1,128,512]{2,1,0:T(8,128)S(1)}) fusion(f32[7,128,512]{2,1,0:T(8,128)} %copy-done.3), kind=kLoop, calls=%fused_computation.8 | loop fusion | bytes 1048576 | tf_op jit(solution)/shard_map/squeeze | solution.py:240
  13.4 1.4 %collective-permute-start.1 = (f32[160,512]{1,0:T(8,128)S(1)}, f32[160,512]{1,0:T(8,128)S(1)}, u32[]{:S(2)}, u32[]{:S(2)}) collective-permute-start(f32[160,512]{1,0:T(8,128)S(1)} %pad_maximum_fusion.1), channel_id=1, source_target_pairs={{0,64},{16,80},{32,96},{48,112},{64,0},{80,16},{96,32},{112,48},{1... | collective-permute-start | bytes 983048 | tf_op jit(solution)/shard_map/ppermute | solution.py:30
  14.7 1.3 %collective-permute-start.2 = (f32[128,512]{1,0:T(8,128)S(1)}, f32[128,512]{1,0:T(8,128)S(1)}, u32[]{:S(2)}, u32[]{:S(2)}) collective-permute-start(f32[128,512]{1,0:T(8,128)S(1)} %get-tuple-element.28), channel_id=1, source_target_pairs={{0,16},{16,0},{32,48},{48,32},{64,80},{80,64},{96,112},{112,96},{1... | collective-permute-start | bytes 786440 | tf_op jit(solution)/shard_map/ppermute | solution.py:30
  16.0 2.2 %copy-done = bf16[1,4096,512]{2,1,0:T(8,128)(2,1)S(1)} copy-done((bf16[1,4096,512]{2,1,0:T(8,128)(2,1)S(1)}, bf16[1,4096,512]{2,1,0:T(8,128)(2,1)}, u32[]{:S(2)}) %copy-start) | copy-done | bytes 4194328
  18.2 10.3 %near_rows.5.refs_7_ = f32[4,1024,128]{2,1,0:T(8,128)S(1)} custom-call(s32[1,768]{1,0:T(1,128)S(1)} %copy-done.1, s32[1,768]{1,0:T(1,128)S(1)} %copy-done.2, bf16[768,4096]{1,0:T(8,128)(2,1)} %bitcast.60, bf16[4096,512]{1,0:T(8,128)(2,1)S(1)} %bitcast.55), custom_call_target="tpu_custom_call" | custom-call | flops 4294967296 | bytes 8388608 | tf_op jit(solution)/shard_map/near_rows/pallas_call | solution.py:108
  28.8 2.0 %collective-permute-start.5 = (f32[104,512]{1,0:T(8,128)S(1)}, f32[104,512]{1,0:T(8,128)S(1)}, u32[]{:S(2)}, u32[]{:S(2)}) collective-permute-start(f32[104,512]{1,0:T(8,128)S(1)} %get-tuple-element.53), channel_id=1, source_target_pairs={{0,48},{16,32},{32,16},{48,0},{64,112},{80,96},{96,80},{112,64},{1... | collective-permute-start | bytes 638984 | tf_op jit(solution)/shard_map/ppermute | solution.py:30
  30.7 0.8 collective-permute-start.4
  31.6 0.5 collective-permute-start.3
  32.1 10.3 %near_rows.6.refs_8_ = f32[4,1024,128]{2,1,0:T(8,128)S(1)} custom-call(s32[1,768]{1,0:T(1,128)S(1)} %copy-done.1, s32[1,768]{1,0:T(1,128)S(1)} %copy-done.2, bf16[768,4096]{1,0:T(8,128)(2,1)} %bitcast.61, bf16[4096,512]{1,0:T(8,128)(2,1)S(1)} %bitcast.56), custom_call_target="tpu_custom_call" | custom-call | flops 4294967296 | bytes 8388608 | tf_op jit(solution)/shard_map/near_rows/pallas_call | solution.py:108
  42.5 4.1 %collective-permute-start.10 = (f32[16,512]{1,0:T(8,128)S(1)}, f32[16,512]{1,0:T(8,128)S(1)}, u32[]{:S(2)}, u32[]{:S(2)}) collective-permute-start(f32[16,512]{1,0:T(8,128)S(1)} %get-tuple-element.57), channel_id=1, source_target_pairs={{0,6},{16,22},{32,38},{48,54},{64,70},{80,86},{96,102},{112,118},{... | collective-permute-start | bytes 98312 | tf_op jit(solution)/shard_map/ppermute | solution.py:30
  46.6 0.7 collective-permute-start.8
  47.2 1.5 %collective-permute-start.7 = (f32[16,512]{1,0:T(8,128)S(1)}, f32[16,512]{1,0:T(8,128)S(1)}, u32[]{:S(2)}, u32[]{:S(2)}) collective-permute-start(f32[16,512]{1,0:T(8,128)S(1)} %get-tuple-element.58), channel_id=1, source_target_pairs={{0,1},{16,17},{32,33},{48,49},{64,65},{80,81},{96,97},{112,113},{1... | collective-permute-start | bytes 98312 | tf_op jit(solution)/shard_map/ppermute | solution.py:30
  48.8 0.3 collective-permute-start.6
  49.0 10.3 %near_rows.7.refs_9_ = f32[4,1024,128]{2,1,0:T(8,128)S(1)} custom-call(s32[1,768]{1,0:T(1,128)S(1)} %copy-done.1, s32[1,768]{1,0:T(1,128)S(1)} %copy-done.2, bf16[768,4096]{1,0:T(8,128)(2,1)} %bitcast.62, bf16[4096,512]{1,0:T(8,128)(2,1)S(1)} %bitcast.57), custom_call_target="tpu_custom_call" | custom-call | flops 4294967296 | bytes 8388608 | tf_op jit(solution)/shard_map/near_rows/pallas_call | solution.py:108
  59.4 2.6 %collective-permute-start.11 = (f32[8,512]{1,0:T(8,128)S(1)}, f32[8,512]{1,0:T(8,128)S(1)}, u32[]{:S(2)}, u32[]{:S(2)}) collective-permute-start(f32[8,512]{1,0:T(8,128)S(1)} %get-tuple-element.38), channel_id=1, source_target_pairs={{0,8},{16,24},{32,40},{48,56},{64,72},{80,88},{96,104},{112,120},{... | collective-permute-start | bytes 49160 | tf_op jit(solution)/shard_map/ppermute | solution.py:30
  62.0 1.6 %collective-permute-done.11 = f32[8,512]{1,0:T(8,128)S(1)} collective-permute-done((f32[8,512]{1,0:T(8,128)S(1)}, f32[8,512]{1,0:T(8,128)S(1)}, u32[]{:S(2)}, u32[]{:S(2)}) %collective-permute-start.11) | collective-permute-done | bytes 16416 | tf_op jit(solution)/shard_map/ppermute | solution.py:30
  63.6 1.9 %collective-permute-start.14 = (f32[104,512]{1,0:T(8,128)S(1)}, f32[104,512]{1,0:T(8,128)S(1)}, u32[]{:S(2)}, u32[]{:S(2)}) collective-permute-start(f32[104,512]{1,0:T(8,128)S(1)} %get-tuple-element.70), channel_id=1, source_target_pairs={{0,48},{16,32},{32,16},{48,0},{64,112},{80,96},{96,80},{112,64},{1... | collective-permute-start | bytes 638984 | tf_op jit(solution)/shard_map/ppermute | solution.py:30
  65.5 1.0 %collective-permute-start.13 = (f32[104,512]{1,0:T(8,128)S(1)}, f32[104,512]{1,0:T(8,128)S(1)}, u32[]{:S(2)}, u32[]{:S(2)}) collective-permute-start(f32[104,512]{1,0:T(8,128)S(1)} %get-tuple-element.70), channel_id=1, source_target_pairs={{0,32},{16,48},{32,0},{48,16},{64,96},{80,112},{96,64},{112,80},{1... | collective-permute-start | bytes 638984 | tf_op jit(solution)/shard_map/ppermute | solution.py:30
  66.5 0.4 collective-permute-start.12
  66.9 6.6 %near_rows.8.refs_10_ = f32[4,512,128]{2,1,0:T(8,128)S(1)} custom-call(s32[1,768]{1,0:T(1,128)S(1)} %copy-done.1, s32[1,768]{1,0:T(1,128)S(1)} %copy-done.2, bf16[768,4096]{1,0:T(8,128)(2,1)} %bitcast.63, bf16[4096,512]{1,0:T(8,128)(2,1)S(1)} %bitcast.58), custom_call_target="tpu_custom_call" | custom-call | flops 2147483648 | bytes 8388608 | tf_op jit(solution)/shard_map/near_rows/pallas_call | solution.py:108
  73.4 0.4 collective-permute-done.14.refs_3_
  73.8 1.5 %collective-permute-done.12.refs_1_ = f32[104,512]{1,0:T(8,128)S(1)} collective-permute-done((f32[104,512]{1,0:T(8,128)S(1)}, f32[104,512]{1,0:T(8,128)S(1)}, u32[]{:S(2)}, u32[]{:S(2)}) %collective-permute-start.12) | collective-permute-done | bytes 213024 | tf_op jit(solution)/shard_map/ppermute | solution.py:30
  75.4 0.3 collective-permute-start.15
  75.7 3.5 %collective-permute-start.16 = (f32[4,24,512]{2,1,0:T(8,128)S(1)}, f32[4,24,512]{2,1,0:T(8,128)S(1)}, u32[]{:S(2)}, u32[]{:S(2)}) collective-permute-start(f32[4,24,512]{2,1,0:T(8,128)S(1)} %slice.136), channel_id=1, source_target_pairs={{0,1},{16,17},{32,33},{48,49},{64,65},{80,81},{96,97},{112,113},{1... | collective-permute-start | bytes 589832 | tf_op jit(solution)/shard_map/ppermute | solution.py:30
  79.2 6.1 %near_rows.9.refs_11_ = f32[4,512,128]{2,1,0:T(8,128)S(1)} custom-call(s32[1,768]{1,0:T(1,128)S(1)} %copy-done.1, s32[1,768]{1,0:T(1,128)S(1)} %copy-done.2, bf16[768,4096]{1,0:T(8,128)(2,1)} %bitcast.64, bf16[4096,512]{1,0:T(8,128)(2,1)S(1)} %bitcast.59), custom_call_target="tpu_custom_call" | custom-call | flops 2147483648 | bytes 8388608 | tf_op jit(solution)/shard_map/near_rows/pallas_call | solution.py:108
  85.3 0.4 collective-permute-start.17
  85.7 1.1 %collective-permute-done.17.refs_6_ = f32[4,24,512]{2,1,0:T(8,128)S(1)} collective-permute-done((f32[4,24,512]{2,1,0:T(8,128)S(1)}, f32[4,24,512]{2,1,0:T(8,128)S(1)}, u32[]{:S(2)}, u32[]{:S(2)}) %collective-permute-start.17) | collective-permute-done | bytes 196640 | tf_op jit(solution)/shard_map/ppermute | solution.py:30
  86.9 7.8 %far_rows.1 = bf16[4096,512]{1,0:T(8,128)(2,1)} custom-call(bf16[7,1,4096,128]{3,2,1,0:T(8,128)(2,1)} %bases_h.1, f32[128,512]{1,0:T(8,128)S(1)} %collective-permute-done.2.first, f32[104,512]{1,0:T(8,128)S(1)} %get-tuple-element.39.refs_0_, f32[104,512]{1,0:T(8,128)S(1)} %collective-permute-done.12.refs_1_, f32[104,512]{1,0:T(8,128)S(1)} %collective-permute-done.13.refs_2_, ...), custom_call_target="tpu_custom_call" | custom-call | tf_op jit(solution)/shard_map/far_rows/pallas_call | solution.py:192
  (51 shorter events, 0.7 us)
Async XLA Ops:
  8.1 1.2 %copy-start.3 = (f32[7,128,512]{2,1,0:T(8,128)}, f32[7,128,512]{2,1,0:T(8,128)S(1)}, u32[]{:S(2)}) copy-start(f32[7,128,512]{2,1,0:T(8,128)S(1)} %fusion) | copy-start | bytes 5505028
  9.3 6.7 %copy-start.1 = (s32[1,768]{1,0:T(1,128)S(1)}, s32[1,768]{1,0:T(1,128)}, u32[]{:S(2)}) copy-start(s32[1,768]{1,0:T(1,128)} %refs_0_.4) | copy-start | bytes 9220
  9.3 6.7 %copy-start.2 = (s32[1,768]{1,0:T(1,128)S(1)}, s32[1,768]{1,0:T(1,128)}, u32[]{:S(2)}) copy-start(s32[1,768]{1,0:T(1,128)} %refs_1_.9) | copy-start | bytes 9220
  9.4 3.8 %collective-permute-start = (f32[3,64,512]{2,1,0:T(8,128)S(1)}, f32[3,64,512]{2,1,0:T(8,128)S(1)}, u32[]{:S(2)}, u32[]{:S(2)}) collective-permute-start(f32[3,64,512]{2,1,0:T(8,128)S(1)} %dynamic-slice_bitcast_fusion), channel_id=1, source_target_pairs={{0,1},{16,17},{32,33},{48,49},{64,65},{80,81},{96,97},{112,113},{1... | collective-permute-start | bytes 1179656 | tf_op jit(solution)/shard_map/ppermute | solution.py:30
  13.4 15.1 %collective-permute-start.1 = (f32[160,512]{1,0:T(8,128)S(1)}, f32[160,512]{1,0:T(8,128)S(1)}, u32[]{:S(2)}, u32[]{:S(2)}) collective-permute-start(f32[160,512]{1,0:T(8,128)S(1)} %pad_maximum_fusion.1), channel_id=1, source_target_pairs={{0,64},{16,80},{32,96},{48,112},{64,0},{80,16},{96,32},{112,48},{1... | collective-permute-start | bytes 983048 | tf_op jit(solution)/shard_map/ppermute | solution.py:30
  14.7 13.8 %collective-permute-start.2 = (f32[128,512]{1,0:T(8,128)S(1)}, f32[128,512]{1,0:T(8,128)S(1)}, u32[]{:S(2)}, u32[]{:S(2)}) collective-permute-start(f32[128,512]{1,0:T(8,128)S(1)} %get-tuple-element.28), channel_id=1, source_target_pairs={{0,16},{16,0},{32,48},{48,32},{64,80},{80,64},{96,112},{112,96},{1... | collective-permute-start | bytes 786440 | tf_op jit(solution)/shard_map/ppermute | solution.py:30
  16.0 2.2 %copy-start = (bf16[1,4096,512]{2,1,0:T(8,128)(2,1)S(1)}, bf16[1,4096,512]{2,1,0:T(8,128)(2,1)}, u32[]{:S(2)}) copy-start(bf16[1,4096,512]{2,1,0:T(8,128)(2,1)} %param.5) | copy-start | bytes 12582916
  28.8 13.6 %collective-permute-start.5 = (f32[104,512]{1,0:T(8,128)S(1)}, f32[104,512]{1,0:T(8,128)S(1)}, u32[]{:S(2)}, u32[]{:S(2)}) collective-permute-start(f32[104,512]{1,0:T(8,128)S(1)} %get-tuple-element.53), channel_id=1, source_target_pairs={{0,48},{16,32},{32,16},{48,0},{64,112},{80,96},{96,80},{112,64},{1... | collective-permute-start | bytes 638984 | tf_op jit(solution)/shard_map/ppermute | solution.py:30
  30.7 11.6 %collective-permute-start.4 = (f32[104,512]{1,0:T(8,128)S(1)}, f32[104,512]{1,0:T(8,128)S(1)}, u32[]{:S(2)}, u32[]{:S(2)}) collective-permute-start(f32[104,512]{1,0:T(8,128)S(1)} %get-tuple-element.54), channel_id=1, source_target_pairs={{0,32},{16,48},{32,0},{48,16},{64,96},{80,112},{96,64},{112,80},{1... | collective-permute-start | bytes 638984 | tf_op jit(solution)/shard_map/ppermute | solution.py:30
  31.6 10.8 %collective-permute-start.3 = (f32[104,512]{1,0:T(8,128)S(1)}, f32[104,512]{1,0:T(8,128)S(1)}, u32[]{:S(2)}, u32[]{:S(2)}) collective-permute-start(f32[104,512]{1,0:T(8,128)S(1)} %get-tuple-element.55), channel_id=1, source_target_pairs={{0,16},{16,0},{32,48},{48,32},{64,80},{80,64},{96,112},{112,96},{1... | collective-permute-start | bytes 638984 | tf_op jit(solution)/shard_map/ppermute | solution.py:30
  42.5 16.9 %collective-permute-start.10 = (f32[16,512]{1,0:T(8,128)S(1)}, f32[16,512]{1,0:T(8,128)S(1)}, u32[]{:S(2)}, u32[]{:S(2)}) collective-permute-start(f32[16,512]{1,0:T(8,128)S(1)} %get-tuple-element.57), channel_id=1, source_target_pairs={{0,6},{16,22},{32,38},{48,54},{64,70},{80,86},{96,102},{112,118},{... | collective-permute-start | bytes 98312 | tf_op jit(solution)/shard_map/ppermute | solution.py:30
  46.6 12.8 %collective-permute-start.9 = (f32[16,512]{1,0:T(8,128)S(1)}, f32[16,512]{1,0:T(8,128)S(1)}, u32[]{:S(2)}, u32[]{:S(2)}) collective-permute-start(f32[16,512]{1,0:T(8,128)S(1)} %get-tuple-element.57), channel_id=1, source_target_pairs={{0,4},{16,20},{32,36},{48,52},{64,68},{80,84},{96,100},{112,116},{... | collective-permute-start | bytes 98312 | tf_op jit(solution)/shard_map/ppermute | solution.py:30
  46.6 12.8 %collective-permute-start.8 = (f32[16,512]{1,0:T(8,128)S(1)}, f32[16,512]{1,0:T(8,128)S(1)}, u32[]{:S(2)}, u32[]{:S(2)}) collective-permute-start(f32[16,512]{1,0:T(8,128)S(1)} %pad_maximum_fusion.3), channel_id=1, source_target_pairs={{0,2},{16,18},{32,34},{48,50},{64,66},{80,82},{96,98},{112,114},{1... | collective-permute-start | bytes 98312 | tf_op jit(solution)/shard_map/ppermute | solution.py:30
  47.2 12.1 %collective-permute-start.7 = (f32[16,512]{1,0:T(8,128)S(1)}, f32[16,512]{1,0:T(8,128)S(1)}, u32[]{:S(2)}, u32[]{:S(2)}) collective-permute-start(f32[16,512]{1,0:T(8,128)S(1)} %get-tuple-element.58), channel_id=1, source_target_pairs={{0,1},{16,17},{32,33},{48,49},{64,65},{80,81},{96,97},{112,113},{1... | collective-permute-start | bytes 98312 | tf_op jit(solution)/shard_map/ppermute | solution.py:30
  48.8 10.6 %collective-permute-start.6 = (f32[32,512]{1,0:T(8,128)S(1)}, f32[32,512]{1,0:T(8,128)S(1)}, u32[]{:S(2)}, u32[]{:S(2)}) collective-permute-start(f32[32,512]{1,0:T(8,128)S(1)} %slice.126), channel_id=1, source_target_pairs={{0,64},{16,80},{32,96},{48,112},{64,0},{80,16},{96,32},{112,48},{1... | collective-permute-start | bytes 196616 | tf_op jit(solution)/shard_map/ppermute | solution.py:30
  59.4 4.2 %collective-permute-start.11 = (f32[8,512]{1,0:T(8,128)S(1)}, f32[8,512]{1,0:T(8,128)S(1)}, u32[]{:S(2)}, u32[]{:S(2)}) collective-permute-start(f32[8,512]{1,0:T(8,128)S(1)} %get-tuple-element.38), channel_id=1, source_target_pairs={{0,8},{16,24},{32,40},{48,56},{64,72},{80,88},{96,104},{112,120},{... | collective-permute-start | bytes 49160 | tf_op jit(solution)/shard_map/ppermute | solution.py:30
  63.6 10.2 %collective-permute-start.14 = (f32[104,512]{1,0:T(8,128)S(1)}, f32[104,512]{1,0:T(8,128)S(1)}, u32[]{:S(2)}, u32[]{:S(2)}) collective-permute-start(f32[104,512]{1,0:T(8,128)S(1)} %get-tuple-element.70), channel_id=1, source_target_pairs={{0,48},{16,32},{32,16},{48,0},{64,112},{80,96},{96,80},{112,64},{1... | collective-permute-start | bytes 638984 | tf_op jit(solution)/shard_map/ppermute | solution.py:30
  65.5 8.3 %collective-permute-start.13 = (f32[104,512]{1,0:T(8,128)S(1)}, f32[104,512]{1,0:T(8,128)S(1)}, u32[]{:S(2)}, u32[]{:S(2)}) collective-permute-start(f32[104,512]{1,0:T(8,128)S(1)} %get-tuple-element.70), channel_id=1, source_target_pairs={{0,32},{16,48},{32,0},{48,16},{64,96},{80,112},{96,64},{112,80},{1... | collective-permute-start | bytes 638984 | tf_op jit(solution)/shard_map/ppermute | solution.py:30
  66.5 8.8 %collective-permute-start.12 = (f32[104,512]{1,0:T(8,128)S(1)}, f32[104,512]{1,0:T(8,128)S(1)}, u32[]{:S(2)}, u32[]{:S(2)}) collective-permute-start(f32[104,512]{1,0:T(8,128)S(1)} %get-tuple-element.39.refs_0_), channel_id=1, source_target_pairs={{0,16},{16,0},{32,48},{48,32},{64,80},{80,64},{96,112},{112,96},{1... | collective-permute-start | bytes 638984 | tf_op jit(solution)/shard_map/ppermute | solution.py:30
  75.4 9.9 %collective-permute-start.15 = (f32[4,40,512]{2,1,0:T(8,128)S(1)}, f32[4,40,512]{2,1,0:T(8,128)S(1)}, u32[]{:S(2)}, u32[]{:S(2)}) collective-permute-start(f32[4,40,512]{2,1,0:T(8,128)S(1)} %pad_maximum_fusion.2), channel_id=1, source_target_pairs={{0,64},{16,80},{32,96},{48,112},{64,0},{80,16},{96,32},{112,48},{1... | collective-permute-start | bytes 983048 | tf_op jit(solution)/shard_map/ppermute | solution.py:30
  75.7 9.6 %collective-permute-start.16 = (f32[4,24,512]{2,1,0:T(8,128)S(1)}, f32[4,24,512]{2,1,0:T(8,128)S(1)}, u32[]{:S(2)}, u32[]{:S(2)}) collective-permute-start(f32[4,24,512]{2,1,0:T(8,128)S(1)} %slice.136), channel_id=1, source_target_pairs={{0,1},{16,17},{32,33},{48,49},{64,65},{80,81},{96,97},{112,113},{1... | collective-permute-start | bytes 589832 | tf_op jit(solution)/shard_map/ppermute | solution.py:30
  85.3 1.5 %collective-permute-start.17 = (f32[4,24,512]{2,1,0:T(8,128)S(1)}, f32[4,24,512]{2,1,0:T(8,128)S(1)}, u32[]{:S(2)}, u32[]{:S(2)}) collective-permute-start(f32[4,24,512]{2,1,0:T(8,128)S(1)} %slice.121), channel_id=1, source_target_pairs={{0,1},{16,17},{32,33},{48,49},{64,65},{80,81},{96,97},{112,113},{1... | collective-permute-start | bytes 589832 | tf_op jit(solution)/shard_map/ppermute | solution.py:30

commit v4 on v3

--- a/solution.py
+++ b/solution.py
@@ -15,7 +15,7 @@
 PAIR = TILE // 2
 LANES = 128
 PEERS = 8
-CHUNKS = ((0, 16), (16, 16), (32, 16), (48, 8), (56, 8))
+CHUNKS = ((0, 16), (16, 16), (32, 8), (40, 16), (56, 8))
 MM_ROWS = 512
 
 BF16 = jnp.bfloat16
@@ -118,7 +118,7 @@
             pltpu.SemaphoreType.DMA,
         ],
         out_shape=jax.ShapeDtypeStruct((4, size, LANES), F32),
-        compiler_params=pltpu.CompilerParams(vmem_limit_bytes=44 << 20),
+        compiler_params=pltpu.CompilerParams(vmem_limit_bytes=(44 if first else 54) << 20),
         cost_estimate=pl.CostEstimate(
             flops=2 * size * LEAF * width, bytes_accessed=8 << 20, transcendentals=0
         ),

time: 95.4 us -> 93.2 us (0.977)
  local copies, waits for them, and re-layouts: 5.92 us -> 3.74 us
  waiting for transfers between devices: 4.71 us -> 2.6 us
  Pallas kernels: 51.3 us -> 52.7 us
  starting transfers between devices: 23.9 us -> 25.1 us
    unnamed x11 -> x13, local copies, waits for them, and re-layouts: 3.44 us -> 1.27 us
    ppermute x18, waiting for transfers between devices: 4.71 us -> 2.6 us  [flip(): return lax.ppermute(block, ('inner', 'outer'), route)]
    pallas_call x5, Pallas kernels: 43.5 us -> 44.9 us  [near_rows(): pl.pallas_call(body, in_specs=[pl.BlockSpec(memory_space=pltpu.SMEM)] * 2...]
    ppermute x18, starting transfers between devices: 23.9 us -> 25.1 us  [flip(): return lax.ppermute(block, ('inner', 'outer'), route)]
  transfers between devices with their start and end apart: 18 -> 18, of which waited for: 4 -> 2; matrix products, arithmetic and copies ran while one was open for 2% -> 2% of each run, Pallas kernels for 46% -> 48%
where the time goes in v4:
time: 93.2 us
  Pallas kernels  52.7 us (57%)
  starting transfers between devices  25.1 us (27%)
  matrix products  8.11 us (9%)
  local copies, waits for them, and re-layouts  3.74 us (4%)
  waiting for transfers between devices  2.6 us (3%)
    pallas_call x5, Pallas kernels, near_rows(): pl.pallas_call(body, in_specs=[pl.BlockSpec(memory_space=pltpu.SMEM)] * 2...  44.9 us
    ppermute x18, starting transfers between devices, flip(): return lax.ppermute(block, ('inner', 'outer'), route)  25.1 us
    dot_general x1, matrix products, local(): jnp.einsum('hpr,pb->hrb', bases[:, 0], local_points, preferred_element_ty...  8.11 us
    pallas_call x1, Pallas kernels, far_rows(): pl.pallas_call(body, in_specs=[pl.BlockSpec(memory_space=pl.ANY)] + [pl.B...  7.8 us
    ppermute x18, waiting for transfers between devices, flip(): return lax.ppermute(block, ('inner', 'outer'), route)  2.6 us
  transfers between devices with their start and end apart: 18, of which 2 were waited for; matrix products, arithmetic and copies ran while one was open for 2% of the time, Pallas kernels for 48%

profile of v4, /device:TPU:1, one launch (start us, length us, event | category | flops | bytes accessed | tf_op | source)
XLA Modules:
  0.0 93.2 jit_solution(10719258128551080167)
XLA Ops:
  0.0 8.1 %fusion = f32[7,128,512]{2,1,0:T(8,128)S(1)} fusion(bf16[7,1,4096,128]{3,2,1,0:T(8,128)(2,1)} %bases_h.1, bf16[1,4096,512]{2,1,0:T(8,128)(2,1)} %param.5), kind=kOutput, calls=%fused_computation | convolution fusion | flops 3758096384 | bytes 13369344 | tf_op jit(solution)/shard_map/hpr,pb->hrb/dot_general | solution.py:282
  8.1 1.2 %copy-done.4 = f32[7,128,512]{2,1,0:T(8,128)} copy-done((f32[7,128,512]{2,1,0:T(8,128)}, f32[7,128,512]{2,1,0:T(8,128)S(1)}, u32[]{:S(2)}) %copy-start.4) | copy-done | bytes 1835032
  9.4 1.5 %collective-permute-start = (f32[3,64,512]{2,1,0:T(8,128)S(1)}, f32[3,64,512]{2,1,0:T(8,128)S(1)}, u32[]{:S(2)}, u32[]{:S(2)}) collective-permute-start(f32[3,64,512]{2,1,0:T(8,128)S(1)} %dynamic-slice_bitcast_fusion), channel_id=1, source_target_pairs={{0,1},{16,17},{32,33},{48,49},{64,65},{80,81},{96,97},{112,113},{1... | collective-permute-start | bytes 1179656 | tf_op jit(solution)/shard_map/ppermute | solution.py:30
  10.9 1.1 %slice.125 = f32[2,128,512]{2,1,0:T(8,128)S(1)} slice(f32[7,128,512]{2,1,0:T(8,128)} %copy-done.4), slice={[1:3], [0:128], [0:512]} | slice | bytes 1048576 | tf_op jit(solution)/shard_map/slice | solution.py:244
  12.1 1.1 %slice_bitcast_fusion = (f32[128,512]{1,0:T(8,128)S(1)}, f32[1,128,512]{2,1,0:T(8,128)S(1)}) fusion(f32[7,128,512]{2,1,0:T(8,128)} %copy-done.4), kind=kLoop, calls=%fused_computation.8 | loop fusion | bytes 1048576 | tf_op jit(solution)/shard_map/squeeze | solution.py:240
  13.2 0.1 bitcast_add_fusion
  13.4 1.4 %collective-permute-start.1 = (f32[160,512]{1,0:T(8,128)S(1)}, f32[160,512]{1,0:T(8,128)S(1)}, u32[]{:S(2)}, u32[]{:S(2)}) collective-permute-start(f32[160,512]{1,0:T(8,128)S(1)} %pad_maximum_fusion.1), channel_id=1, source_target_pairs={{0,64},{16,80},{32,96},{48,112},{64,0},{80,16},{96,32},{112,48},{1... | collective-permute-start | bytes 983048 | tf_op jit(solution)/shard_map/ppermute | solution.py:30
  14.7 1.3 %collective-permute-start.2 = (f32[128,512]{1,0:T(8,128)S(1)}, f32[128,512]{1,0:T(8,128)S(1)}, u32[]{:S(2)}, u32[]{:S(2)}) collective-permute-start(f32[128,512]{1,0:T(8,128)S(1)} %get-tuple-element.28), channel_id=1, source_target_pairs={{0,16},{16,0},{32,48},{48,32},{64,80},{80,64},{96,112},{112,96},{1... | collective-permute-start | bytes 786440 | tf_op jit(solution)/shard_map/ppermute | solution.py:30
  16.0 11.7 %near_rows.5.refs_7_ = f32[4,1024,128]{2,1,0:T(8,128)} custom-call(s32[1,768]{1,0:T(1,128)} %refs_0_.4, s32[1,768]{1,0:T(1,128)} %refs_1_.9, bf16[768,4096]{1,0:T(8,128)(2,1)} %bitcast.60, bf16[4096,512]{1,0:T(8,128)(2,1)} %bitcast.55), custom_call_target="tpu_custom_call" | custom-call | flops 4294967296 | bytes 8388608 | tf_op jit(solution)/shard_map/near_rows/pallas_call | solution.py:108
  27.8 0.1 pad_maximum_fusion
  27.9 0.1 dynamic-slice_bitcast_fusion.1
  28.0 2.0 %collective-permute-start.5 = (f32[104,512]{1,0:T(8,128)S(1)}, f32[104,512]{1,0:T(8,128)S(1)}, u32[]{:S(2)}, u32[]{:S(2)}) collective-permute-start(f32[104,512]{1,0:T(8,128)S(1)} %get-tuple-element.53), channel_id=1, source_target_pairs={{0,48},{16,32},{32,16},{48,0},{64,112},{80,96},{96,80},{112,64},{1... | collective-permute-start | bytes 638984 | tf_op jit(solution)/shard_map/ppermute | solution.py:30
  30.0 0.6 collective-permute-start.4
  30.5 0.8 collective-permute-start.3
  31.3 10.3 %near_rows.6.refs_8_ = f32[4,1024,128]{2,1,0:T(8,128)S(1)} custom-call(s32[1,768]{1,0:T(1,128)S(1)} %copy-done.2, s32[1,768]{1,0:T(1,128)S(1)} %copy-done.3, bf16[768,4096]{1,0:T(8,128)(2,1)} %bitcast.61, bf16[4096,512]{1,0:T(8,128)(2,1)S(1)} %bitcast.56), custom_call_target="tpu_custom_call" | custom-call | flops 4294967296 | bytes 8388608 | tf_op jit(solution)/shard_map/near_rows/pallas_call | solution.py:108
  41.7 3.6 %collective-permute-start.10 = (f32[16,512]{1,0:T(8,128)S(1)}, f32[16,512]{1,0:T(8,128)S(1)}, u32[]{:S(2)}, u32[]{:S(2)}) collective-permute-start(f32[16,512]{1,0:T(8,128)S(1)} %get-tuple-element.57), channel_id=1, source_target_pairs={{0,6},{16,22},{32,38},{48,54},{64,70},{80,86},{96,102},{112,118},{... | collective-permute-start | bytes 98312 | tf_op jit(solution)/shard_map/ppermute | solution.py:30
  45.3 0.2 collective-permute-start.9
  45.5 0.5 collective-permute-start.8
  46.0 2.5 %collective-permute-start.7 = (f32[16,512]{1,0:T(8,128)S(1)}, f32[16,512]{1,0:T(8,128)S(1)}, u32[]{:S(2)}, u32[]{:S(2)}) collective-permute-start(f32[16,512]{1,0:T(8,128)S(1)} %get-tuple-element.58), channel_id=1, source_target_pairs={{0,1},{16,17},{32,33},{48,49},{64,65},{80,81},{96,97},{112,113},{1... | collective-permute-start | bytes 98312 | tf_op jit(solution)/shard_map/ppermute | solution.py:30
  48.5 6.1 %near_rows.7.refs_9_ = f32[4,512,128]{2,1,0:T(8,128)S(1)} custom-call(s32[1,768]{1,0:T(1,128)S(1)} %copy-done.2, s32[1,768]{1,0:T(1,128)S(1)} %copy-done.3, bf16[768,4096]{1,0:T(8,128)(2,1)} %bitcast.62, bf16[4096,512]{1,0:T(8,128)(2,1)S(1)} %bitcast.57), custom_call_target="tpu_custom_call" | custom-call | flops 2147483648 | bytes 8388608 | tf_op jit(solution)/shard_map/near_rows/pallas_call | solution.py:108
  54.8 3.1 %collective-permute-start.11 = (f32[8,512]{1,0:T(8,128)S(1)}, f32[8,512]{1,0:T(8,128)S(1)}, u32[]{:S(2)}, u32[]{:S(2)}) collective-permute-start(f32[8,512]{1,0:T(8,128)S(1)} %get-tuple-element.38), channel_id=1, source_target_pairs={{0,8},{16,24},{32,40},{48,56},{64,72},{80,88},{96,104},{112,120},{... | collective-permute-start | bytes 49160 | tf_op jit(solution)/shard_map/ppermute | solution.py:30
  57.9 1.1 %collective-permute-done.11 = f32[8,512]{1,0:T(8,128)S(1)} collective-permute-done((f32[8,512]{1,0:T(8,128)S(1)}, f32[8,512]{1,0:T(8,128)S(1)}, u32[]{:S(2)}, u32[]{:S(2)}) %collective-permute-start.11) | collective-permute-done | bytes 16416 | tf_op jit(solution)/shard_map/ppermute | solution.py:30
  59.0 1.9 %collective-permute-start.14 = (f32[104,512]{1,0:T(8,128)S(1)}, f32[104,512]{1,0:T(8,128)S(1)}, u32[]{:S(2)}, u32[]{:S(2)}) collective-permute-start(f32[104,512]{1,0:T(8,128)S(1)} %get-tuple-element.70), channel_id=1, source_target_pairs={{0,48},{16,32},{32,16},{48,0},{64,112},{80,96},{96,80},{112,64},{1... | collective-permute-start | bytes 638984 | tf_op jit(solution)/shard_map/ppermute | solution.py:30
  60.9 1.0 %collective-permute-start.13 = (f32[104,512]{1,0:T(8,128)S(1)}, f32[104,512]{1,0:T(8,128)S(1)}, u32[]{:S(2)}, u32[]{:S(2)}) collective-permute-start(f32[104,512]{1,0:T(8,128)S(1)} %get-tuple-element.70), channel_id=1, source_target_pairs={{0,32},{16,48},{32,0},{48,16},{64,96},{80,112},{96,64},{112,80},{1... | collective-permute-start | bytes 638984 | tf_op jit(solution)/shard_map/ppermute | solution.py:30
  61.8 0.4 collective-permute-start.12
  62.2 10.4 %near_rows.8.refs_10_ = f32[4,1024,128]{2,1,0:T(8,128)S(1)} custom-call(s32[1,768]{1,0:T(1,128)S(1)} %copy-done.2, s32[1,768]{1,0:T(1,128)S(1)} %copy-done.3, bf16[768,4096]{1,0:T(8,128)(2,1)} %bitcast.63, bf16[4096,512]{1,0:T(8,128)(2,1)S(1)} %bitcast.58), custom_call_target="tpu_custom_call" | custom-call | flops 4294967296 | bytes 8388608 | tf_op jit(solution)/shard_map/near_rows/pallas_call | solution.py:108
  72.8 2.0 %collective-permute-start.15 = (f32[4,40,512]{2,1,0:T(8,128)S(1)}, f32[4,40,512]{2,1,0:T(8,128)S(1)}, u32[]{:S(2)}, u32[]{:S(2)}) collective-permute-start(f32[4,40,512]{2,1,0:T(8,128)S(1)} %pad_maximum_fusion.2), channel_id=1, source_target_pairs={{0,64},{16,80},{32,96},{48,112},{64,0},{80,16},{96,32},{112,48},{1... | collective-permute-start | bytes 983048 | tf_op jit(solution)/shard_map/ppermute | solution.py:30
  74.9 2.4 %collective-permute-start.16 = (f32[4,24,512]{2,1,0:T(8,128)S(1)}, f32[4,24,512]{2,1,0:T(8,128)S(1)}, u32[]{:S(2)}, u32[]{:S(2)}) collective-permute-start(f32[4,24,512]{2,1,0:T(8,128)S(1)} %slice.136), channel_id=1, source_target_pairs={{0,1},{16,17},{32,33},{48,49},{64,65},{80,81},{96,97},{112,113},{1... | collective-permute-start | bytes 589832 | tf_op jit(solution)/shard_map/ppermute | solution.py:30
  77.2 6.4 %near_rows.9.refs_11_ = f32[4,512,128]{2,1,0:T(8,128)S(1)} custom-call(s32[1,768]{1,0:T(1,128)S(1)} %copy-done.2, s32[1,768]{1,0:T(1,128)S(1)} %copy-done.3, bf16[768,4096]{1,0:T(8,128)(2,1)} %bitcast.64, bf16[4096,512]{1,0:T(8,128)(2,1)S(1)} %bitcast.59), custom_call_target="tpu_custom_call" | custom-call | flops 2147483648 | bytes 8388608 | tf_op jit(solution)/shard_map/near_rows/pallas_call | solution.py:108
  83.7 0.1 collective-permute-start.17
  83.8 1.4 %collective-permute-done.17.refs_6_ = f32[4,24,512]{2,1,0:T(8,128)S(1)} collective-permute-done((f32[4,24,512]{2,1,0:T(8,128)S(1)}, f32[4,24,512]{2,1,0:T(8,128)S(1)}, u32[]{:S(2)}, u32[]{:S(2)}) %collective-permute-start.17) | collective-permute-done | bytes 196640 | tf_op jit(solution)/shard_map/ppermute | solution.py:30
  85.2 7.8 %far_rows.1 = bf16[4096,512]{1,0:T(8,128)(2,1)} custom-call(bf16[7,1,4096,128]{3,2,1,0:T(8,128)(2,1)} %bases_h.1, f32[128,512]{1,0:T(8,128)S(1)} %collective-permute-done.2.first, f32[104,512]{1,0:T(8,128)S(1)} %get-tuple-element.39.refs_0_, f32[104,512]{1,0:T(8,128)S(1)} %collective-permute-done.12.refs_1_, f32[104,512]{1,0:T(8,128)S(1)} %collective-permute-done.13.refs_2_, ...), custom_call_target="tpu_custom_call" | custom-call | tf_op jit(solution)/shard_map/far_rows/pallas_call | solution.py:192
  (53 shorter events, 0.5 us)
Async XLA Ops:
  8.1 1.2 %copy-start.4 = (f32[7,128,512]{2,1,0:T(8,128)}, f32[7,128,512]{2,1,0:T(8,128)S(1)}, u32[]{:S(2)}) copy-start(f32[7,128,512]{2,1,0:T(8,128)S(1)} %fusion) | copy-start | bytes 5505028
  9.4 3.8 %collective-permute-start = (f32[3,64,512]{2,1,0:T(8,128)S(1)}, f32[3,64,512]{2,1,0:T(8,128)S(1)}, u32[]{:S(2)}, u32[]{:S(2)}) collective-permute-start(f32[3,64,512]{2,1,0:T(8,128)S(1)} %dynamic-slice_bitcast_fusion), channel_id=1, source_target_pairs={{0,1},{16,17},{32,33},{48,49},{64,65},{80,81},{96,97},{112,113},{1... | collective-permute-start | bytes 1179656 | tf_op jit(solution)/shard_map/ppermute | solution.py:30
  13.4 14.4 %collective-permute-start.1 = (f32[160,512]{1,0:T(8,128)S(1)}, f32[160,512]{1,0:T(8,128)S(1)}, u32[]{:S(2)}, u32[]{:S(2)}) collective-permute-start(f32[160,512]{1,0:T(8,128)S(1)} %pad_maximum_fusion.1), channel_id=1, source_target_pairs={{0,64},{16,80},{32,96},{48,112},{64,0},{80,16},{96,32},{112,48},{1... | collective-permute-start | bytes 983048 | tf_op jit(solution)/shard_map/ppermute | solution.py:30
  14.7 13.0 %collective-permute-start.2 = (f32[128,512]{1,0:T(8,128)S(1)}, f32[128,512]{1,0:T(8,128)S(1)}, u32[]{:S(2)}, u32[]{:S(2)}) collective-permute-start(f32[128,512]{1,0:T(8,128)S(1)} %get-tuple-element.28), channel_id=1, source_target_pairs={{0,16},{16,0},{32,48},{48,32},{64,80},{80,64},{96,112},{112,96},{1... | collective-permute-start | bytes 786440 | tf_op jit(solution)/shard_map/ppermute | solution.py:30
  27.7 3.6 %copy-start = (bf16[1,4096,512]{2,1,0:T(8,128)(2,1)S(1)}, bf16[1,4096,512]{2,1,0:T(8,128)(2,1)}, u32[]{:S(2)}) copy-start(bf16[1,4096,512]{2,1,0:T(8,128)(2,1)} %param.5) | copy-start | bytes 12582916
  27.7 3.6 %copy-start.2 = (s32[1,768]{1,0:T(1,128)S(1)}, s32[1,768]{1,0:T(1,128)}, u32[]{:S(2)}) copy-start(s32[1,768]{1,0:T(1,128)} %refs_0_.4) | copy-start | bytes 9220
  27.7 3.6 %copy-start.3 = (s32[1,768]{1,0:T(1,128)S(1)}, s32[1,768]{1,0:T(1,128)}, u32[]{:S(2)}) copy-start(s32[1,768]{1,0:T(1,128)} %refs_1_.9) | copy-start | bytes 9220
  28.0 13.6 %collective-permute-start.5 = (f32[104,512]{1,0:T(8,128)S(1)}, f32[104,512]{1,0:T(8,128)S(1)}, u32[]{:S(2)}, u32[]{:S(2)}) collective-permute-start(f32[104,512]{1,0:T(8,128)S(1)} %get-tuple-element.53), channel_id=1, source_target_pairs={{0,48},{16,32},{32,16},{48,0},{64,112},{80,96},{96,80},{112,64},{1... | collective-permute-start | bytes 638984 | tf_op jit(solution)/shard_map/ppermute | solution.py:30
  30.0 11.6 %collective-permute-start.4 = (f32[104,512]{1,0:T(8,128)S(1)}, f32[104,512]{1,0:T(8,128)S(1)}, u32[]{:S(2)}, u32[]{:S(2)}) collective-permute-start(f32[104,512]{1,0:T(8,128)S(1)} %get-tuple-element.54), channel_id=1, source_target_pairs={{0,32},{16,48},{32,0},{48,16},{64,96},{80,112},{96,64},{112,80},{1... | collective-permute-start | bytes 638984 | tf_op jit(solution)/shard_map/ppermute | solution.py:30
  30.5 11.1 %collective-permute-start.3 = (f32[104,512]{1,0:T(8,128)S(1)}, f32[104,512]{1,0:T(8,128)S(1)}, u32[]{:S(2)}, u32[]{:S(2)}) collective-permute-start(f32[104,512]{1,0:T(8,128)S(1)} %get-tuple-element.55), channel_id=1, source_target_pairs={{0,16},{16,0},{32,48},{48,32},{64,80},{80,64},{96,112},{112,96},{1... | collective-permute-start | bytes 638984 | tf_op jit(solution)/shard_map/ppermute | solution.py:30
  41.7 13.0 %collective-permute-start.10 = (f32[16,512]{1,0:T(8,128)S(1)}, f32[16,512]{1,0:T(8,128)S(1)}, u32[]{:S(2)}, u32[]{:S(2)}) collective-permute-start(f32[16,512]{1,0:T(8,128)S(1)} %get-tuple-element.57), channel_id=1, source_target_pairs={{0,6},{16,22},{32,38},{48,54},{64,70},{80,86},{96,102},{112,118},{... | collective-permute-start | bytes 98312 | tf_op jit(solution)/shard_map/ppermute | solution.py:30
  45.3 9.4 %collective-permute-start.9 = (f32[16,512]{1,0:T(8,128)S(1)}, f32[16,512]{1,0:T(8,128)S(1)}, u32[]{:S(2)}, u32[]{:S(2)}) collective-permute-start(f32[16,512]{1,0:T(8,128)S(1)} %get-tuple-element.57), channel_id=1, source_target_pairs={{0,4},{16,20},{32,36},{48,52},{64,68},{80,84},{96,100},{112,116},{... | collective-permute-start | bytes 98312 | tf_op jit(solution)/shard_map/ppermute | solution.py:30
  45.5 9.2 %collective-permute-start.8 = (f32[16,512]{1,0:T(8,128)S(1)}, f32[16,512]{1,0:T(8,128)S(1)}, u32[]{:S(2)}, u32[]{:S(2)}) collective-permute-start(f32[16,512]{1,0:T(8,128)S(1)} %pad_maximum_fusion.3), channel_id=1, source_target_pairs={{0,2},{16,18},{32,34},{48,50},{64,66},{80,82},{96,98},{112,114},{1... | collective-permute-start | bytes 98312 | tf_op jit(solution)/shard_map/ppermute | solution.py:30
  46.0 8.7 %collective-permute-start.7 = (f32[16,512]{1,0:T(8,128)S(1)}, f32[16,512]{1,0:T(8,128)S(1)}, u32[]{:S(2)}, u32[]{:S(2)}) collective-permute-start(f32[16,512]{1,0:T(8,128)S(1)} %get-tuple-element.58), channel_id=1, source_target_pairs={{0,1},{16,17},{32,33},{48,49},{64,65},{80,81},{96,97},{112,113},{1... | collective-permute-start | bytes 98312 | tf_op jit(solution)/shard_map/ppermute | solution.py:30
  48.5 6.1 %collective-permute-start.6 = (f32[32,512]{1,0:T(8,128)S(1)}, f32[32,512]{1,0:T(8,128)S(1)}, u32[]{:S(2)}, u32[]{:S(2)}) collective-permute-start(f32[32,512]{1,0:T(8,128)S(1)} %slice.126), channel_id=1, source_target_pairs={{0,64},{16,80},{32,96},{48,112},{64,0},{80,16},{96,32},{112,48},{1... | collective-permute-start | bytes 196616 | tf_op jit(solution)/shard_map/ppermute | solution.py:30
  54.8 4.2 %collective-permute-start.11 = (f32[8,512]{1,0:T(8,128)S(1)}, f32[8,512]{1,0:T(8,128)S(1)}, u32[]{:S(2)}, u32[]{:S(2)}) collective-permute-start(f32[8,512]{1,0:T(8,128)S(1)} %get-tuple-element.38), channel_id=1, source_target_pairs={{0,8},{16,24},{32,40},{48,56},{64,72},{80,88},{96,104},{112,120},{... | collective-permute-start | bytes 49160 | tf_op jit(solution)/shard_map/ppermute | solution.py:30
  59.0 13.7 %collective-permute-start.14 = (f32[104,512]{1,0:T(8,128)S(1)}, f32[104,512]{1,0:T(8,128)S(1)}, u32[]{:S(2)}, u32[]{:S(2)}) collective-permute-start(f32[104,512]{1,0:T(8,128)S(1)} %get-tuple-element.70), channel_id=1, source_target_pairs={{0,48},{16,32},{32,16},{48,0},{64,112},{80,96},{96,80},{112,64},{1... | collective-permute-start | bytes 638984 | tf_op jit(solution)/shard_map/ppermute | solution.py:30
  60.9 11.8 %collective-permute-start.13 = (f32[104,512]{1,0:T(8,128)S(1)}, f32[104,512]{1,0:T(8,128)S(1)}, u32[]{:S(2)}, u32[]{:S(2)}) collective-permute-start(f32[104,512]{1,0:T(8,128)S(1)} %get-tuple-element.70), channel_id=1, source_target_pairs={{0,32},{16,48},{32,0},{48,16},{64,96},{80,112},{96,64},{112,80},{1... | collective-permute-start | bytes 638984 | tf_op jit(solution)/shard_map/ppermute | solution.py:30
  61.8 10.9 %collective-permute-start.12 = (f32[104,512]{1,0:T(8,128)S(1)}, f32[104,512]{1,0:T(8,128)S(1)}, u32[]{:S(2)}, u32[]{:S(2)}) collective-permute-start(f32[104,512]{1,0:T(8,128)S(1)} %get-tuple-element.39.refs_0_), channel_id=1, source_target_pairs={{0,16},{16,0},{32,48},{48,32},{64,80},{80,64},{96,112},{112,96},{1... | collective-permute-start | bytes 638984 | tf_op jit(solution)/shard_map/ppermute | solution.py:30
  72.8 10.8 %collective-permute-start.15 = (f32[4,40,512]{2,1,0:T(8,128)S(1)}, f32[4,40,512]{2,1,0:T(8,128)S(1)}, u32[]{:S(2)}, u32[]{:S(2)}) collective-permute-start(f32[4,40,512]{2,1,0:T(8,128)S(1)} %pad_maximum_fusion.2), channel_id=1, source_target_pairs={{0,64},{16,80},{32,96},{48,112},{64,0},{80,16},{96,32},{112,48},{1... | collective-permute-start | bytes 983048 | tf_op jit(solution)/shard_map/ppermute | solution.py:30
  74.9 10.3 %copy-start.1 = (f32[4,1024,128]{2,1,0:T(8,128)S(1)}, f32[4,1024,128]{2,1,0:T(8,128)}, u32[]{:S(2)}) copy-start(f32[4,1024,128]{2,1,0:T(8,128)} %near_rows.5.refs_7_) | copy-start | bytes 6291460
  74.9 8.8 %collective-permute-start.16 = (f32[4,24,512]{2,1,0:T(8,128)S(1)}, f32[4,24,512]{2,1,0:T(8,128)S(1)}, u32[]{:S(2)}, u32[]{:S(2)}) collective-permute-start(f32[4,24,512]{2,1,0:T(8,128)S(1)} %slice.136), channel_id=1, source_target_pairs={{0,1},{16,17},{32,33},{48,49},{64,65},{80,81},{96,97},{112,113},{1... | collective-permute-start | bytes 589832 | tf_op jit(solution)/shard_map/ppermute | solution.py:30
  83.7 1.5 %collective-permute-start.17 = (f32[4,24,512]{2,1,0:T(8,128)S(1)}, f32[4,24,512]{2,1,0:T(8,128)S(1)}, u32[]{:S(2)}, u32[]{:S(2)}) collective-permute-start(f32[4,24,512]{2,1,0:T(8,128)S(1)} %slice.121), channel_id=1, source_target_pairs={{0,1},{16,17},{32,33},{48,49},{64,65},{80,81},{96,97},{112,113},{1... | collective-permute-start | bytes 589832 | tf_op jit(solution)/shard_map/ppermute | solution.py:30

commit v5 on v4

--- a/solution.py
+++ b/solution.py
@@ -216,12 +216,12 @@
     return block.reshape(levels, parts, size, width).transpose(1, 0, 2, 3).reshape(parts, levels * size, width)
 
 
-def halves_of(block, bit):
-    levels, rows, width = block.shape
-    cut = block.reshape(levels, 2, rows // 2, width)
+def halves_of(block, level, levels, bit):
+    _, rows, width = block.shape
+    size = (levels, rows // 2, width)
     return (
-        lax.dynamic_index_in_dim(cut, bit, 1, keepdims=False),
-        lax.dynamic_index_in_dim(cut, 1 - bit, 1, keepdims=False),
+        lax.dynamic_slice(block, (level, bit * (rows // 2), 0), size),
+        lax.dynamic_slice(block, (level, (1 - bit) * (rows // 2), 0), size),
     )
 
 
@@ -230,10 +230,10 @@
     me = lax.axis_index("inner")
     ring, side = lax.rem(me, 4), me // 4
     core = lax.rem(lax.axis_index("outer"), 2)
-    mine, other = halves_of(partial[4:], core)
+    mine, other = halves_of(partial, 4, 3, core)
     upper = mine + flip(other, 8)
-    mine3, other3 = halves_of(partial[3:4], side)
-    mine, other = halves_of(upper, side)
+    mine3, other3 = halves_of(partial, 3, 1, side)
+    mine, other = halves_of(upper, 0, 3, side)
     sent = jnp.concatenate([other3.reshape(64, width), other.reshape(96, width)], axis=0)
     near = [near_part(0, after(own_rows, sent))]
     received = flip(sent, 4)

time: 93.2 us -> 90.9 us (0.975)
  local copies, waits for them, and re-layouts: 3.74 us -> 0.38 us
  waiting for transfers between devices: 2.6 us -> 3.9 us
    ppermute x18, waiting for transfers between devices: 2.6 us -> 3.9 us  [flip(): return lax.ppermute(block, ('inner', 'outer'), route)]
    unnamed x13 -> x11, local copies, waits for them, and re-layouts: 1.27 us -> 0.05 us
    squeeze x1, local copies, waits for them, and re-layouts: 1.07 us -> 0.02 us  [siblings(): first = flip(after(partial[0], sent), 1)]
    slice x1, local copies, waits for them, and re-layouts: 1.08 us -> 0.03 us  [siblings(): partial[1:3]]
  transfers between devices with their start and end apart: 18 -> 18, of which waited for: 2 -> 3; matrix products, arithmetic and copies ran while one was open for 2% -> 0% of each run, Pallas kernels for 48% -> 50%
where the time goes in v5:
time: 90.9 us; the launch traced here: 90.5 us
  Pallas kernels  52.7 us (58%)
  starting transfers between devices  24.5 us (27%)
  matrix products  8.11 us (9%)
  waiting for transfers between devices  3.9 us (4%)
    pallas_call x5, Pallas kernels, near_rows(): pl.pallas_call(body, in_specs=[pl.BlockSpec(memory_space=pltpu.SMEM)] * 2...  44.9 us
    ppermute x18, starting transfers between devices, flip(): return lax.ppermute(block, ('inner', 'outer'), route)  24.5 us
    dot_general x1, matrix products, local(): jnp.einsum('hpr,pb->hrb', bases[:, 0], local_points, preferred_element_ty...  8.11 us
    pallas_call x1, Pallas kernels, far_rows(): pl.pallas_call(body, in_specs=[pl.BlockSpec(memory_space=pl.ANY)] + [pl.B...  7.8 us
    ppermute x18, waiting for transfers between devices, flip(): return lax.ppermute(block, ('inner', 'outer'), route)  3.9 us
  transfers between devices with their start and end apart: 18, of which 3 were waited for; matrix products, arithmetic and copies ran while one was open for 0% of the time, Pallas kernels for 50%

profile of v5, /device:TPU:1, one launch (start us, length us, event | category | flops | bytes accessed | tf_op | source)
XLA Modules:
  0.0 90.5 jit_solution(14659660105440456608)
XLA Ops:
  0.0 8.1 %fusion = f32[7,128,512]{2,1,0:T(8,128)S(1)} fusion(bf16[7,1,4096,128]{3,2,1,0:T(8,128)(2,1)} %bases_h.1, bf16[1,4096,512]{2,1,0:T(8,128)(2,1)} %param.5), kind=kOutput, calls=%fused_computation | convolution fusion | flops 3758096384 | bytes 13369344 | tf_op jit(solution)/shard_map/hpr,pb->hrb/dot_general | solution.py:282
  8.2 1.5 %collective-permute-start = (f32[3,64,512]{2,1,0:T(8,128)S(1)}, f32[3,64,512]{2,1,0:T(8,128)S(1)}, u32[]{:S(2)}, u32[]{:S(2)}) collective-permute-start(f32[3,64,512]{2,1,0:T(8,128)S(1)} %constant_dynamic-slice_fusion.1), channel_id=1, source_target_pairs={{0,1},{16,17},{32,33},{48,49},{64,65},{80,81},{96,97},{112,113},{1... | collective-permute-start | bytes 1179656 | tf_op jit(solution)/shard_map/ppermute | solution.py:30
  9.8 1.2 %collective-permute-done = f32[3,64,512]{2,1,0:T(8,128)S(1)} collective-permute-done((f32[3,64,512]{2,1,0:T(8,128)S(1)}, f32[3,64,512]{2,1,0:T(8,128)S(1)}, u32[]{:S(2)}, u32[]{:S(2)}) %collective-permute-start) | collective-permute-done | bytes 393248 | tf_op jit(solution)/shard_map/ppermute | solution.py:30
  11.0 0.1 dynamic-slice_add_fusion
  11.1 1.4 %collective-permute-start.1 = (f32[160,512]{1,0:T(8,128)S(1)}, f32[160,512]{1,0:T(8,128)S(1)}, u32[]{:S(2)}, u32[]{:S(2)}) collective-permute-start(f32[160,512]{1,0:T(8,128)S(1)} %pad_maximum_fusion.1), channel_id=1, source_target_pairs={{0,64},{16,80},{32,96},{48,112},{64,0},{80,16},{96,32},{112,48},{1... | collective-permute-start | bytes 983048 | tf_op jit(solution)/shard_map/ppermute | solution.py:30
  12.5 1.3 %collective-permute-start.2 = (f32[128,512]{1,0:T(8,128)S(1)}, f32[128,512]{1,0:T(8,128)S(1)}, u32[]{:S(2)}, u32[]{:S(2)}) collective-permute-start(f32[128,512]{1,0:T(8,128)S(1)} %slice_bitcast_fusion), channel_id=1, source_target_pairs={{0,16},{16,0},{32,48},{48,32},{64,80},{80,64},{96,112},{112,96},{1... | collective-permute-start | bytes 786440 | tf_op jit(solution)/shard_map/ppermute | solution.py:30
  13.8 11.7 %near_rows.5.refs_7_ = f32[4,1024,128]{2,1,0:T(8,128)} custom-call(s32[1,768]{1,0:T(1,128)} %refs_0_.4, s32[1,768]{1,0:T(1,128)} %refs_1_.9, bf16[768,4096]{1,0:T(8,128)(2,1)} %bitcast.50, bf16[4096,512]{1,0:T(8,128)(2,1)} %bitcast.45), custom_call_target="tpu_custom_call" | custom-call | flops 4294967296 | bytes 8388608 | tf_op jit(solution)/shard_map/near_rows/pallas_call | solution.py:108
  25.5 0.0 copy-start
  25.5 0.0 copy-start.2
  25.6 0.1 pad_maximum_fusion
  25.7 0.1 dynamic-slice_bitcast_fusion
  25.8 2.0 %collective-permute-start.5 = (f32[104,512]{1,0:T(8,128)S(1)}, f32[104,512]{1,0:T(8,128)S(1)}, u32[]{:S(2)}, u32[]{:S(2)}) collective-permute-start(f32[104,512]{1,0:T(8,128)S(1)} %get-tuple-element.51), channel_id=1, source_target_pairs={{0,48},{16,32},{32,16},{48,0},{64,112},{80,96},{96,80},{112,64},{1... | collective-permute-start | bytes 638984 | tf_op jit(solution)/shard_map/ppermute | solution.py:30
  27.7 0.8 collective-permute-start.4
  28.5 0.5 collective-permute-start.3
  29.1 10.0 %near_rows.6.refs_8_ = f32[4,1024,128]{2,1,0:T(8,128)S(1)} custom-call(s32[1,768]{1,0:T(1,128)S(1)} %copy-done.2, s32[1,768]{1,0:T(1,128)S(1)} %copy-done.3, bf16[768,4096]{1,0:T(8,128)(2,1)} %bitcast.51, bf16[4096,512]{1,0:T(8,128)(2,1)S(1)} %bitcast.46), custom_call_target="tpu_custom_call" | custom-call | flops 4294967296 | bytes 8388608 | tf_op jit(solution)/shard_map/near_rows/pallas_call | solution.py:108
  39.3 3.8 %collective-permute-start.10 = (f32[16,512]{1,0:T(8,128)S(1)}, f32[16,512]{1,0:T(8,128)S(1)}, u32[]{:S(2)}, u32[]{:S(2)}) collective-permute-start(f32[16,512]{1,0:T(8,128)S(1)} %get-tuple-element.55), channel_id=1, source_target_pairs={{0,6},{16,22},{32,38},{48,54},{64,70},{80,86},{96,102},{112,118},{... | collective-permute-start | bytes 98312 | tf_op jit(solution)/shard_map/ppermute | solution.py:30
  43.1 0.2 collective-permute-start.9
  43.3 0.5 collective-permute-start.8
  43.8 2.3 %collective-permute-start.7 = (f32[16,512]{1,0:T(8,128)S(1)}, f32[16,512]{1,0:T(8,128)S(1)}, u32[]{:S(2)}, u32[]{:S(2)}) collective-permute-start(f32[16,512]{1,0:T(8,128)S(1)} %get-tuple-element.56), channel_id=1, source_target_pairs={{0,1},{16,17},{32,33},{48,49},{64,65},{80,81},{96,97},{112,113},{1... | collective-permute-start | bytes 98312 | tf_op jit(solution)/shard_map/ppermute | solution.py:30
  46.1 0.3 collective-permute-start.6
  46.4 6.1 %near_rows.7.refs_9_ = f32[4,512,128]{2,1,0:T(8,128)S(1)} custom-call(s32[1,768]{1,0:T(1,128)S(1)} %copy-done.2, s32[1,768]{1,0:T(1,128)S(1)} %copy-done.3, bf16[768,4096]{1,0:T(8,128)(2,1)} %bitcast.52, bf16[4096,512]{1,0:T(8,128)(2,1)S(1)} %bitcast.47), custom_call_target="tpu_custom_call" | custom-call | flops 2147483648 | bytes 8388608 | tf_op jit(solution)/shard_map/near_rows/pallas_call | solution.py:108
  52.6 2.6 %collective-permute-start.11 = (f32[8,512]{1,0:T(8,128)S(1)}, f32[8,512]{1,0:T(8,128)S(1)}, u32[]{:S(2)}, u32[]{:S(2)}) collective-permute-start(f32[8,512]{1,0:T(8,128)S(1)} %get-tuple-element.38), channel_id=1, source_target_pairs={{0,8},{16,24},{32,40},{48,56},{64,72},{80,88},{96,104},{112,120},{... | collective-permute-start | bytes 49160 | tf_op jit(solution)/shard_map/ppermute | solution.py:30
  55.2 1.6 %collective-permute-done.11 = f32[8,512]{1,0:T(8,128)S(1)} collective-permute-done((f32[8,512]{1,0:T(8,128)S(1)}, f32[8,512]{1,0:T(8,128)S(1)}, u32[]{:S(2)}, u32[]{:S(2)}) %collective-permute-start.11) | collective-permute-done | bytes 16416 | tf_op jit(solution)/shard_map/ppermute | solution.py:30
  56.8 2.2 %collective-permute-start.14 = (f32[104,512]{1,0:T(8,128)S(1)}, f32[104,512]{1,0:T(8,128)S(1)}, u32[]{:S(2)}, u32[]{:S(2)}) collective-permute-start(f32[104,512]{1,0:T(8,128)S(1)} %get-tuple-element.68), channel_id=1, source_target_pairs={{0,48},{16,32},{32,16},{48,0},{64,112},{80,96},{96,80},{112,64},{1... | collective-permute-start | bytes 638984 | tf_op jit(solution)/shard_map/ppermute | solution.py:30
  59.0 1.3 %collective-permute-start.13 = (f32[104,512]{1,0:T(8,128)S(1)}, f32[104,512]{1,0:T(8,128)S(1)}, u32[]{:S(2)}, u32[]{:S(2)}) collective-permute-start(f32[104,512]{1,0:T(8,128)S(1)} %get-tuple-element.68), channel_id=1, source_target_pairs={{0,32},{16,48},{32,0},{48,16},{64,96},{80,112},{96,64},{112,80},{1... | collective-permute-start | bytes 638984 | tf_op jit(solution)/shard_map/ppermute | solution.py:30
  60.3 10.7 %near_rows.8.refs_10_ = f32[4,1024,128]{2,1,0:T(8,128)S(1)} custom-call(s32[1,768]{1,0:T(1,128)S(1)} %copy-done.2, s32[1,768]{1,0:T(1,128)S(1)} %copy-done.3, bf16[768,4096]{1,0:T(8,128)(2,1)} %bitcast.53, bf16[4096,512]{1,0:T(8,128)(2,1)S(1)} %bitcast.48), custom_call_target="tpu_custom_call" | custom-call | flops 4294967296 | bytes 8388608 | tf_op jit(solution)/shard_map/near_rows/pallas_call | solution.py:108
  71.1 1.0 %collective-permute-start.15 = (f32[4,40,512]{2,1,0:T(8,128)S(1)}, f32[4,40,512]{2,1,0:T(8,128)S(1)}, u32[]{:S(2)}, u32[]{:S(2)}) collective-permute-start(f32[4,40,512]{2,1,0:T(8,128)S(1)} %pad_maximum_fusion.2), channel_id=1, source_target_pairs={{0,64},{16,80},{32,96},{48,112},{64,0},{80,16},{96,32},{112,48},{1... | collective-permute-start | bytes 983048 | tf_op jit(solution)/shard_map/ppermute | solution.py:30
  72.2 2.4 %collective-permute-start.16 = (f32[4,24,512]{2,1,0:T(8,128)S(1)}, f32[4,24,512]{2,1,0:T(8,128)S(1)}, u32[]{:S(2)}, u32[]{:S(2)}) collective-permute-start(f32[4,24,512]{2,1,0:T(8,128)S(1)} %slice.126), channel_id=1, source_target_pairs={{0,1},{16,17},{32,33},{48,49},{64,65},{80,81},{96,97},{112,113},{1... | collective-permute-start | bytes 589832 | tf_op jit(solution)/shard_map/ppermute | solution.py:30
  74.6 6.4 %near_rows.9.refs_11_ = f32[4,512,128]{2,1,0:T(8,128)S(1)} custom-call(s32[1,768]{1,0:T(1,128)S(1)} %copy-done.2, s32[1,768]{1,0:T(1,128)S(1)} %copy-done.3, bf16[768,4096]{1,0:T(8,128)(2,1)} %bitcast.54, bf16[4096,512]{1,0:T(8,128)(2,1)S(1)} %bitcast.49), custom_call_target="tpu_custom_call" | custom-call | flops 2147483648 | bytes 8388608 | tf_op jit(solution)/shard_map/near_rows/pallas_call | solution.py:108
  81.0 0.4 collective-permute-start.17
  81.4 1.1 %collective-permute-done.17.refs_6_ = f32[4,24,512]{2,1,0:T(8,128)S(1)} collective-permute-done((f32[4,24,512]{2,1,0:T(8,128)S(1)}, f32[4,24,512]{2,1,0:T(8,128)S(1)}, u32[]{:S(2)}, u32[]{:S(2)}) %collective-permute-start.17) | collective-permute-done | bytes 196640 | tf_op jit(solution)/shard_map/ppermute | solution.py:30
  82.5 7.8 %far_rows.1 = bf16[4096,512]{1,0:T(8,128)(2,1)} custom-call(bf16[7,1,4096,128]{3,2,1,0:T(8,128)(2,1)} %bases_h.1, f32[128,512]{1,0:T(8,128)S(1)} %collective-permute-done.2.first, f32[104,512]{1,0:T(8,128)S(1)} %get-tuple-element.39.refs_0_, f32[104,512]{1,0:T(8,128)S(1)} %collective-permute-done.12.refs_1_, f32[104,512]{1,0:T(8,128)S(1)} %collective-permute-done.13.refs_2_, ...), custom_call_target="tpu_custom_call" | custom-call | tf_op jit(solution)/shard_map/far_rows/pallas_call | solution.py:192
  (50 shorter events, 0.5 us)
Async XLA Ops:
  8.2 2.8 %collective-permute-start = (f32[3,64,512]{2,1,0:T(8,128)S(1)}, f32[3,64,512]{2,1,0:T(8,128)S(1)}, u32[]{:S(2)}, u32[]{:S(2)}) collective-permute-start(f32[3,64,512]{2,1,0:T(8,128)S(1)} %constant_dynamic-slice_fusion.1), channel_id=1, source_target_pairs={{0,1},{16,17},{32,33},{48,49},{64,65},{80,81},{96,97},{112,113},{1... | collective-permute-start | bytes 1179656 | tf_op jit(solution)/shard_map/ppermute | solution.py:30
  11.1 14.4 %collective-permute-start.1 = (f32[160,512]{1,0:T(8,128)S(1)}, f32[160,512]{1,0:T(8,128)S(1)}, u32[]{:S(2)}, u32[]{:S(2)}) collective-permute-start(f32[160,512]{1,0:T(8,128)S(1)} %pad_maximum_fusion.1), channel_id=1, source_target_pairs={{0,64},{16,80},{32,96},{48,112},{64,0},{80,16},{96,32},{112,48},{1... | collective-permute-start | bytes 983048 | tf_op jit(solution)/shard_map/ppermute | solution.py:30
  12.5 13.0 %collective-permute-start.2 = (f32[128,512]{1,0:T(8,128)S(1)}, f32[128,512]{1,0:T(8,128)S(1)}, u32[]{:S(2)}, u32[]{:S(2)}) collective-permute-start(f32[128,512]{1,0:T(8,128)S(1)} %slice_bitcast_fusion), channel_id=1, source_target_pairs={{0,16},{16,0},{32,48},{48,32},{64,80},{80,64},{96,112},{112,96},{1... | collective-permute-start | bytes 786440 | tf_op jit(solution)/shard_map/ppermute | solution.py:30
  25.5 3.6 %copy-start = (bf16[1,4096,512]{2,1,0:T(8,128)(2,1)S(1)}, bf16[1,4096,512]{2,1,0:T(8,128)(2,1)}, u32[]{:S(2)}) copy-start(bf16[1,4096,512]{2,1,0:T(8,128)(2,1)} %param.5) | copy-start | bytes 12582916
  25.5 3.6 %copy-start.2 = (s32[1,768]{1,0:T(1,128)S(1)}, s32[1,768]{1,0:T(1,128)}, u32[]{:S(2)}) copy-start(s32[1,768]{1,0:T(1,128)} %refs_0_.4) | copy-start | bytes 9220
  25.5 3.6 %copy-start.3 = (s32[1,768]{1,0:T(1,128)S(1)}, s32[1,768]{1,0:T(1,128)}, u32[]{:S(2)}) copy-start(s32[1,768]{1,0:T(1,128)} %refs_1_.9) | copy-start | bytes 9220
  25.8 13.4 %collective-permute-start.5 = (f32[104,512]{1,0:T(8,128)S(1)}, f32[104,512]{1,0:T(8,128)S(1)}, u32[]{:S(2)}, u32[]{:S(2)}) collective-permute-start(f32[104,512]{1,0:T(8,128)S(1)} %get-tuple-element.51), channel_id=1, source_target_pairs={{0,48},{16,32},{32,16},{48,0},{64,112},{80,96},{96,80},{112,64},{1... | collective-permute-start | bytes 638984 | tf_op jit(solution)/shard_map/ppermute | solution.py:30
  27.7 11.4 %collective-permute-start.4 = (f32[104,512]{1,0:T(8,128)S(1)}, f32[104,512]{1,0:T(8,128)S(1)}, u32[]{:S(2)}, u32[]{:S(2)}) collective-permute-start(f32[104,512]{1,0:T(8,128)S(1)} %get-tuple-element.52), channel_id=1, source_target_pairs={{0,32},{16,48},{32,0},{48,16},{64,96},{80,112},{96,64},{112,80},{1... | collective-permute-start | bytes 638984 | tf_op jit(solution)/shard_map/ppermute | solution.py:30
  28.5 10.6 %collective-permute-start.3 = (f32[104,512]{1,0:T(8,128)S(1)}, f32[104,512]{1,0:T(8,128)S(1)}, u32[]{:S(2)}, u32[]{:S(2)}) collective-permute-start(f32[104,512]{1,0:T(8,128)S(1)} %get-tuple-element.53), channel_id=1, source_target_pairs={{0,16},{16,0},{32,48},{48,32},{64,80},{80,64},{96,112},{112,96},{1... | collective-permute-start | bytes 638984 | tf_op jit(solution)/shard_map/ppermute | solution.py:30
  39.3 13.3 %collective-permute-start.10 = (f32[16,512]{1,0:T(8,128)S(1)}, f32[16,512]{1,0:T(8,128)S(1)}, u32[]{:S(2)}, u32[]{:S(2)}) collective-permute-start(f32[16,512]{1,0:T(8,128)S(1)} %get-tuple-element.55), channel_id=1, source_target_pairs={{0,6},{16,22},{32,38},{48,54},{64,70},{80,86},{96,102},{112,118},{... | collective-permute-start | bytes 98312 | tf_op jit(solution)/shard_map/ppermute | solution.py:30
  43.1 9.5 %collective-permute-start.9 = (f32[16,512]{1,0:T(8,128)S(1)}, f32[16,512]{1,0:T(8,128)S(1)}, u32[]{:S(2)}, u32[]{:S(2)}) collective-permute-start(f32[16,512]{1,0:T(8,128)S(1)} %get-tuple-element.55), channel_id=1, source_target_pairs={{0,4},{16,20},{32,36},{48,52},{64,68},{80,84},{96,100},{112,116},{... | collective-permute-start | bytes 98312 | tf_op jit(solution)/shard_map/ppermute | solution.py:30
  43.3 9.3 %collective-permute-start.8 = (f32[16,512]{1,0:T(8,128)S(1)}, f32[16,512]{1,0:T(8,128)S(1)}, u32[]{:S(2)}, u32[]{:S(2)}) collective-permute-start(f32[16,512]{1,0:T(8,128)S(1)} %pad_maximum_fusion.3), channel_id=1, source_target_pairs={{0,2},{16,18},{32,34},{48,50},{64,66},{80,82},{96,98},{112,114},{1... | collective-permute-start | bytes 98312 | tf_op jit(solution)/shard_map/ppermute | solution.py:30
  43.8 8.8 %collective-permute-start.7 = (f32[16,512]{1,0:T(8,128)S(1)}, f32[16,512]{1,0:T(8,128)S(1)}, u32[]{:S(2)}, u32[]{:S(2)}) collective-permute-start(f32[16,512]{1,0:T(8,128)S(1)} %get-tuple-element.56), channel_id=1, source_target_pairs={{0,1},{16,17},{32,33},{48,49},{64,65},{80,81},{96,97},{112,113},{1... | collective-permute-start | bytes 98312 | tf_op jit(solution)/shard_map/ppermute | solution.py:30
  46.1 6.4 %collective-permute-start.6 = (f32[32,512]{1,0:T(8,128)S(1)}, f32[32,512]{1,0:T(8,128)S(1)}, u32[]{:S(2)}, u32[]{:S(2)}) collective-permute-start(f32[32,512]{1,0:T(8,128)S(1)} %slice.116), channel_id=1, source_target_pairs={{0,64},{16,80},{32,96},{48,112},{64,0},{80,16},{96,32},{112,48},{1... | collective-permute-start | bytes 196616 | tf_op jit(solution)/shard_map/ppermute | solution.py:30
  52.6 4.2 %collective-permute-start.11 = (f32[8,512]{1,0:T(8,128)S(1)}, f32[8,512]{1,0:T(8,128)S(1)}, u32[]{:S(2)}, u32[]{:S(2)}) collective-permute-start(f32[8,512]{1,0:T(8,128)S(1)} %get-tuple-element.38), channel_id=1, source_target_pairs={{0,8},{16,24},{32,40},{48,56},{64,72},{80,88},{96,104},{112,120},{... | collective-permute-start | bytes 49160 | tf_op jit(solution)/shard_map/ppermute | solution.py:30
  56.8 14.2 %collective-permute-start.14 = (f32[104,512]{1,0:T(8,128)S(1)}, f32[104,512]{1,0:T(8,128)S(1)}, u32[]{:S(2)}, u32[]{:S(2)}) collective-permute-start(f32[104,512]{1,0:T(8,128)S(1)} %get-tuple-element.68), channel_id=1, source_target_pairs={{0,48},{16,32},{32,16},{48,0},{64,112},{80,96},{96,80},{112,64},{1... | collective-permute-start | bytes 638984 | tf_op jit(solution)/shard_map/ppermute | solution.py:30
  59.0 12.1 %collective-permute-start.13 = (f32[104,512]{1,0:T(8,128)S(1)}, f32[104,512]{1,0:T(8,128)S(1)}, u32[]{:S(2)}, u32[]{:S(2)}) collective-permute-start(f32[104,512]{1,0:T(8,128)S(1)} %get-tuple-element.68), channel_id=1, source_target_pairs={{0,32},{16,48},{32,0},{48,16},{64,96},{80,112},{96,64},{112,80},{1... | collective-permute-start | bytes 638984 | tf_op jit(solution)/shard_map/ppermute | solution.py:30
  60.3 10.7 %collective-permute-start.12 = (f32[104,512]{1,0:T(8,128)S(1)}, f32[104,512]{1,0:T(8,128)S(1)}, u32[]{:S(2)}, u32[]{:S(2)}) collective-permute-start(f32[104,512]{1,0:T(8,128)S(1)} %get-tuple-element.39.refs_0_), channel_id=1, source_target_pairs={{0,16},{16,0},{32,48},{48,32},{64,80},{80,64},{96,112},{112,96},{1... | collective-permute-start | bytes 638984 | tf_op jit(solution)/shard_map/ppermute | solution.py:30
  71.1 9.8 %collective-permute-start.15 = (f32[4,40,512]{2,1,0:T(8,128)S(1)}, f32[4,40,512]{2,1,0:T(8,128)S(1)}, u32[]{:S(2)}, u32[]{:S(2)}) collective-permute-start(f32[4,40,512]{2,1,0:T(8,128)S(1)} %pad_maximum_fusion.2), channel_id=1, source_target_pairs={{0,64},{16,80},{32,96},{48,112},{64,0},{80,16},{96,32},{112,48},{1... | collective-permute-start | bytes 983048 | tf_op jit(solution)/shard_map/ppermute | solution.py:30
  72.2 10.3 %copy-start.1 = (f32[4,1024,128]{2,1,0:T(8,128)S(1)}, f32[4,1024,128]{2,1,0:T(8,128)}, u32[]{:S(2)}) copy-start(f32[4,1024,128]{2,1,0:T(8,128)} %near_rows.5.refs_7_) | copy-start | bytes 6291460
  72.2 8.8 %collective-permute-start.16 = (f32[4,24,512]{2,1,0:T(8,128)S(1)}, f32[4,24,512]{2,1,0:T(8,128)S(1)}, u32[]{:S(2)}, u32[]{:S(2)}) collective-permute-start(f32[4,24,512]{2,1,0:T(8,128)S(1)} %slice.126), channel_id=1, source_target_pairs={{0,1},{16,17},{32,33},{48,49},{64,65},{80,81},{96,97},{112,113},{1... | collective-permute-start | bytes 589832 | tf_op jit(solution)/shard_map/ppermute | solution.py:30
  81.0 1.5 %collective-permute-start.17 = (f32[4,24,512]{2,1,0:T(8,128)S(1)}, f32[4,24,512]{2,1,0:T(8,128)S(1)}, u32[]{:S(2)}, u32[]{:S(2)}) collective-permute-start(f32[4,24,512]{2,1,0:T(8,128)S(1)} %slice.113), channel_id=1, source_target_pairs={{0,1},{16,17},{32,33},{48,49},{64,65},{80,81},{96,97},{112,113},{1... | collective-permute-start | bytes 589832 | tf_op jit(solution)/shard_map/ppermute | solution.py:30
